TPU v7x, 256 devices: a whole 4x4x8 slice. The times are simulated.
256 devices in a mesh: dom: 64 (over x, z, core), rhs: 4 (over y).
Axes of the slice: x: 4, y: 4, z: 8, core: 2. Of those that a mesh axis runs over, the one named last changes fastest.
Arguments:
- solution: float32 [768, 64, 192], P('dom', 'rhs'), may hold values from -6 to 6
- loads: float32 [768, 64, 192], P('dom', 'rhs'), may hold values from -6 to 6
- blocks: float32 [768, 4, 36864], P('dom'), may hold values from -0.21875 to 0.21875
- columns: int32 [768, 4], P('dom'), may hold values from 0 to 767, as said below
- row_source: int32 [768], P('dom'), may hold values from 0 to 767, each once
- inverses: bfloat16 [512, 36864], P('dom'), may hold values from -0.4375 to 0.4375
- tiles: bfloat16 [512, 8, 36864], P('dom'), may hold values from -0.15625 to 0.15625
- targets: int32 [512, 8], P('dom'), may hold values from 0 to 255, as said below
Outputs:
- level_solution: bfloat16 [512, 64, 192], P('dom', 'rhs')
- ancestor_rhs: float32 [256, 64, 192], P('dom', 'rhs')
- residual_rms: float32 [], replicated
Inputs may be any that keep to these rules, and one draw needn't show every extreme that they name: `columns`: for a block row in partition d (rows d * 12 to d * 12 + 11), every column lies in partitions d - 1 to d + 1. `targets`: ancestor block t is held by owner t // 4. Of the 64 tiles of one owner, at most 2 target blocks of any one owner, and one owner receives exactly 2 tiles from every owner.
All inputs are finite; a program needn't handle non-finite values.
Results may differ from a plain program's by a relative error of at most 0.0055.
Values may be sent and summed in bfloat16 or wider, within the bound.
No kernel may reach another device: no remote copies, remote signals or barrier semaphores. Data moves between devices by JAX's collectives and lax.ppermute only.
A program may use at most 128 MiB of HBM per device.

v0:
```python
import jax
import jax.numpy as jnp
from jax import lax
from jax.sharding import PartitionSpec as P

B = 192
LEAF = 8
ANC = 4
UPD = 8
P_SIZE = 12


def padded(cells, sides, width):
    for axis, dim in sides:
        count = lax.axis_size(axis)
        ends = count - 1
        head = lax.slice_in_dim(cells, 0, width, axis=dim)
        tail = lax.slice_in_dim(cells, cells.shape[dim] - width, cells.shape[dim], axis=dim)
        cells = jnp.concatenate(
            [
                lax.ppermute(tail, axis, [(i, (i + 1) % count) for i in range(ends)]),
                cells,
                lax.ppermute(head, axis, [((i + 1) % count, i) for i in range(ends)]),
            ],
            axis=dim,
        )
    return cells


def on_device(solution, loads, blocks, columns, row_source, inverses, tiles, targets):
    case_count = solution.shape[1]
    dom_count = lax.axis_size("dom")
    device_index = lax.axis_index("dom")
    window = padded(solution, (("dom", 0),), P_SIZE)
    local_columns = columns - (device_index * P_SIZE - P_SIZE)
    neighbours = jnp.take(window, local_columns, axis=0)
    square_blocks = blocks.reshape(blocks.shape[0], blocks.shape[1], B, B)
    products = jnp.einsum(
        "gjae,gjce->gca", square_blocks, neighbours, precision=lax.Precision.HIGHEST
    )
    residual = loads - products
    squares = lax.psum(jnp.sum(residual * residual), ("dom", "rhs"))
    residual_rms = jnp.sqrt(squares / (P_SIZE * dom_count * case_count * lax.axis_size("rhs") * B))
    rounded = residual.astype(jnp.bfloat16).reshape(P_SIZE, case_count * B)
    shard_rows = lax.all_gather(rounded, "dom", axis=0, tiled=True)
    width_rows = shard_rows.shape[0]
    select = (row_source[:, None] == jnp.arange(width_rows, dtype=jnp.int32)[None, :]).astype(
        jnp.bfloat16
    )
    relaid = jnp.dot(select, shard_rows, preferred_element_type=jnp.float32)
    relaid = relaid.astype(jnp.bfloat16).reshape(P_SIZE, case_count, B)
    leaf_rows = relaid[:LEAF]
    ancestor_rows = relaid[LEAF:]
    square_inverses = inverses.reshape(inverses.shape[0], B, B)
    level_solution = jnp.einsum(
        "kae,kce->kca", square_inverses, leaf_rows, preferred_element_type=jnp.float32
    ).astype(jnp.bfloat16)
    square_tiles = tiles.reshape(tiles.shape[0], tiles.shape[1], B, B)
    updates = jnp.einsum(
        "kmae,kce->kmca", square_tiles, level_solution, preferred_element_type=jnp.float32
    )
    tile_count = LEAF * UPD
    updates = updates.reshape(tile_count, case_count * B)
    flat_targets = targets.reshape(tile_count)
    select = (
        jnp.arange(ANC * lax.axis_size("dom"), dtype=jnp.int32)[:, None] == flat_targets[None, :]
    ).astype(jnp.float32)
    summed_rows = jnp.dot(select, updates, precision=lax.Precision.HIGHEST)
    summed = lax.psum_scatter(
        summed_rows.reshape(ANC * lax.axis_size("dom"), case_count, B),
        "dom",
        scatter_dimension=0,
        tiled=True,
    )
    ancestor_rhs = ancestor_rows.astype(jnp.float32) - summed
    return (level_solution, ancestor_rhs, residual_rms)


def solution(mesh):
    placed = (
        P("dom", "rhs", None),
        P("dom", "rhs", None),
        P("dom", None, None),
        P("dom", None),
        P("dom"),
        P("dom", None),
        P("dom", None, None),
        P("dom", None),
    )
    return jax.shard_map(
        on_device,
        mesh=mesh,
        in_specs=placed,
        out_specs=(P("dom", "rhs", None), P("dom", "rhs", None), P()),
        check_vma=False,
    )
```

profile of v0, /device:TPU:1, one launch (start us, length us, event | category | flops | bytes accessed | tf_op | source)
XLA Modules:
  0.0 290.4 jit_solution(17247273464740744710)
XLA Ops:
  7.2 0.0 all-gather.3.cloned.1.call-start
  7.2 4.9 %collective-permute-start = (f32[12,16,192]{2,1,0:T(8,128)}, f32[12,16,192]{2,1,0:T(8,128)S(1)}, u32[]{:S(2)}, u32[]{:S(2)}) collective-permute-start(f32[12,16,192]{2,1,0:T(8,128)} %param.8), channel_id=1, source_target_pairs={{0,4},{4,8},{8,12},{12,16},{16,20},{20,24},{24,28},{28,32},{32,36}... | collective-permute-start | bytes 442376 | tf_op jit(solution)/shard_map/ppermute | solution.py:21
  12.2 1.9 collective-permute-start.1
  14.1 0.7 compare_and_fusion
  14.8 0.1 copy.21
  14.9 0.1 reshape.43
  15.0 0.1 copy.20
  15.1 0.0 copy-start.2
  15.1 0.0 copy-start.3
  15.1 10.1 %reshape.35 = f32[12,4,192,192]{3,2,1,0:T(8,128)} reshape(f32[12,4,36864]{2,1,0:T(4,128)} %param.10) | data formatting | bytes 14155776 | tf_op jit(solution)/shard_map/reshape | solution.py:37
  25.2 0.0 collective-permute-done
  25.2 0.0 collective-permute-done.1
  25.2 0.0 copy-done.2
  25.2 0.0 copy-start
  25.2 0.6 gather_fusion
  25.9 0.0 copy-done.3
  25.9 10.6 %multiply_reduce_fusion = (f32[]{:T(128)}, bf16[12,16,192]{2,1,0:T(8,128)(2,1)S(1)}) fusion(f32[12,16,192]{2,1,0:T(8,128)S(1)} %copy-done.3, f32[12,4,192,192]{3,2,1,0:T(8,128)} %reshape.35, f32[12,4,16,192]{3,2,1,0:T(8,128)S(1)} %bitcast.27, pred[12,4]{1,0:T(8,128)(4,1)S(1)} %copy.20), kind=kOutput, calls=%fused_computation.12 | convolution fusion | flops 340033536 | bytes 7888948 | tf_op jit(solution)/shard_map/gjae,gjce->gca/dot_general | solution.py:38
  36.5 0.8 reshape.51
  37.3 0.0 copy-start.4
  37.3 0.0 all-gather.3.cloned.1.call-update
  37.3 0.2 reduce-scatter.2.cloned.1.call-start
  37.5 0.0 copy-done
  37.5 0.9 reshape.37
  38.4 10.8 %reshape.38 = bf16[8,8,192,192]{3,2,1,0:T(8,128)(2,1)} reshape(bf16[8,8,36864]{2,1,0:T(8,128)(2,1)} %param.14) | data formatting | bytes 9437184 | tf_op jit(solution)/shard_map/reshape | solution.py:58
  49.2 0.0 copy-done.4
  49.2 0.0 copy-start.5
  49.2 0.1 eq.32
  49.3 73.4 %all-gather.3.cloned.1.call-done = bf16[64,12,3072]{2,1,0:T(8,128)(2,1)} async-done(((bf16[1,12,3072]{2,1,0:T(8,128)(2,1)}), bf16[64,12,3072]{2,1,0:T(8,128)(2,1)}) %all-gather.3.cloned.1.call-update) | async-done | bytes 4718608 | tf_op jit(solution)/shard_map/all_gather | solution.py:45
  122.7 7.5 %reshape.52 = bf16[768,3072]{1,0:T(8,128)(2,1)} reshape(bf16[64,12,3072]{2,1,0:T(8,128)(2,1)} %all-gather.3.cloned.1.call-done) | data formatting | bytes 9437184
  130.2 0.0 copy-done.5
  130.2 3.1 %convolution_convert_fusion = bf16[12,3072]{1,0:T(8,128)(2,1)S(1)} fusion(bf16[768,3072]{1,0:T(8,128)(2,1)} %reshape.52, s32[12]{0:T(128)S(1)} %copy-done.5), kind=kOutput, calls=%fused_computation.1 | convolution fusion | flops 56669184 | bytes 4792368 | tf_op jit(solution)/shard_map/dot_general | solution.py:50
  133.3 0.1 slice.11
  133.4 0.3 convolution_convert_fusion.1
  133.7 0.0 copy-start.1
  133.7 4.5 %convolution_bitcast_fusion = f32[8,8,16,192]{3,2,1,0:T(8,128)S(1)} fusion(bf16[8,8,192,192]{3,2,1,0:T(8,128)(2,1)} %reshape.38, bf16[8,16,192]{2,1,0:T(8,128)(2,1)S(1)} %convolution_convert_fusion.1), kind=kOutput, calls=%fused_computation.2 | convolution fusion | flops 75497472 | bytes 5554176 | tf_op jit(solution)/shard_map/kmae,kce->kmca/dot_general | solution.py:59
  138.3 0.4 reshape.39
  138.7 0.5 dot_general.24
  139.2 2.3 fusion.1
  141.5 0.0 copy-done.1
  141.5 4.4 %copy.23 = f32[256,16,192]{2,1,0:T(8,128)} copy(f32[256,16,192]{2,0,1:T(8,128)S(1)} %fusion.1) | data formatting | bytes 6291456 | tf_op jit(solution)/shard_map/dot_general | solution.py:68
  145.9 0.0 reduce-scatter.2.cloned.1.call-update
  145.9 74.7 %psum.7 = f32[]{:T(128)} all-reduce(f32[]{:T(128)} %get-tuple-element.11), channel_id=1, replica_groups=mesh['dom'=64,'rhs'=4] {'dom','rhs'}, use_global_device_ids=true, to_apply=%region_2.3 | all-reduce | flops 1 | bytes 8 | tf_op jit(solution)/shard_map/psum | solution.py:42
  221.3 0.1 reshape.40
  221.4 59.6 %reduce-scatter.2.cloned.1.call-done = f32[4,16,192]{2,1,0:T(8,128)} async-done(((f32[256,16,192]{2,1,0:T(8,128)}), f32[4,16,192]{2,1,0:T(8,128)}) %reduce-scatter.2.cloned.1.call-update) | async-done | bytes 49168 | tf_op jit(solution)/shard_map/reduce_scatter | solution.py:69
  281.0 1.5 sub.19
  (4 shorter events, 0.1 us)
Async XLA Ops:
  7.2 115.5 %all-gather.3.cloned.1.call-start = ((), (), s32[]{:S(2)}) async-start(), calls=%async_computation.2 | async-start | bytes 6389760 | tf_op jit(solution)/shard_map/all_gather | solution.py:45
  7.2 18.0 %collective-permute-start = (f32[12,16,192]{2,1,0:T(8,128)}, f32[12,16,192]{2,1,0:T(8,128)S(1)}, u32[]{:S(2)}, u32[]{:S(2)}) collective-permute-start(f32[12,16,192]{2,1,0:T(8,128)} %param.8), channel_id=1, source_target_pairs={{0,4},{4,8},{8,12},{12,16},{16,20},{20,24},{24,28},{28,32},{32,36}... | collective-permute-start | bytes 442376 | tf_op jit(solution)/shard_map/ppermute | solution.py:21
  12.2 13.0 %collective-permute-start.1 = (f32[12,16,192]{2,1,0:T(8,128)}, f32[12,16,192]{2,1,0:T(8,128)S(1)}, u32[]{:S(2)}, u32[]{:S(2)}) collective-permute-start(f32[12,16,192]{2,1,0:T(8,128)} %param.8), channel_id=1, source_target_pairs={{4,0},{8,4},{12,8},{16,12},{20,16},{24,20},{28,24},{32,28},{36,32}... | collective-permute-start | bytes 442376 | tf_op jit(solution)/shard_map/ppermute | solution.py:23
  15.1 10.1 %copy-start.2 = (f32[12,16,192]{2,1,0:T(8,128)S(1)}, f32[12,16,192]{2,1,0:T(8,128)}, u32[]{:S(2)}) copy-start(f32[12,16,192]{2,1,0:T(8,128)} %param.8) | copy-start | bytes 442372
  15.1 10.8 %copy-start.3 = (f32[12,16,192]{2,1,0:T(8,128)S(1)}, f32[12,16,192]{2,1,0:T(8,128)}, u32[]{:S(2)}) copy-start(f32[12,16,192]{2,1,0:T(8,128)} %param.9) | copy-start | bytes 442372
  25.2 12.3 %copy-start = (bf16[8,36864]{1,0:T(8,128)(2,1)S(1)}, bf16[8,36864]{1,0:T(8,128)(2,1)}, u32[]{:S(2)}) copy-start(bf16[8,36864]{1,0:T(8,128)(2,1)} %param.13) | copy-start | bytes 1769476
  37.3 11.9 %copy-start.4 = (s32[8,8]{1,0:T(8,128)S(1)}, s32[8,8]{1,0:T(8,128)}, u32[]{:S(2)}) copy-start(s32[8,8]{1,0:T(8,128)} %param.15) | copy-start | bytes 772
  37.3 243.7 %reduce-scatter.2.cloned.1.call-start = ((), (), s32[]{:S(2)}) async-start(), calls=%async_computation.1 | async-start | bytes 4259840 | tf_op jit(solution)/shard_map/reduce_scatter | solution.py:69
  49.2 81.0 %copy-start.5 = (s32[12]{0:T(128)S(1)}, s32[12]{0:T(128)}, u32[]{:S(2)}) copy-start(s32[12]{0:T(128)} %param.12) | copy-start | bytes 148
  133.7 7.8 %copy-start.1 = (bf16[8,16,192]{2,1,0:T(8,128)(2,1)}, bf16[8,16,192]{2,1,0:T(8,128)(2,1)S(1)}, u32[]{:S(2)}) copy-start(bf16[8,16,192]{2,1,0:T(8,128)(2,1)S(1)} %convolution_convert_fusion.1) | copy-start | bytes 147460
Sparse Core Ops, SparseCore 0:
  37.4 85.1 all-gather.2
  146.0 134.8 reduce-scatter.1
where the time goes:
time: 296 us; the launch traced here: 290 us
  waiting for transfers between devices  133 us (45%)
  blocking collectives  74.7 us (25%)
  local copies, waits for them, and re-layouts  36.5 us (12%)
  matrix products  20.9 us (7%)
  between operations  16 us (5%)
  starting transfers between devices  7.12 us (2%)
    psum x1, blocking collectives, on_device(): squares = lax.psum(jnp.sum(residual * residual), ('dom', 'rhs'))  74.7 us
    all_gather x1, waiting for transfers between devices, on_device(): shard_rows = lax.all_gather(rounded, 'dom', axis=0, tiled=True)  73.4 us
    reduce_scatter x1, waiting for transfers between devices, on_device(): lax.psum_scatter(summed_rows.reshape(ANC * lax.axis_size('dom'), case_cou...  59.6 us
    reshape x1, local copies, waits for them, and re-layouts, on_device(): square_tiles = tiles.reshape(tiles.shape[0], tiles.shape[1], B, B)  10.8 us
    dot_general x1, matrix products, on_device(): jnp.einsum('gjae,gjce->gca', square_blocks, neighbours, precision=lax.Pre...  10.6 us
    reshape x1, local copies, waits for them, and re-layouts, on_device(): square_blocks = blocks.reshape(blocks.shape[0], blocks.shape[1], B, B)  10.1 us
    unnamed x14, local copies, waits for them, and re-layouts  8.32 us
  transfers between devices with their start and end apart: 4, of which 2 were waited for; matrix products, arithmetic and copies ran while one was open for 8% of the time, Pallas kernels for 0%

commit v1 on v0

v1 whole, which is shorter than its diff:
```python
import jax
import jax.numpy as jnp
from jax import lax
from jax.experimental import pallas as pl
from jax.experimental.pallas import tpu as pltpu
from jax.sharding import PartitionSpec as P

B = 192
LEAF = 8
ANC = 4
NNZ = 4
UPD = 8
P_SIZE = 12
CASES = 16
DOM = 64
N_X, N_Z, N_CORE = 4, 8, 2
GROUP = N_X * N_CORE
LANES = 128
ROWS = 8
PAIRS = B // 2
BF16 = jnp.bfloat16
F32 = jnp.float32
NT = (((1,), (1,)), ((), ()))


def iota(shape, dim):
    return lax.broadcasted_iota(jnp.int32, shape, dim)


def one_hot(condition):
    return jnp.where(condition, 1.0, 0.0).astype(BF16)


def halves(x):
    high = x.astype(BF16)
    return high, (x - high.astype(F32)).astype(BF16)


def dot(a, b):
    return jnp.dot(a, b, preferred_element_type=F32)


def residual_kernel(columns, blocks, before, own, after, loads, info, out, cells, placed, message):
    spread_row, spread_col = iota((B, 768), 0), iota((B, 768), 1)
    spread = one_hot((spread_col == spread_row) | (spread_col == spread_row + 576))

    def place(i, carry):
        parts = []
        for source in (before, own, after, loads):
            parts.extend(halves(source[i]))
        both = dot(jnp.concatenate(parts, axis=0), spread)
        for s in range(4):
            pieces = []
            for part in range(2):
                for v in range(2):
                    row = s * 32 + part * 16 + v * 8
                    pieces.append(both[row:row + 8, :384])
                    pieces.append(both[row:row + 8, 384:])
            cells[s * P_SIZE + i] = jnp.concatenate(pieces, axis=0).astype(BF16)
        return carry

    lax.fori_loop(0, P_SIZE, place, 0)

    unit_row, unit_col = iota((PAIRS, 384), 0), iota((PAIRS, 384), 1)
    pair = (unit_row % 32) * 3 + unit_row // 32
    unit = one_hot((unit_col == 2 * pair) | (unit_col == 2 * pair + B + 1))
    put_row, put_col = iota((32, 512), 0), iota((32, 512), 1)

    placed[...] = jnp.zeros((PAIRS, 512), F32)

    def block_row(g, squares):
        total = lax.dot_general(unit, cells[3 * P_SIZE + g], NT, preferred_element_type=F32)
        low_total = jnp.zeros((PAIRS, 32), F32)
        for j in range(NNZ):
            cell = columns[g, j]
            wide = []
            for k in range(3):
                start = g * 1152 + 12 * k + j
                wide.append(jnp.concatenate(
                    [blocks[pl.ds(start + 4 * t, 32, stride=36), :] for t in range(3)], axis=1))
            high, low = halves(jnp.concatenate(wide, axis=0))
            right = cells[cell]
            total = total - lax.dot_general(high, right, NT, preferred_element_type=F32)
            low_total = low_total + lax.dot_general(low, right[:32], NT, preferred_element_type=F32)
        residual = total[:, :32] + total[:, 32:] - low_total
        put = one_hot(put_col == (put_row // 16) * 256 + (g // 6) * LANES + (g % 6) * 16 + put_row % 16)
        placed[...] += dot(residual.astype(BF16), put)
        return squares + jnp.sum(residual * residual, axis=0, keepdims=True)

    squares = lax.fori_loop(0, P_SIZE, block_row, jnp.zeros((1, 32), F32))
    whole = jnp.sum(squares, axis=1, keepdims=True)
    first = whole.astype(BF16).astype(F32)
    second = (whole - first).astype(BF16).astype(F32)
    third = whole - first - second
    lane = iota((DOM, LANES), 1)
    for v in range(2):
        for k in range(3):
            for t in range(2):
                message[pl.ds(v * 256 + 2 * k + t, 32, stride=ROWS), :] = placed[
                    k * 32:(k + 1) * 32, v * 256 + t * LANES:v * 256 + (t + 1) * LANES]
    message[pl.ds(6, DOM, stride=ROWS), :] = jnp.broadcast_to(info[...], (DOM, LANES))
    message[pl.ds(7, DOM, stride=ROWS), :] = jnp.where(
        lane == 0, first, jnp.where(lane == 1, second, jnp.where(lane == 2, third, 0.0)))
    out[...] = message[...].astype(BF16)


def permute_kernel(received, out, notes, squares, wide, message):
    wide[...] = received[...].astype(F32)
    info = wide[pl.ds(6, DOM, stride=ROWS), :]
    notes[...] = info
    squares[...] = jnp.broadcast_to(jnp.sum(wide[pl.ds(7, DOM, stride=ROWS), :]).reshape(1, 1), (1, LANES))
    rows = jnp.concatenate(
        [wide[pl.ds(s, DOM, stride=ROWS), :].astype(BF16) for s in range(6)], axis=1)
    lane = iota((DOM, LANES), 1)
    source = iota((DOM, DOM), 1).astype(F32)
    place = iota((DOM, 256), 1)
    place = jnp.where(place % LANES < 96, (place // LANES) * 6 + (place % LANES) // 16, -1).astype(F32)
    fold_row, fold_col = iota((256, LANES), 0), iota((256, LANES), 1)
    for t in range(2):
        moved = jnp.zeros((3 * DOM, LANES), F32)
        for i in range(6):
            slot = 6 * t + i
            device = jnp.sum(jnp.where(lane == 64 + slot, info, 0.0), axis=1, keepdims=True)
            row = jnp.sum(jnp.where(lane == 76 + slot, info, 0.0), axis=1, keepdims=True)
            taken = dot(one_hot(device == source), rows)
            keep = row == place
            kept = jnp.concatenate(
                [jnp.where(keep, taken[:, k * 256:(k + 1) * 256], 0.0) for k in range(3)], axis=0)
            fold = one_hot((fold_row % 16 == fold_col % 16) & (fold_col // 16 == i))
            moved = moved + dot(kept.astype(BF16), fold)
        for k in range(3):
            message[pl.ds(2 * k + t, DOM, stride=ROWS), :] = moved[k * DOM:(k + 1) * DOM]
    for s in (6, 7):
        message[pl.ds(s, DOM, stride=ROWS), :] = jnp.zeros((DOM, LANES), F32)
    out[...] = message[...].astype(BF16)


def update_kernel(received, inverses, tiles, level, ancestors, out, wide, leaf, rest, right):
    wide[...] = received[...].astype(F32)
    slabs = []
    for k in range(3):
        slabs.append(jnp.concatenate(
            [wide[pl.ds(v * 256 + 2 * k + t, 32, stride=ROWS), :] for v in range(2) for t in range(2)],
            axis=1))
    slab = jnp.concatenate(slabs, axis=0).astype(BF16)
    row, col = iota((512, 512), 0), iota((512, 512), 1)
    inner = row % LANES
    slot = (row // LANES) % 2 * 6 + inner // 16
    target = (row // 8) % 2 * 256 + slot * 16 + (row // 256) * 8 + row % 8
    spread = dot(slab, one_hot((col == target) & (inner < 96)))
    for k in range(3):
        for par in range(2):
            part = spread[k * 32:(k + 1) * 32, par * 256:(par + 1) * 256]
            leaf[pl.ds(2 * k + par, 32, stride=6), :] = part[:, :LANES]
            rest[pl.ds(2 * k + par, 32, stride=6), :] = part[:, LANES:]

    def doubled(x):
        zeros = jnp.zeros_like(x)
        return jnp.concatenate(
            [jnp.concatenate([x, zeros], axis=1), jnp.concatenate([zeros, x], axis=1)], axis=0)

    def left(ref, start, count):
        return jnp.concatenate(
            [ref[pl.ds(start, count), t].reshape(count * 8, LANES) for t in range(3)], axis=1)

    solved = dot(left(inverses, 0, PAIRS), doubled(leaf[...].astype(BF16)))
    own = iota((768, 256), 0) % 8 == (iota((768, 256), 1) % LANES) // 16
    solved = jnp.where(own, solved, 0.0).astype(BF16)
    gather = one_hot(iota((B, 768), 1) // 8 == iota((B, 768), 0) // 2)
    solved = dot(gather, solved)
    solved = jnp.where(iota((B, LANES), 0) % 2 == 0, solved[:, :LANES], solved[:, LANES:])
    unit = one_hot(iota((LANES, LANES), 0) == iota((LANES, LANES), 1))
    level[...] = lax.dot_general(unit, solved.astype(BF16), NT, preferred_element_type=F32).astype(BF16)
    ancestors[...] = lax.dot_general(
        unit[:64], rest[...].astype(BF16), NT, preferred_element_type=F32)
    owner = iota((B, LANES), 1) // 16
    for k in range(LEAF):
        right[k * 384:(k + 1) * 384] = doubled(jnp.where(owner == k, solved, 0.0)).astype(BF16)
    half = PAIRS // 2
    for h in range(2):
        total = jnp.zeros((half * 8, 256), F32)
        for k in range(LEAF):
            total = total + dot(left(tiles, k * PAIRS + h * half, half), right[k * 384:(k + 1) * 384])
        out[h * half * 8:(h + 1) * half * 8] = total.astype(BF16)


def sum_kernel(received, targets, out):
    select = one_hot(targets[...] == iota((256, 512), 0).astype(F32))
    owner = (iota((64, 256), 1) % LANES) // 16
    group = iota((256, LANES), 1) // 16
    for tile in range(3):
        packed = jnp.zeros((256, LANES), F32)
        for part in range(4):
            pair = tile * 4 + part
            rows = jnp.concatenate(
                [received[s, pair * 8:(pair + 1) * 8, :].astype(F32) for s in range(GROUP)], axis=0)
            right = jnp.concatenate(
                [jnp.where(owner == k, rows, 0.0) for k in range(LEAF)], axis=0).astype(BF16)
            summed = dot(select, right)
            for par in range(2):
                one = summed[:, par * LANES:(par + 1) * LANES]
                for shift in (64, 32, 16):
                    one = one + pltpu.roll(one, shift, 1)
                packed = jnp.where(group == part * 2 + par, one, packed)
        out[:, tile * LANES:(tile + 1) * LANES] = packed.astype(BF16)


def final_kernel(received, ancestors, out):
    place = iota((32, 256), 1)
    source, block = place // ANC, place % ANC
    group = source // (N_Z * N_CORE) * N_CORE + source % N_CORE
    row = iota((32, 256), 0)
    pick = one_hot((row // GROUP == block) & (row % GROUP == group))
    summed = dot(pick, received[...])
    own = iota((CASES, 384), 1) % CASES == iota((CASES, 384), 0)
    to_row, to_col = iota((384, B), 0), iota((384, B), 1)
    total = jnp.zeros((3 * ANC * CASES, B), F32)
    for q in range(GROUP):
        left = jnp.concatenate(
            [jnp.where(own, jnp.broadcast_to(summed[t * GROUP + q:t * GROUP + q + 1], (CASES, 384)), 0.0)
             for t in range(ANC)], axis=0)
        first = left.astype(BF16)
        second, third = halves(left - first.astype(F32))
        total = total + dot(
            jnp.concatenate([first, second, third], axis=0),
            one_hot(to_col == q * 24 + to_row // 16))
    count = ANC * CASES
    out[...] = ancestors[...] - (total[:count] + total[count:2 * count] + total[2 * count:])


def call(kernel, name, shapes, in_specs, scratch, megabytes=16):
    outs = [jax.ShapeDtypeStruct(*s) for s in shapes]
    return pl.pallas_call(
        kernel,
        out_shape=outs,
        in_specs=in_specs,
        out_specs=[pl.BlockSpec(memory_space=pltpu.VMEM)] * len(outs),
        scratch_shapes=scratch,
        compiler_params=pltpu.CompilerParams(vmem_limit_bytes=megabytes * 2**20),
        name=name,
    )


def on_device(solution, loads, blocks, columns, row_source, inverses, tiles, targets):
    vmem = pl.BlockSpec(memory_space=pltpu.VMEM)
    smem = pl.BlockSpec(memory_space=pltpu.SMEM)
    device = lax.axis_index("dom")
    before = lax.ppermute(solution, "dom", [(i, i + 1) for i in range(DOM - 1)])
    after = lax.ppermute(solution, "dom", [(i + 1, i) for i in range(DOM - 1)])
    local = columns - (device * P_SIZE - P_SIZE)
    natural = blocks.reshape(P_SIZE, NNZ, 288, LANES).transpose(0, 2, 1, 3).reshape(P_SIZE * 1152, LANES)
    info = jnp.concatenate([
        targets.reshape(LEAF * UPD), row_source // P_SIZE, row_source % P_SIZE,
        jnp.zeros((LANES - 88,), jnp.int32)]).astype(F32).reshape(1, LANES)
    (message,) = call(
        residual_kernel, "residual", [((DOM * ROWS, LANES), BF16)],
        [smem] + [vmem] * 6,
        [pltpu.VMEM((4 * P_SIZE, 64, 384), BF16), pltpu.VMEM((PAIRS, 512), F32),
         pltpu.VMEM((DOM * ROWS, LANES), F32)], 24,
    )(local, natural, before, solution, after, loads, info)

    def exchange(x):
        x = x.reshape(DOM, ROWS, LANES)
        return lax.all_to_all(x, "dom", 0, 0, tiled=True).reshape(DOM * ROWS, LANES)

    message, notes, squares = call(
        permute_kernel, "permute",
        [((DOM * ROWS, LANES), BF16), ((DOM, LANES), F32), ((1, LANES), F32)], [vmem],
        [pltpu.VMEM((DOM * ROWS, LANES), F32), pltpu.VMEM((DOM * ROWS, LANES), F32)],
    )(exchange(message))
    for step in (1, 2):
        squares = squares + lax.ppermute(squares, "rhs", [(i, i ^ step) for i in range(4)])
    residual_rms = jnp.sqrt(squares[0, 0] / (DOM * P_SIZE * CASES * 4 * B))

    natural_inverses = inverses.reshape(LEAF, 288, LANES).transpose(1, 0, 2).reshape(PAIRS, 3, LEAF, LANES)
    natural_tiles = tiles.reshape(LEAF, UPD, 288, LANES).transpose(0, 2, 1, 3)
    natural_tiles = natural_tiles.reshape(LEAF * PAIRS, 3, UPD, LANES)
    level, ancestors, message = call(
        update_kernel, "update",
        [((LEAF * CASES, B), BF16), ((ANC * CASES, B), F32), ((PAIRS * UPD, 256), BF16)], [vmem] * 3,
        [pltpu.VMEM((DOM * ROWS, LANES), F32), pltpu.VMEM((B, LANES), F32), pltpu.VMEM((B, LANES), F32),
         pltpu.VMEM((LEAF * 384, 256), BF16)], 24,
    )(exchange(message), natural_inverses, natural_tiles)

    groups = [[(x * N_Z + z) * N_CORE + c for x in range(N_X) for c in range(N_CORE)] for z in range(N_Z)]
    received = lax.all_to_all(
        message.reshape(GROUP, 96, 256), "dom", 0, 0, axis_index_groups=groups, tiled=True)
    z = (device // N_CORE) % N_Z
    near = lax.dynamic_index_in_dim(notes.reshape(N_X, N_Z, N_CORE, LANES), z, axis=1, keepdims=False)
    near = near.reshape(GROUP, LANES)[:, :LEAF * UPD].reshape(GROUP, LEAF, UPD)
    near = near.transpose(1, 0, 2).reshape(1, LEAF * GROUP * UPD)
    (sums,) = call(sum_kernel, "sum", [((DOM * ANC, 384), BF16)], [vmem] * 2, [])(received, near)
    sums = lax.all_to_all(sums.reshape(DOM, ANC, 384), "dom", 0, 0, tiled=True)
    (ancestor_rhs,) = call(final_kernel, "final", [((ANC * CASES, B), F32)], [vmem] * 2, [])(
        sums.reshape(DOM * ANC, 384), ancestors)
    return (level.reshape(LEAF, CASES, B), ancestor_rhs.reshape(ANC, CASES, B), residual_rms)


def solution(mesh):
    placed = (
        P("dom", "rhs", None),
        P("dom", "rhs", None),
        P("dom", None, None),
        P("dom", None),
        P("dom"),
        P("dom", None),
        P("dom", None, None),
        P("dom", None),
    )
    return jax.shard_map(
        on_device,
        mesh=mesh,
        in_specs=placed,
        out_specs=(P("dom", "rhs", None), P("dom", "rhs", None), P()),
        check_vma=False,
    )
```

time: 296 us -> 105 us (0.35); the launches traced: 290 us -> 104 us
  waiting for transfers between devices: 133 us -> 17.4 us
  blocking collectives: 74.7 us -> 36.7 us
  local copies, waits for them, and re-layouts: 36.5 us -> 7.39 us
  matrix products: 20.9 us -> 0 us
  Pallas kernels: 0 us -> 19.9 us
  between operations: 16 us -> 1.92 us
  starting transfers between devices: 7.12 us -> 20 us
    psum x1 -> x0, blocking collectives: 74.7 us -> none  [on_device(): squares = lax.psum(jnp.sum(residual * residual), ('dom', 'rhs'))]
    all_gather x1 -> x0, waiting for transfers between devices: 73.4 us -> none  [on_device(): shard_rows = lax.all_gather(rounded, 'dom', axis=0, tiled=True)]
    reduce_scatter x1 -> x0, waiting for transfers between devices: 59.6 us -> none  [on_device(): lax.psum_scatter(summed_rows.reshape(ANC * lax.axis_size('dom'), case_cou...]
    all_to_all x0 -> x2, blocking collectives: none -> 36.7 us  [exchange(): return lax.all_to_all(x, 'dom', 0, 0, tiled=True).reshape(DOM * ROWS, LANES)]
    reshape x4, local copies, waits for them, and re-layouts: 22.1 us -> 0.95 us  [the longest x1 0.73 us: on_device(): sums = lax.all_to_all(sums.reshape(DOM, ANC, 384), 'dom', 0, 0, tiled=True)]
    dot_general x5 -> x0, matrix products: 20.9 us -> none  [the longest x1 10.6 us: on_device(): jnp.einsum('gjae,gjce->gca', square_blocks, neighbours, precision=lax.Pre...]
    pallas_call x0 -> x5, Pallas kernels: none -> 19.9 us  [the longest x1 9.41 us: on_device(): call(residual_kernel, 'residual', [((DOM * ROWS, LANES), BF16)], [smem] +...]
    all_to_all x0 -> x2, waiting for transfers between devices: none -> 12 us  [the longest x1 7.91 us: on_device(): lax.all_to_all(message.reshape(GROUP, 96, 256), 'dom', 0, 0, axis_index_g...]
  transfers between devices with their start and end apart: 4 -> 6, of which waited for: 2 -> 5; matrix products, arithmetic and copies ran while one was open for 8% -> 2% of each run, Pallas kernels for 0% -> 0%
where the time goes in v1:
time: 105 us; the launch traced here: 104 us
  blocking collectives  36.7 us (35%)
  starting transfers between devices  20 us (19%)
  Pallas kernels  19.9 us (19%)
  waiting for transfers between devices  17.4 us (17%)
  local copies, waits for them, and re-layouts  7.39 us (7%)
  between operations  1.92 us (2%)
    all_to_all x2, blocking collectives, exchange(): return lax.all_to_all(x, 'dom', 0, 0, tiled=True).reshape(DOM * ROWS, LANES)  36.7 us
    pallas_call x1, Pallas kernels, on_device(): call(residual_kernel, 'residual', [((DOM * ROWS, LANES), BF16)], [smem] +...  9.41 us
    all_to_all x1, waiting for transfers between devices, on_device(): lax.all_to_all(message.reshape(GROUP, 96, 256), 'dom', 0, 0, axis_index_g...  7.91 us
    unnamed x11, local copies, waits for them, and re-layouts  5.66 us
    all_to_all x1, starting transfers between devices, on_device(): sums = lax.all_to_all(sums.reshape(DOM, ANC, 384), 'dom', 0, 0, tiled=True)  5.06 us
    ppermute x1, starting transfers between devices, on_device(): before = lax.ppermute(solution, 'dom', [(i, i + 1) for i in range(DOM - 1)])  4.94 us
    ppermute x2, starting transfers between devices, on_device(): lax.ppermute(squares, 'rhs', [(i, i ^ step) for i in range(4)])  4.3 us
    pallas_call x1, Pallas kernels, on_device(): call(sum_kernel, 'sum', [((DOM * ANC, 384), BF16)], [vmem] * 2, [])  4.24 us
  transfers between devices with their start and end apart: 6, of which 5 were waited for; matrix products, arithmetic and copies ran while one was open for 2% of the time, Pallas kernels for 0%

profile of v1, /device:TPU:1, one launch (start us, length us, event | category | flops | bytes accessed | tf_op | source)
XLA Modules:
  0.0 104.0 jit_solution(7454144935771507886)
XLA Ops:
  0.6 4.9 %collective-permute-start = (f32[12,16,192]{2,1,0:T(8,128)}, f32[12,16,192]{2,1,0:T(8,128)S(1)}, u32[]{:S(2)}, u32[]{:S(2)}) collective-permute-start(f32[12,16,192]{2,1,0:T(8,128)} %own.1), channel_id=1, source_target_pairs={{0,4},{4,8},{8,12},{12,16},{16,20},{20,24},{24,28},{28,32},{32,36}... | collective-permute-start | bytes 442376 | tf_op jit(solution)/shard_map/ppermute | solution.py:248
  5.6 1.9 %collective-permute-start.1 = (f32[12,16,192]{2,1,0:T(8,128)}, f32[12,16,192]{2,1,0:T(8,128)S(1)}, u32[]{:S(2)}, u32[]{:S(2)}) collective-permute-start(f32[12,16,192]{2,1,0:T(8,128)} %own.1), channel_id=1, source_target_pairs={{4,0},{8,4},{12,8},{16,12},{20,16},{24,20},{28,24},{32,28},{36,32}... | collective-permute-start | bytes 442376 | tf_op jit(solution)/shard_map/ppermute | solution.py:249
  7.5 0.8 copy.16
  8.3 0.7 fusion.2
  9.0 0.8 concatenate.16
  9.7 0.1 fusion.1.info
  9.8 0.0 collective-permute-done.before
  9.8 3.0 %collective-permute-done.1.after = f32[12,16,192]{2,1,0:T(8,128)S(1)} collective-permute-done((f32[12,16,192]{2,1,0:T(8,128)}, f32[12,16,192]{2,1,0:T(8,128)S(1)}, u32[]{:S(2)}, u32[]{:S(2)}) %collective-permute-start.1) | collective-permute-done | bytes 147488 | tf_op jit(solution)/shard_map/ppermute | solution.py:249
  12.8 0.0 copy-start
  12.8 3.0 %copy-done = f32[12,4,36864]{2,1,0:T(4,128)S(1)} copy-done((f32[12,4,36864]{2,1,0:T(4,128)S(1)}, f32[12,4,36864]{2,1,0:T(4,128)}, u32[]{:S(2)}) %copy-start) | copy-done | bytes 7077912
  15.8 0.0 copy-start.3
  15.8 0.9 copy-done.3
  16.7 0.0 copy-start.4
  16.7 0.9 copy-done.4
  17.7 0.0 copy-start.1
  17.7 0.0 copy-start.2
  17.7 9.4 %residual.1 = bf16[512,128]{1,0:T(8,128)(2,1)S(1)} custom-call(s32[12,4]{1,0:T(8,128)S(1)} %broadcast_subtract_fusion.columns, f32[13824,128]{1,0:T(8,128)S(1)} %bitcast.36, f32[12,16,192]{2,1,0:T(8,128)S(1)} %collective-permute-done.before, f32[12,16,192]{2,1,0:T(8,128)S(1)} %copy-done.3, f32[12,16,192]{2,1,0:T(8,128)S(1)} %collective-permute-done.1.after, ...), custom_call_target="tpu_custom_call" | custom-call | tf_op jit(solution)/shard_map/residual/pallas_call | solution.py:255
  27.1 21.6 %all_to_all.20 = bf16[64,8,128]{2,1,0:T(8,128)(2,1)S(1)} all-to-all(bf16[64,8,128]{2,1,0:T(8,128)(2,1)S(1)} %bitcast.39), channel_id=1, replica_groups=mesh['dom'=64,'rhs'=4] {'dom'}, dimensions={0} | all-to-all | bytes 262144 | tf_op jit(solution)/shard_map/all_to_all | solution.py:264
  48.7 1.3 %permute.1 = (bf16[512,128]{1,0:T(8,128)(2,1)S(1)}, f32[64,128]{1,0:T(8,128)S(1)}, f32[1,128]{1,0:T(1,128)S(1)}) custom-call(bf16[512,128]{1,0:T(8,128)(2,1)S(1)} %bitcast.41), custom_call_target="tpu_custom_call" | custom-call | tf_op jit(solution)/shard_map/permute/pallas_call | solution.py:266
  50.0 15.0 %all_to_all.21 = bf16[64,8,128]{2,1,0:T(8,128)(2,1)S(1)} all-to-all(bf16[64,8,128]{2,1,0:T(8,128)(2,1)S(1)} %bitcast.42), channel_id=1, replica_groups=mesh['dom'=64,'rhs'=4] {'dom'}, dimensions={0} | all-to-all | bytes 262144 | tf_op jit(solution)/shard_map/all_to_all | solution.py:264
  65.0 0.0 copy-done.1
  65.0 0.0 copy-done.2
  65.0 3.6 %update.1 = (bf16[128,192]{1,0:T(8,128)(2,1)}, f32[64,192]{1,0:T(8,128)S(1)}, bf16[768,256]{1,0:T(8,128)(2,1)}) custom-call(bf16[512,128]{1,0:T(8,128)(2,1)S(1)} %bitcast.40, bf16[96,3,8,128]{3,2,1,0:T(8,128)(2,1)S(1)} %bitcast.38, bf16[768,3,8,128]{3,2,1,0:T(8,128)(2,1)S(1)} %bitcast.37), custom_call_target="tpu_custom_call" | custom-call | tf_op jit(solution)/shard_map/update/pallas_call | solution.py:278
  68.7 3.8 %all-to-all-start.2 = ((bf16[8,96,256]{2,1,0:T(8,128)(2,1)}), bf16[8,96,256]{2,1,0:T(8,128)(2,1)S(1)}, u32[]{:S(2)}, u32[]{:S(2)}) async-start(bf16[8,96,256]{2,1,0:T(8,128)(2,1)} %bitcast.16), calls=%async_computation.2 | async-start | bytes 786432 | tf_op jit(solution)/shard_map/all_to_all | solution.py:286
  72.4 0.1 reshape.133
  72.5 0.1 reshape.134.targets
  72.6 7.9 %all-to-all-done.2.received = bf16[8,96,256]{2,1,0:T(8,128)(2,1)S(1)} async-done(((bf16[8,96,256]{2,1,0:T(8,128)(2,1)}), bf16[8,96,256]{2,1,0:T(8,128)(2,1)S(1)}, u32[]{:S(2)}, u32[]{:S(2)}) %all-to-all-start.2) | async-done | bytes 393248 | tf_op jit(solution)/shard_map/all_to_all | solution.py:286
  80.5 4.2 %sum.1 = bf16[256,384]{1,0:T(8,128)(2,1)S(1)} custom-call(bf16[8,96,256]{2,1,0:T(8,128)(2,1)S(1)} %all-to-all-done.2.received, f32[1,512]{1,0:T(1,128)S(1)} %reshape.134.targets), custom_call_target="tpu_custom_call" | custom-call | tf_op jit(solution)/shard_map/sum/pallas_call | solution.py:292
  84.8 0.7 reshape.135
  85.5 5.1 %all-to-all-start.3 = ((bf16[64,4,384]{2,1,0:T(4,128)(2,1)}), bf16[64,4,384]{2,1,0:T(4,128)(2,1)S(1)}, u32[]{:S(2)}, u32[]{:S(2)}) async-start(bf16[64,4,384]{2,1,0:T(4,128)(2,1)} %reshape.135), calls=%async_computation.3 | async-start | bytes 393216 | tf_op jit(solution)/shard_map/all_to_all | solution.py:293
  90.6 1.4 %collective-permute-start.2 = (f32[1,128]{1,0:T(1,128)S(1)}, f32[1,128]{1,0:T(1,128)S(1)}, u32[]{:S(2)}, u32[]{:S(2)}) collective-permute-start(f32[1,128]{1,0:T(1,128)S(1)} %get-tuple-element.14), channel_id=1, source_target_pairs={{0,1},{1,0},{2,3},{3,2},{4,5},{5,4},{6,7},{7,6},{8,9},{9,8},{10,11... | collective-permute-start | bytes 1544 | tf_op jit(solution)/shard_map/ppermute | solution.py:272
  92.0 1.1 %collective-permute-done.2 = f32[1,128]{1,0:T(1,128)S(1)} collective-permute-done((f32[1,128]{1,0:T(1,128)S(1)}, f32[1,128]{1,0:T(1,128)S(1)}, u32[]{:S(2)}, u32[]{:S(2)}) %collective-permute-start.2) | collective-permute-done | bytes 544 | tf_op jit(solution)/shard_map/ppermute | solution.py:272
  93.1 2.9 %collective-permute-start.3 = (f32[1,128]{1,0:T(1,128)S(1)}, f32[1,128]{1,0:T(1,128)S(1)}, u32[]{:S(2)}, u32[]{:S(2)}) collective-permute-start(f32[1,128]{1,0:T(1,128)S(1)} %add.26), channel_id=1, source_target_pairs={{0,2},{1,3},{2,0},{3,1},{4,6},{5,7},{6,4},{7,5},{8,10},{9,11},{10,... | collective-permute-start | bytes 1544 | tf_op jit(solution)/shard_map/ppermute | solution.py:272
  96.0 1.3 %collective-permute-done.3 = f32[1,128]{1,0:T(1,128)S(1)} collective-permute-done((f32[1,128]{1,0:T(1,128)S(1)}, f32[1,128]{1,0:T(1,128)S(1)}, u32[]{:S(2)}, u32[]{:S(2)}) %collective-permute-start.3) | collective-permute-done | bytes 544 | tf_op jit(solution)/shard_map/ppermute | solution.py:272
  97.4 4.1 %all-to-all-done.3 = bf16[64,4,384]{2,1,0:T(4,128)(2,1)S(1)} async-done(((bf16[64,4,384]{2,1,0:T(4,128)(2,1)}), bf16[64,4,384]{2,1,0:T(4,128)(2,1)S(1)}, u32[]{:S(2)}, u32[]{:S(2)}) %all-to-all-start.3) | async-done | bytes 196640 | tf_op jit(solution)/shard_map/all_to_all | solution.py:293
  101.5 0.1 reshape.136.received
  101.6 1.3 %final.1 = f32[64,192]{1,0:T(8,128)} custom-call(bf16[256,384]{1,0:T(8,128)(2,1)S(1)} %reshape.136.received, f32[64,192]{1,0:T(8,128)S(1)} %get-tuple-element.13.ancestors), custom_call_target="tpu_custom_call" | custom-call | tf_op jit(solution)/shard_map/final/pallas_call | solution.py:294
  (6 shorter events, 0.0 us)
Async XLA Ops:
  0.6 9.2 %collective-permute-start = (f32[12,16,192]{2,1,0:T(8,128)}, f32[12,16,192]{2,1,0:T(8,128)S(1)}, u32[]{:S(2)}, u32[]{:S(2)}) collective-permute-start(f32[12,16,192]{2,1,0:T(8,128)} %own.1), channel_id=1, source_target_pairs={{0,4},{4,8},{8,12},{12,16},{16,20},{20,24},{24,28},{28,32},{32,36}... | collective-permute-start | bytes 442376 | tf_op jit(solution)/shard_map/ppermute | solution.py:248
  5.6 7.2 %collective-permute-start.1 = (f32[12,16,192]{2,1,0:T(8,128)}, f32[12,16,192]{2,1,0:T(8,128)S(1)}, u32[]{:S(2)}, u32[]{:S(2)}) collective-permute-start(f32[12,16,192]{2,1,0:T(8,128)} %own.1), channel_id=1, source_target_pairs={{4,0},{8,4},{12,8},{16,12},{20,16},{24,20},{28,24},{32,28},{36,32}... | collective-permute-start | bytes 442376 | tf_op jit(solution)/shard_map/ppermute | solution.py:249
  12.8 3.0 %copy-start = (f32[12,4,36864]{2,1,0:T(4,128)S(1)}, f32[12,4,36864]{2,1,0:T(4,128)}, u32[]{:S(2)}) copy-start(f32[12,4,36864]{2,1,0:T(4,128)} %param.10) | copy-start | bytes 21233668
  15.8 0.9 copy-start.3
  16.7 0.9 copy-start.4
  17.7 47.4 %copy-start.1 = (bf16[8,8,36864]{2,1,0:T(8,128)(2,1)S(1)}, bf16[8,8,36864]{2,1,0:T(8,128)(2,1)}, u32[]{:S(2)}) copy-start(bf16[8,8,36864]{2,1,0:T(8,128)(2,1)} %param.14) | copy-start | bytes 14155780
  17.7 47.4 %copy-start.2 = (bf16[8,36864]{1,0:T(8,128)(2,1)S(1)}, bf16[8,36864]{1,0:T(8,128)(2,1)}, u32[]{:S(2)}) copy-start(bf16[8,36864]{1,0:T(8,128)(2,1)} %param.13) | copy-start | bytes 1769476
  68.7 11.9 %all-to-all-start.2 = ((bf16[8,96,256]{2,1,0:T(8,128)(2,1)}), bf16[8,96,256]{2,1,0:T(8,128)(2,1)S(1)}, u32[]{:S(2)}, u32[]{:S(2)}) async-start(bf16[8,96,256]{2,1,0:T(8,128)(2,1)} %bitcast.16), calls=%async_computation.2 | async-start | bytes 786432 | tf_op jit(solution)/shard_map/all_to_all | solution.py:286
  85.5 16.0 %all-to-all-start.3 = ((bf16[64,4,384]{2,1,0:T(4,128)(2,1)}), bf16[64,4,384]{2,1,0:T(4,128)(2,1)S(1)}, u32[]{:S(2)}, u32[]{:S(2)}) async-start(bf16[64,4,384]{2,1,0:T(4,128)(2,1)} %reshape.135), calls=%async_computation.3 | async-start | bytes 393216 | tf_op jit(solution)/shard_map/all_to_all | solution.py:293
  90.6 2.5 %collective-permute-start.2 = (f32[1,128]{1,0:T(1,128)S(1)}, f32[1,128]{1,0:T(1,128)S(1)}, u32[]{:S(2)}, u32[]{:S(2)}) collective-permute-start(f32[1,128]{1,0:T(1,128)S(1)} %get-tuple-element.14), channel_id=1, source_target_pairs={{0,1},{1,0},{2,3},{3,2},{4,5},{5,4},{6,7},{7,6},{8,9},{9,8},{10,11... | collective-permute-start | bytes 1544 | tf_op jit(solution)/shard_map/ppermute | solution.py:272
  93.1 4.2 %collective-permute-start.3 = (f32[1,128]{1,0:T(1,128)S(1)}, f32[1,128]{1,0:T(1,128)S(1)}, u32[]{:S(2)}, u32[]{:S(2)}) collective-permute-start(f32[1,128]{1,0:T(1,128)S(1)} %add.26), channel_id=1, source_target_pairs={{0,2},{1,3},{2,0},{3,1},{4,6},{5,7},{6,4},{7,5},{8,10},{9,11},{10,... | collective-permute-start | bytes 1544 | tf_op jit(solution)/shard_map/ppermute | solution.py:272

commit v2 on v1

v2 whole, which is shorter than its diff:
```python
import jax
import jax.numpy as jnp
from jax import lax
from jax.experimental import pallas as pl
from jax.experimental.pallas import tpu as pltpu
from jax.sharding import PartitionSpec as P

B = 192
LEAF = 8
ANC = 4
NNZ = 4
UPD = 8
P_SIZE = 12
CASES = 16
DOM = 64
N_X, N_Z, N_CORE = 4, 8, 2
GROUP = N_X * N_CORE
LANES = 128
ROWS = 8
PAIRS = B // 2
BF16 = jnp.bfloat16
F32 = jnp.float32
NT = (((1,), (1,)), ((), ()))


def iota(shape, dim):
    return lax.broadcasted_iota(jnp.int32, shape, dim)


def one_hot(condition):
    return jnp.where(condition, 1.0, 0.0).astype(BF16)


def halves(x):
    high = x.astype(BF16)
    return high, (x - high.astype(F32)).astype(BF16)


def dot(a, b):
    return jnp.dot(a, b, preferred_element_type=F32)


def put_cells(x, cells, slot):
    wide, narrow = x[:, :LANES], jnp.concatenate([x[:, LANES:], jnp.zeros((CASES, 64), F32)], axis=1)
    lower = iota((CASES, LANES), 1) < 64
    zeros = jnp.zeros((CASES, LANES), F32)
    turned = pltpu.roll(wide, 64, 1)
    lines = (
        (wide, narrow, zeros),
        (zeros, jnp.where(lower, 0.0, turned), jnp.where(lower, turned, pltpu.roll(narrow, 64, 1))),
    )
    for par in range(2):
        for t in range(3):
            for part, value in enumerate(halves(lines[par][t])):
                row = (2 * par + part) * CASES
                cells[slot, row:row + CASES, t * LANES:(t + 1) * LANES] = value


def residual_kernel(table, blocks, before, after, rows, out,
                    wide, cells, load_cells, message, sems):
    count = NNZ * 288
    copies = [pltpu.make_async_copy(blocks.at[pl.ds(g * count, count)], wide.at[pl.ds(g * count, count)],
                                    sems.at[g]) for g in range(P_SIZE)]
    for copy in copies:
        copy.start()

    for i in range(P_SIZE):
        put_cells(before[i], cells, i)
        put_cells(rows[i], cells, P_SIZE + i)
        put_cells(after[i], cells, 2 * P_SIZE + i)
        put_cells(rows[P_SIZE + i], load_cells, i)

    unit_row, unit_col = iota((PAIRS, 384), 0), iota((PAIRS, 384), 1)
    pair = (unit_row % 32) * 3 + unit_row // 32
    unit = one_hot((unit_col == 2 * pair) | (unit_col == 2 * pair + B + 1))
    residuals = ([], [])
    for g in range(P_SIZE):
        if g % 3 == 0:
            for copy in copies[g:g + 3]:
                copy.wait()
        high, low = [], []
        for j in range(NNZ):
            for t in range(3):
                tall = jnp.concatenate(
                    [wide[pl.ds(g * count + 12 * k + j + 4 * t, 32, stride=36), :] for k in range(3)], axis=0)
                first, second = halves(tall)
                high.append(first)
                low.append(second)
        right = jnp.concatenate([cells[table[j, g]] for j in range(NNZ)], axis=1)
        total = lax.dot_general(unit, load_cells[g], NT, preferred_element_type=F32)
        for side in (high, low):
            total = total - lax.dot_general(
                jnp.concatenate(side, axis=1), right, NT, preferred_element_type=F32)
        for par in range(2):
            one = total[:, par * 32:par * 32 + 16] + total[:, par * 32 + 16:par * 32 + 32]
            residuals[par].append(one)

    lane = iota((ROWS, LANES), 1)
    info = jnp.zeros((ROWS, LANES), jnp.int32)
    for k in range(LEAF):
        for m in range(UPD):
            info = jnp.where(lane == k * UPD + m, table[8 + k, m], info)
    for i in range(P_SIZE):
        source = table[4, i]
        info = jnp.where(lane == 64 + i, source // P_SIZE, info)
        info = jnp.where(lane == 76 + i, source % P_SIZE, info)
    info = info.astype(F32)[:1]
    squares = jnp.zeros((PAIRS, LANES), F32)
    for par in range(2):
        ones = residuals[par] + [jnp.zeros((PAIRS, CASES), F32)] * 4
        for t in range(2):
            tile = jnp.concatenate(ones[8 * t:8 * t + 8], axis=1)
            squares = squares + tile * tile
            for k in range(3):
                message[pl.ds(par * 256 + 2 * k + t, 32, stride=ROWS), :] = tile[k * 32:(k + 1) * 32]
    whole = jnp.sum(squares).reshape(1, 1)
    first = whole.astype(BF16).astype(F32)
    second = (whole - first).astype(BF16).astype(F32)
    third = whole - first - second
    lane = iota((DOM, LANES), 1)
    message[pl.ds(6, DOM, stride=ROWS), :] = jnp.broadcast_to(info, (DOM, LANES))
    message[pl.ds(7, DOM, stride=ROWS), :] = jnp.where(
        lane == 0, first, jnp.where(lane == 1, second, jnp.where(lane == 2, third, 0.0)))
    out[...] = message[...].astype(BF16)


def permute_kernel(received, out, notes, squares, wide, message):
    wide[...] = received[...].astype(F32)
    info = wide[pl.ds(6, DOM, stride=ROWS), :]
    notes[...] = info
    squares[...] = jnp.broadcast_to(jnp.sum(wide[pl.ds(7, DOM, stride=ROWS), :]).reshape(1, 1), (1, LANES))
    rows = jnp.concatenate(
        [wide[pl.ds(s, DOM, stride=ROWS), :].astype(BF16) for s in range(6)], axis=1)
    lane = iota((DOM, LANES), 1)
    source = iota((DOM, DOM), 1).astype(F32)
    place = (iota((DOM, 256), 1) // CASES).astype(F32)
    chosen, keep = [], []
    for i in range(P_SIZE):
        device = jnp.sum(jnp.where(lane == 64 + i, info, 0.0), axis=1, keepdims=True)
        row = jnp.sum(jnp.where(lane == 76 + i, info, 0.0), axis=1, keepdims=True)
        chosen.append(one_hot(device == source))
        keep.append(row == place)
    taken = dot(jnp.concatenate(chosen, axis=0), rows)
    fold = one_hot(iota((256, LANES), 0) % CASES == iota((256, LANES), 1) % CASES)
    for k in range(3):
        kept = jnp.concatenate(
            [jnp.where(keep[i], taken[i * DOM:(i + 1) * DOM, k * 256:(k + 1) * 256], 0.0).astype(BF16)
             for i in range(P_SIZE)], axis=0)
        copies = dot(kept, fold)
        for t, count in ((0, LEAF), (1, ANC)):
            moved = jnp.zeros((DOM, LANES), F32)
            for i in range(count):
                at = (LEAF * t + i) * DOM
                moved = jnp.where(lane // CASES == i, copies[at:at + DOM], moved)
            message[pl.ds(2 * k + t, DOM, stride=ROWS), :] = moved
    for s in (6, 7):
        message[pl.ds(s, DOM, stride=ROWS), :] = jnp.zeros((DOM, LANES), F32)
    out[...] = message[...].astype(BF16)


def update_kernel(received, inverses, tiles, squares, level, ancestors, out, squares_out,
                  wide, leaf, rest, right, near, sems, partial):
    copies = [pltpu.make_async_copy(tiles.at[pl.ds(k * PAIRS, PAIRS)], near.at[pl.ds(k * PAIRS, PAIRS)],
                                    sems.at[k]) for k in range(LEAF)]
    for copy in copies:
        copy.start()
    squares_out[...] = squares[...]
    wide[...] = received[...].astype(F32)
    for k in range(3):
        for par in range(2):
            at = pl.ds(2 * k + par, 32, stride=6)
            leaf[at, :] = wide[pl.ds(par * 256 + 2 * k, 32, stride=ROWS), :]
            rest[at, :] = wide[pl.ds(par * 256 + 2 * k + 1, 32, stride=ROWS), :]

    def doubled(x):
        zeros = jnp.zeros_like(x)
        return jnp.concatenate(
            [jnp.concatenate([x, zeros], axis=1), jnp.concatenate([zeros, x], axis=1)], axis=0)

    def left(ref, start, count):
        return jnp.concatenate(
            [ref[pl.ds(start, count), t].reshape(count * 8, LANES) for t in range(3)], axis=1)

    solved = dot(left(inverses, 0, PAIRS), doubled(leaf[...].astype(BF16)))
    own = iota((768, 256), 0) % 8 == (iota((768, 256), 1) % LANES) // 16
    solved = jnp.where(own, solved, 0.0).astype(BF16)
    gather = one_hot(iota((B, 768), 1) // 8 == iota((B, 768), 0) // 2)
    solved = dot(gather, solved)
    solved = jnp.where(iota((B, LANES), 0) % 2 == 0, solved[:, :LANES], solved[:, LANES:])
    unit = one_hot(iota((LANES, LANES), 0) == iota((LANES, LANES), 1))
    level[...] = lax.dot_general(unit, solved.astype(BF16), NT, preferred_element_type=F32).astype(BF16)
    ancestors[...] = lax.dot_general(
        unit[:64], rest[...].astype(BF16), NT, preferred_element_type=F32)
    owner = iota((B, LANES), 1) // 16
    for k in range(LEAF):
        right[k * 384:(k + 1) * 384] = doubled(jnp.where(owner == k, solved, 0.0)).astype(BF16)
    step, band = LEAF // 2, PAIRS // 2
    for first in range(0, LEAF, step):
        for copy in copies[first:first + step]:
            copy.wait()
        for r in range(0, PAIRS, band):
            at = slice(r * 8, (r + band) * 8)
            wide_left = jnp.concatenate(
                [left(near, k * PAIRS + r, band) for k in range(first, first + step)], axis=1)
            total = dot(wide_left, right[first * 384:(first + step) * 384])
            if first == 0:
                partial[at] = total
            else:
                out[at] = (partial[at] + total).astype(BF16)


def sum_kernel(received, targets, squares, out, squares_out, right):
    squares_out[...] = squares[...]
    select = one_hot(targets[...] == iota((256, 512), 0).astype(F32))
    group = iota((64, LANES), 1) // CASES
    for tile in range(3):
        parts = []
        for pair in range(tile * 4, tile * 4 + 4):
            rows = jnp.concatenate(
                [received[s, pair * 8:(pair + 1) * 8, :].astype(F32) for s in range(GROUP)], axis=0)
            parts.extend([rows[:, :LANES], rows[:, LANES:]])
        for step in (4, 2, 1):
            upper = (group // step) % 2 == 1
            turned = list(parts)
            for i in range(8):
                if not i & step:
                    a, b = parts[i], parts[i + step]
                    turned[i] = jnp.where(upper, pltpu.roll(b, step * CASES, 1), a)
                    turned[i + step] = jnp.where(upper, b, pltpu.roll(a, LANES - step * CASES, 1))
            parts = turned
        for k in range(LEAF):
            right[k * 64:(k + 1) * 64, tile * LANES:(tile + 1) * LANES] = parts[k].astype(BF16)
    out[...] = dot(select, right[...]).reshape(DOM, ANC, 384).astype(BF16)


def final_kernel(received, ancestors, out):
    place = iota((32, 256), 1)
    source, block = place // ANC, place % ANC
    group = source // (N_Z * N_CORE) * N_CORE + source % N_CORE
    row = iota((32, 256), 0)
    pick = one_hot((row // GROUP == block) & (row % GROUP == group))
    summed = dot(pick, received[...])
    own = iota((CASES, 384), 1) % CASES == iota((CASES, 384), 0)
    to_row, to_col = iota((384, B), 0), iota((384, B), 1)
    total = jnp.zeros((3 * ANC * CASES, B), F32)
    for q in range(GROUP):
        left = jnp.concatenate(
            [jnp.where(own, jnp.broadcast_to(summed[t * GROUP + q:t * GROUP + q + 1], (CASES, 384)), 0.0)
             for t in range(ANC)], axis=0)
        first = left.astype(BF16)
        second, third = halves(left - first.astype(F32))
        total = total + dot(
            jnp.concatenate([first, second, third], axis=0),
            one_hot(to_col == q * 24 + to_row // 16))
    count = ANC * CASES
    out[...] = ancestors[...] - (total[:count] + total[count:2 * count] + total[2 * count:])


def call(kernel, name, shapes, in_specs, scratch, megabytes=16, cost=None):
    outs = [jax.ShapeDtypeStruct(*s) for s in shapes]
    return pl.pallas_call(
        kernel,
        out_shape=outs,
        in_specs=in_specs,
        out_specs=[pl.BlockSpec(memory_space=pltpu.VMEM)] * len(outs),
        scratch_shapes=scratch,
        compiler_params=pltpu.CompilerParams(vmem_limit_bytes=megabytes * 2**20),
        cost_estimate=cost,
        name=name,
    )


def on_device(solution, loads, blocks, columns, row_source, inverses, tiles, targets):
    vmem = pl.BlockSpec(memory_space=pltpu.VMEM)
    smem = pl.BlockSpec(memory_space=pltpu.SMEM)
    hbm = pl.BlockSpec(memory_space=pltpu.HBM)
    dma = pltpu.SemaphoreType.DMA
    device = lax.axis_index("dom")
    before = lax.ppermute(solution, "dom", [(i, i + 1) for i in range(DOM - 1)])
    after = lax.ppermute(solution, "dom", [(i + 1, i) for i in range(DOM - 1)])
    table = jnp.concatenate([
        jnp.pad(columns.T - (device * P_SIZE - P_SIZE), ((0, 0), (0, LANES - P_SIZE))),
        jnp.pad(row_source.reshape(1, P_SIZE), ((0, 3), (0, LANES - P_SIZE))),
        jnp.pad(targets, ((0, 0), (0, LANES - UPD)))], axis=0)
    natural = blocks.reshape(P_SIZE, NNZ, 288, LANES).transpose(0, 2, 1, 3).reshape(P_SIZE * 1152, LANES)
    natural_inverses = inverses.reshape(LEAF, 288, LANES).transpose(1, 0, 2).reshape(PAIRS, 3, LEAF, LANES)
    natural_tiles = tiles.reshape(LEAF, UPD, 288, LANES).transpose(0, 2, 1, 3)
    natural_tiles = natural_tiles.reshape(LEAF * PAIRS, 3, UPD, LANES)
    (message,) = call(
        residual_kernel, "residual", [((DOM * ROWS, LANES), BF16)],
        [smem, hbm] + [vmem] * 3,
        [pltpu.VMEM((P_SIZE * 1152, LANES), F32),
         pltpu.VMEM((3 * P_SIZE, 64, 384), BF16), pltpu.VMEM((P_SIZE, 64, 384), BF16),
         pltpu.VMEM((DOM * ROWS, LANES), F32), dma((P_SIZE,))], 50,
    )(table, natural, before, after,
      jnp.concatenate([solution, loads], axis=0))

    def exchange(x):
        x = x.reshape(DOM, ROWS, LANES)
        return lax.all_to_all(x, "dom", 0, 0, tiled=True).reshape(DOM * ROWS, LANES)

    def across(x, step):
        return x + lax.ppermute(x, "rhs", [(i, i ^ step) for i in range(4)])

    message, notes, squares = call(
        permute_kernel, "permute",
        [((DOM * ROWS, LANES), BF16), ((DOM, LANES), F32), ((1, LANES), F32)], [vmem],
        [pltpu.VMEM((DOM * ROWS, LANES), F32), pltpu.VMEM((DOM * ROWS, LANES), F32)], 16,
        pl.CostEstimate(flops=4 * 10**9, bytes_accessed=10**6, transcendentals=0),
    )(exchange(message))

    level, ancestors, message, squares = call(
        update_kernel, "update",
        [((LEAF * CASES, B), BF16), ((ANC * CASES, B), F32), ((PAIRS * UPD, 256), BF16), ((1, LANES), F32)],
        [vmem, vmem, hbm, vmem],
        [pltpu.VMEM((DOM * ROWS, LANES), F32), pltpu.VMEM((B, LANES), F32), pltpu.VMEM((B, LANES), F32),
         pltpu.VMEM((LEAF * 384, 256), BF16), pltpu.VMEM((LEAF * PAIRS, 3, UPD, LANES), BF16),
         dma((LEAF,)), pltpu.VMEM((PAIRS * UPD, 256), F32)], 52,
    )(exchange(message), natural_inverses, natural_tiles, across(squares, 1))

    groups = [[(x * N_Z + z) * N_CORE + c for x in range(N_X) for c in range(N_CORE)] for z in range(N_Z)]
    received = lax.all_to_all(
        message.reshape(GROUP, 96, 256), "dom", 0, 0, axis_index_groups=groups, tiled=True)
    z = (device // N_CORE) % N_Z
    near = lax.dynamic_index_in_dim(notes.reshape(N_X, N_Z, N_CORE, LANES), z, axis=1, keepdims=False)
    near = near.reshape(GROUP, LANES)[:, :LEAF * UPD].reshape(GROUP, LEAF, UPD)
    near = near.transpose(1, 0, 2).reshape(1, LEAF * GROUP * UPD)
    sums, squares = call(
        sum_kernel, "sum", [((DOM, ANC, 384), BF16), ((1, LANES), F32)], [vmem] * 3,
        [pltpu.VMEM((512, 384), BF16)],
    )(received, near, across(squares, 2))
    residual_rms = jnp.sqrt(squares[0, 0] / (DOM * P_SIZE * CASES * 4 * B))
    sums = lax.all_to_all(sums, "dom", 0, 0, tiled=True)
    (ancestor_rhs,) = call(final_kernel, "final", [((ANC * CASES, B), F32)], [vmem] * 2, [])(
        sums.reshape(DOM * ANC, 384), ancestors)
    return (level.reshape(LEAF, CASES, B), ancestor_rhs.reshape(ANC, CASES, B), residual_rms)


def solution(mesh):
    placed = (
        P("dom", "rhs", None),
        P("dom", "rhs", None),
        P("dom", None, None),
        P("dom", None),
        P("dom"),
        P("dom", None),
        P("dom", None, None),
        P("dom", None),
    )
    return jax.shard_map(
        on_device,
        mesh=mesh,
        in_specs=placed,
        out_specs=(P("dom", "rhs", None), P("dom", "rhs", None), P()),
        check_vma=False,
    )
```

time: 105 us -> 93.3 us (0.89)
  blocking collectives: 36.7 us -> 21.6 us
  waiting for transfers between devices: 17.4 us -> 27.6 us
  local copies, waits for them, and re-layouts: 7.39 us -> 0.23 us
  Pallas kernels: 19.9 us -> 14.1 us
  starting transfers between devices: 20 us -> 24.9 us
  other arithmetic: 0.76 us -> 2.44 us
    all_to_all x2 -> x1, blocking collectives: 36.7 us -> 21.6 us  [exchange(): return lax.all_to_all(x, 'dom', 0, 0, tiled=True).reshape(DOM * ROWS, LANES)]
    all_to_all x1 -> x2, waiting for transfers between devices: 4.13 us -> 18.5 us  [the longest x1 10.9 us: on_device(): sums = lax.all_to_all(sums, 'dom', 0, 0, tiled=True)]
    pallas_call x2, Pallas kernels: 13.6 us -> 7.03 us  [the longest x1 5.52 us: on_device(): call(residual_kernel, 'residual', [((DOM * ROWS, LANES), BF16)], [smem, h...]
    unnamed x11 -> x2, local copies, waits for them, and re-layouts: 5.66 us -> 0.01 us
    all_to_all x1 -> x2, starting transfers between devices: 5.06 us -> 9.96 us  [the longest x1 5.08 us: on_device(): sums = lax.all_to_all(sums, 'dom', 0, 0, tiled=True)]
    all_to_all x1, waiting for transfers between devices: 7.91 us -> 4.2 us  [on_device(): lax.all_to_all(message.reshape(GROUP, 96, 256), 'dom', 0, 0, axis_index_g...]
    concatenate x1 -> x2, other arithmetic: 0.67 us -> 1.74 us  [the longest x1 1.05 us: on_device(): jnp.concatenate([solution, loads], axis=0)]
  transfers between devices with their start and end apart: 6 -> 7, of which waited for: 5 -> 6; matrix products, arithmetic and copies ran while one was open for 2% -> 3% of each run, Pallas kernels for 0% -> 0%
where the time goes in v2:
time: 93.3 us; the launch traced here: 92.9 us
  waiting for transfers between devices  27.6 us (30%)
  starting transfers between devices  24.9 us (27%)
  blocking collectives  21.6 us (23%)
  Pallas kernels  14.1 us (15%)
  other arithmetic  2.44 us (3%)
  between operations  1.92 us (2%)
    all_to_all x1, blocking collectives, exchange(): return lax.all_to_all(x, 'dom', 0, 0, tiled=True).reshape(DOM * ROWS, LANES)  21.6 us
    all_to_all x1, waiting for transfers between devices, on_device(): sums = lax.all_to_all(sums, 'dom', 0, 0, tiled=True)  10.9 us
    all_to_all x1, waiting for transfers between devices, exchange(): return lax.all_to_all(x, 'dom', 0, 0, tiled=True).reshape(DOM * ROWS, LANES)  7.65 us
    pallas_call x1, Pallas kernels, on_device(): call(residual_kernel, 'residual', [((DOM * ROWS, LANES), BF16)], [smem, h...  5.52 us
    all_to_all x1, starting transfers between devices, on_device(): sums = lax.all_to_all(sums, 'dom', 0, 0, tiled=True)  5.08 us
    ppermute x1, starting transfers between devices, on_device(): before = lax.ppermute(solution, 'dom', [(i, i + 1) for i in range(DOM - 1)])  4.94 us
    all_to_all x1, starting transfers between devices, exchange(): return lax.all_to_all(x, 'dom', 0, 0, tiled=True).reshape(DOM * ROWS, LANES)  4.88 us
    ppermute x2, starting transfers between devices, across(): return x + lax.ppermute(x, 'rhs', [(i, i ^ step) for i in range(4)])  4.3 us
  transfers between devices with their start and end apart: 7, of which 6 were waited for; matrix products, arithmetic and copies ran while one was open for 3% of the time, Pallas kernels for 0%

profile of v2, /device:TPU:1, one launch (start us, length us, event | category | flops | bytes accessed | tf_op | source)
XLA Modules:
  0.0 92.9 jit_solution(17345849129578023956)
XLA Ops:
  0.6 4.9 %collective-permute-start = (f32[12,16,192]{2,1,0:T(8,128)}, f32[12,16,192]{2,1,0:T(8,128)S(1)}, u32[]{:S(2)}, u32[]{:S(2)}) collective-permute-start(f32[12,16,192]{2,1,0:T(8,128)} %param.8), channel_id=1, source_target_pairs={{0,4},{4,8},{8,12},{12,16},{16,20},{20,24},{24,28},{28,32},{32,36}... | collective-permute-start | bytes 442376 | tf_op jit(solution)/shard_map/ppermute | solution.py:279
  5.6 1.9 %collective-permute-start.1 = (f32[12,16,192]{2,1,0:T(8,128)}, f32[12,16,192]{2,1,0:T(8,128)S(1)}, u32[]{:S(2)}, u32[]{:S(2)}) collective-permute-start(f32[12,16,192]{2,1,0:T(8,128)} %param.8), channel_id=1, source_target_pairs={{4,0},{8,4},{12,8},{16,12},{20,16},{24,20},{28,24},{32,28},{36,32}... | collective-permute-start | bytes 442376 | tf_op jit(solution)/shard_map/ppermute | solution.py:280
  7.5 0.7 subtract_bitcast_fusion
  8.2 0.7 pad_add_fusion.table
  8.9 1.0 %pad_maximum_fusion.rows = f32[24,16,192]{2,1,0:T(8,128)S(1)} fusion(f32[12,16,192]{2,1,0:T(8,128)} %param.9, f32[12,16,192]{2,1,0:T(8,128)} %param.8), kind=kLoop, calls=%fused_computation | loop fusion | flops 73728 | bytes 589824 | tf_op jit(solution)/shard_map/concatenate | solution.py:296
  9.9 0.0 collective-permute-done.before
  10.0 2.8 %collective-permute-done.1.after = f32[12,16,192]{2,1,0:T(8,128)S(1)} collective-permute-done((f32[12,16,192]{2,1,0:T(8,128)}, f32[12,16,192]{2,1,0:T(8,128)S(1)}, u32[]{:S(2)}, u32[]{:S(2)}) %collective-permute-start.1) | collective-permute-done | bytes 147488 | tf_op jit(solution)/shard_map/ppermute | solution.py:280
  12.8 5.5 %residual.1 = bf16[512,128]{1,0:T(8,128)(2,1)S(1)} custom-call(s32[16,128]{1,0:T(8,128)S(1)} %pad_add_fusion.table, f32[13824,128]{1,0:T(8,128)} %bitcast.37, f32[12,16,192]{2,1,0:T(8,128)S(1)} %collective-permute-done.before, f32[12,16,192]{2,1,0:T(8,128)S(1)} %collective-permute-done.1.after, f32[24,16,192]{2,1,0:T(8,128)S(1)} %pad_maximum_fusion.rows), custom_call_target="tpu_custom_call" | custom-call | tf_op jit(solution)/shard_map/residual/pallas_call | solution.py:289
  18.3 21.6 %all_to_all.20 = bf16[64,8,128]{2,1,0:T(8,128)(2,1)S(1)} all-to-all(bf16[64,8,128]{2,1,0:T(8,128)(2,1)S(1)} %bitcast.32), channel_id=1, replica_groups=mesh['dom'=64,'rhs'=4] {'dom'}, dimensions={0} | all-to-all | bytes 262144 | tf_op jit(solution)/shard_map/all_to_all | solution.py:300
  39.9 0.0 copy-start
  39.9 1.5 %permute.1 = (bf16[512,128]{1,0:T(8,128)(2,1)}, f32[64,128]{1,0:T(8,128)S(1)}, f32[1,128]{1,0:T(1,128)S(1)}) custom-call(bf16[512,128]{1,0:T(8,128)(2,1)S(1)} %bitcast.34), custom_call_target="tpu_custom_call" | custom-call | flops 4000000000 | bytes 1000000 | tf_op jit(solution)/shard_map/permute/pallas_call | solution.py:305
  41.4 4.9 %all-to-all-start.1 = ((bf16[64,8,128]{2,1,0:T(8,128)(2,1)}), bf16[64,8,128]{2,1,0:T(8,128)(2,1)S(1)}, u32[]{:S(2)}, u32[]{:S(2)}) async-start(bf16[64,8,128]{2,1,0:T(8,128)(2,1)} %bitcast.7), calls=%async_computation.1 | async-start | bytes 262144 | tf_op jit(solution)/shard_map/all_to_all | solution.py:300
  46.3 1.4 %collective-permute-start.2 = (f32[1,128]{1,0:T(1,128)S(1)}, f32[1,128]{1,0:T(1,128)S(1)}, u32[]{:S(2)}, u32[]{:S(2)}) collective-permute-start(f32[1,128]{1,0:T(1,128)S(1)} %get-tuple-element.13), channel_id=1, source_target_pairs={{0,1},{1,0},{2,3},{3,2},{4,5},{5,4},{6,7},{7,6},{8,9},{9,8},{10,11... | collective-permute-start | bytes 1544 | tf_op jit(solution)/shard_map/ppermute | solution.py:303
  47.7 1.3 %collective-permute-done.2 = f32[1,128]{1,0:T(1,128)S(1)} collective-permute-done((f32[1,128]{1,0:T(1,128)S(1)}, f32[1,128]{1,0:T(1,128)S(1)}, u32[]{:S(2)}, u32[]{:S(2)}) %collective-permute-start.2) | collective-permute-done | bytes 544 | tf_op jit(solution)/shard_map/ppermute | solution.py:303
  49.1 7.6 %all-to-all-done.1 = bf16[64,8,128]{2,1,0:T(8,128)(2,1)S(1)} async-done(((bf16[64,8,128]{2,1,0:T(8,128)(2,1)}), bf16[64,8,128]{2,1,0:T(8,128)(2,1)S(1)}, u32[]{:S(2)}, u32[]{:S(2)}) %all-to-all-start.1) | async-done | bytes 131104 | tf_op jit(solution)/shard_map/all_to_all | solution.py:300
  56.7 0.0 copy-done
  56.7 4.3 %update.1 = (bf16[128,192]{1,0:T(8,128)(2,1)}, f32[64,192]{1,0:T(8,128)S(1)}, bf16[768,256]{1,0:T(8,128)(2,1)}, f32[1,128]{1,0:T(1,128)S(1)}) custom-call(bf16[512,128]{1,0:T(8,128)(2,1)S(1)} %bitcast.33, bf16[96,3,8,128]{3,2,1,0:T(8,128)(2,1)S(1)} %bitcast.31, bf16[768,3,8,128]{3,2,1,0:T(8,128)(2,1)} %bitcast.38, f32[1,128]{1,0:T(1,128)S(1)} %add.22.squares), custom_call_target="tpu_custom_call" | custom-call | tf_op jit(solution)/shard_map/update/pallas_call | solution.py:312
  61.0 3.8 %all-to-all-start.2 = ((bf16[8,96,256]{2,1,0:T(8,128)(2,1)}), bf16[8,96,256]{2,1,0:T(8,128)(2,1)S(1)}, u32[]{:S(2)}, u32[]{:S(2)}) async-start(bf16[8,96,256]{2,1,0:T(8,128)(2,1)} %bitcast.16), calls=%async_computation.2 | async-start | bytes 786432 | tf_op jit(solution)/shard_map/all_to_all | solution.py:322
  64.7 2.9 %collective-permute-start.3 = (f32[1,128]{1,0:T(1,128)S(1)}, f32[1,128]{1,0:T(1,128)S(1)}, u32[]{:S(2)}, u32[]{:S(2)}) collective-permute-start(f32[1,128]{1,0:T(1,128)S(1)} %get-tuple-element.17), channel_id=1, source_target_pairs={{0,2},{1,3},{2,0},{3,1},{4,6},{5,7},{6,4},{7,5},{8,10},{9,11},{10,... | collective-permute-start | bytes 1544 | tf_op jit(solution)/shard_map/ppermute | solution.py:303
  67.7 0.1 reshape.82
  67.7 0.1 reshape.83.targets
  67.8 0.8 collective-permute-done.3
  68.6 4.2 %all-to-all-done.2.received = bf16[8,96,256]{2,1,0:T(8,128)(2,1)S(1)} async-done(((bf16[8,96,256]{2,1,0:T(8,128)(2,1)}), bf16[8,96,256]{2,1,0:T(8,128)(2,1)S(1)}, u32[]{:S(2)}, u32[]{:S(2)}) %all-to-all-start.2) | async-done | bytes 393248 | tf_op jit(solution)/shard_map/all_to_all | solution.py:322
  72.8 1.5 %sum.1 = (bf16[64,4,384]{2,1,0:T(4,128)(2,1)}, f32[1,128]{1,0:T(1,128)S(1)}) custom-call(bf16[8,96,256]{2,1,0:T(8,128)(2,1)S(1)} %all-to-all-done.2.received, f32[1,512]{1,0:T(1,128)S(1)} %reshape.83.targets, f32[1,128]{1,0:T(1,128)S(1)} %add.25.squares), custom_call_target="tpu_custom_call" | custom-call | tf_op jit(solution)/shard_map/sum/pallas_call | solution.py:328
  74.3 5.1 %all-to-all-start.3 = ((bf16[64,4,384]{2,1,0:T(4,128)(2,1)}), bf16[64,4,384]{2,1,0:T(4,128)(2,1)S(1)}, u32[]{:S(2)}, u32[]{:S(2)}) async-start(bf16[64,4,384]{2,1,0:T(4,128)(2,1)} %get-tuple-element.18), calls=%async_computation.3 | async-start | bytes 393216 | tf_op jit(solution)/shard_map/all_to_all | solution.py:333
  79.5 10.9 %all-to-all-done.3 = bf16[64,4,384]{2,1,0:T(4,128)(2,1)S(1)} async-done(((bf16[64,4,384]{2,1,0:T(4,128)(2,1)}), bf16[64,4,384]{2,1,0:T(4,128)(2,1)S(1)}, u32[]{:S(2)}, u32[]{:S(2)}) %all-to-all-start.3) | async-done | bytes 196640 | tf_op jit(solution)/shard_map/all_to_all | solution.py:333
  90.4 0.1 reshape.84.received
  90.4 1.3 %final.1 = f32[64,192]{1,0:T(8,128)} custom-call(bf16[256,384]{1,0:T(8,128)(2,1)S(1)} %reshape.84.received, f32[64,192]{1,0:T(8,128)S(1)} %get-tuple-element.19.ancestors), custom_call_target="tpu_custom_call" | custom-call | tf_op jit(solution)/shard_map/final/pallas_call | solution.py:334
  (4 shorter events, 0.0 us)
Async XLA Ops:
  0.6 9.3 %collective-permute-start = (f32[12,16,192]{2,1,0:T(8,128)}, f32[12,16,192]{2,1,0:T(8,128)S(1)}, u32[]{:S(2)}, u32[]{:S(2)}) collective-permute-start(f32[12,16,192]{2,1,0:T(8,128)} %param.8), channel_id=1, source_target_pairs={{0,4},{4,8},{8,12},{12,16},{16,20},{20,24},{24,28},{28,32},{32,36}... | collective-permute-start | bytes 442376 | tf_op jit(solution)/shard_map/ppermute | solution.py:279
  5.6 7.2 %collective-permute-start.1 = (f32[12,16,192]{2,1,0:T(8,128)}, f32[12,16,192]{2,1,0:T(8,128)S(1)}, u32[]{:S(2)}, u32[]{:S(2)}) collective-permute-start(f32[12,16,192]{2,1,0:T(8,128)} %param.8), channel_id=1, source_target_pairs={{4,0},{8,4},{12,8},{16,12},{20,16},{24,20},{28,24},{32,28},{36,32}... | collective-permute-start | bytes 442376 | tf_op jit(solution)/shard_map/ppermute | solution.py:280
  39.9 16.8 %copy-start = (bf16[8,36864]{1,0:T(8,128)(2,1)S(1)}, bf16[8,36864]{1,0:T(8,128)(2,1)}, u32[]{:S(2)}) copy-start(bf16[8,36864]{1,0:T(8,128)(2,1)} %param.13) | copy-start | bytes 1769476
  41.4 15.2 %all-to-all-start.1 = ((bf16[64,8,128]{2,1,0:T(8,128)(2,1)}), bf16[64,8,128]{2,1,0:T(8,128)(2,1)S(1)}, u32[]{:S(2)}, u32[]{:S(2)}) async-start(bf16[64,8,128]{2,1,0:T(8,128)(2,1)} %bitcast.7), calls=%async_computation.1 | async-start | bytes 262144 | tf_op jit(solution)/shard_map/all_to_all | solution.py:300
  46.3 2.7 %collective-permute-start.2 = (f32[1,128]{1,0:T(1,128)S(1)}, f32[1,128]{1,0:T(1,128)S(1)}, u32[]{:S(2)}, u32[]{:S(2)}) collective-permute-start(f32[1,128]{1,0:T(1,128)S(1)} %get-tuple-element.13), channel_id=1, source_target_pairs={{0,1},{1,0},{2,3},{3,2},{4,5},{5,4},{6,7},{7,6},{8,9},{9,8},{10,11... | collective-permute-start | bytes 1544 | tf_op jit(solution)/shard_map/ppermute | solution.py:303
  61.0 11.9 %all-to-all-start.2 = ((bf16[8,96,256]{2,1,0:T(8,128)(2,1)}), bf16[8,96,256]{2,1,0:T(8,128)(2,1)S(1)}, u32[]{:S(2)}, u32[]{:S(2)}) async-start(bf16[8,96,256]{2,1,0:T(8,128)(2,1)} %bitcast.16), calls=%async_computation.2 | async-start | bytes 786432 | tf_op jit(solution)/shard_map/all_to_all | solution.py:322
  64.7 3.9 %collective-permute-start.3 = (f32[1,128]{1,0:T(1,128)S(1)}, f32[1,128]{1,0:T(1,128)S(1)}, u32[]{:S(2)}, u32[]{:S(2)}) collective-permute-start(f32[1,128]{1,0:T(1,128)S(1)} %get-tuple-element.17), channel_id=1, source_target_pairs={{0,2},{1,3},{2,0},{3,1},{4,6},{5,7},{6,4},{7,5},{8,10},{9,11},{10,... | collective-permute-start | bytes 1544 | tf_op jit(solution)/shard_map/ppermute | solution.py:303
  74.3 16.0 %all-to-all-start.3 = ((bf16[64,4,384]{2,1,0:T(4,128)(2,1)}), bf16[64,4,384]{2,1,0:T(4,128)(2,1)S(1)}, u32[]{:S(2)}, u32[]{:S(2)}) async-start(bf16[64,4,384]{2,1,0:T(4,128)(2,1)} %get-tuple-element.18), calls=%async_computation.3 | async-start | bytes 393216 | tf_op jit(solution)/shard_map/all_to_all | solution.py:333

commit v3 on v2

--- a/solution.py
+++ b/solution.py
@@ -56,7 +56,11 @@
                 cells[slot, row:row + CASES, t * LANES:(t + 1) * LANES] = value
 
 
-def residual_kernel(table, blocks, before, after, rows, out,
+def lane_kernel(out):
+    out[...] = iota((ROWS, LANES), 1)
+
+
+def residual_kernel(table, blocks, chip, far, own, loads, lanes, out,
                     wide, cells, load_cells, message, sems):
     count = NNZ * 288
     copies = [pltpu.make_async_copy(blocks.at[pl.ds(g * count, count)], wide.at[pl.ds(g * count, count)],
@@ -65,10 +69,10 @@
         copy.start()
 
     for i in range(P_SIZE):
-        put_cells(before[i], cells, i)
-        put_cells(rows[i], cells, P_SIZE + i)
-        put_cells(after[i], cells, 2 * P_SIZE + i)
-        put_cells(rows[P_SIZE + i], load_cells, i)
+        put_cells(chip[i], cells, i)
+        put_cells(own[i], cells, P_SIZE + i)
+        put_cells(far[i], cells, 2 * P_SIZE + i)
+        put_cells(loads[i], load_cells, i)
 
     unit_row, unit_col = iota((PAIRS, 384), 0), iota((PAIRS, 384), 1)
     pair = (unit_row % 32) * 3 + unit_row // 32
@@ -95,7 +99,7 @@
             one = total[:, par * 32:par * 32 + 16] + total[:, par * 32 + 16:par * 32 + 32]
             residuals[par].append(one)
 
-    lane = iota((ROWS, LANES), 1)
+    lane = lanes[...]
     info = jnp.zeros((ROWS, LANES), jnp.int32)
     for k in range(LEAF):
         for m in range(UPD):
@@ -276,24 +280,29 @@
     hbm = pl.BlockSpec(memory_space=pltpu.HBM)
     dma = pltpu.SemaphoreType.DMA
     device = lax.axis_index("dom")
-    before = lax.ppermute(solution, "dom", [(i, i + 1) for i in range(DOM - 1)])
-    after = lax.ppermute(solution, "dom", [(i + 1, i) for i in range(DOM - 1)])
+    far = lax.ppermute(solution, "dom", [(i, i + 1 if i % 2 else i - 1) for i in range(1, DOM - 1)])
+    chip = lax.ppermute(solution, "dom", [(i, i ^ 1) for i in range(DOM)])
+    local = columns.T - (device * P_SIZE - P_SIZE)
+    turn = jnp.where(local < P_SIZE, 2 * P_SIZE, jnp.where(local < 2 * P_SIZE, 0, -2 * P_SIZE))
+    local = local + jnp.where(device % 2 == 0, turn, 0)
     table = jnp.concatenate([
-        jnp.pad(columns.T - (device * P_SIZE - P_SIZE), ((0, 0), (0, LANES - P_SIZE))),
+        jnp.pad(local, ((0, 0), (0, LANES - P_SIZE))),
         jnp.pad(row_source.reshape(1, P_SIZE), ((0, 3), (0, LANES - P_SIZE))),
         jnp.pad(targets, ((0, 0), (0, LANES - UPD)))], axis=0)
     natural = blocks.reshape(P_SIZE, NNZ, 288, LANES).transpose(0, 2, 1, 3).reshape(P_SIZE * 1152, LANES)
     natural_inverses = inverses.reshape(LEAF, 288, LANES).transpose(1, 0, 2).reshape(PAIRS, 3, LEAF, LANES)
     natural_tiles = tiles.reshape(LEAF, UPD, 288, LANES).transpose(0, 2, 1, 3)
     natural_tiles = natural_tiles.reshape(LEAF * PAIRS, 3, UPD, LANES)
+    (lanes,) = call(
+        lane_kernel, "lanes", [((ROWS, LANES), jnp.int32)], [], [], 16,
+        pl.CostEstimate(flops=3 * 10**10, bytes_accessed=10**6, transcendentals=0))()
     (message,) = call(
         residual_kernel, "residual", [((DOM * ROWS, LANES), BF16)],
-        [smem, hbm] + [vmem] * 3,
+        [smem, hbm] + [vmem] * 5,
         [pltpu.VMEM((P_SIZE * 1152, LANES), F32),
          pltpu.VMEM((3 * P_SIZE, 64, 384), BF16), pltpu.VMEM((P_SIZE, 64, 384), BF16),
          pltpu.VMEM((DOM * ROWS, LANES), F32), dma((P_SIZE,))], 50,
-    )(table, natural, before, after,
-      jnp.concatenate([solution, loads], axis=0))
+    )(table, natural, chip, far, solution, loads, lanes)
 
     def exchange(x):
         x = x.reshape(DOM, ROWS, LANES)

time: 93.3 us -> 91.2 us (0.977)
  other arithmetic: 2.44 us -> 0.02 us
  waiting for transfers between devices: 27.6 us -> 29.4 us
  starting transfers between devices: 24.9 us -> 23.3 us
    concatenate x2 -> x1, other arithmetic: 1.74 us -> 0.01 us  [on_device(): jnp.concatenate([jnp.pad(local, ((0, 0), (0, LANES - P_SIZE))), jnp.pad(r...]
    ppermute x2, waiting for transfers between devices: 2.82 us -> 4.53 us  [the longest x1 4.53 us: on_device(): lax.ppermute(solution, 'dom', [(i, i + 1 if i % 2 else i - 1) for i in ra...]
    ppermute x2, starting transfers between devices: 6.86 us -> 5.24 us  [the longest x1 3.33 us: on_device(): chip = lax.ppermute(solution, 'dom', [(i, i ^ 1) for i in range(DOM)])]
  transfers between devices with their start and end apart: 7 -> 7, of which waited for: 6 -> 6; matrix products, arithmetic and copies ran while one was open for 3% -> 0% of each run, Pallas kernels for 0% -> 0%
where the time goes in v3:
time: 91.2 us; the launch traced here: 90.8 us
  waiting for transfers between devices  29.4 us (32%)
  starting transfers between devices  23.3 us (26%)
  blocking collectives  21.1 us (23%)
  Pallas kernels  14.2 us (16%)
  between operations  1.99 us (2%)
    all_to_all x1, blocking collectives, exchange(): return lax.all_to_all(x, 'dom', 0, 0, tiled=True).reshape(DOM * ROWS, LANES)  21.1 us
    all_to_all x1, waiting for transfers between devices, on_device(): sums = lax.all_to_all(sums, 'dom', 0, 0, tiled=True)  10.9 us
    all_to_all x1, waiting for transfers between devices, exchange(): return lax.all_to_all(x, 'dom', 0, 0, tiled=True).reshape(DOM * ROWS, LANES)  7.65 us
    pallas_call x1, Pallas kernels, on_device(): call(residual_kernel, 'residual', [((DOM * ROWS, LANES), BF16)], [smem, h...  5.52 us
    all_to_all x1, starting transfers between devices, on_device(): sums = lax.all_to_all(sums, 'dom', 0, 0, tiled=True)  5.08 us
    all_to_all x1, starting transfers between devices, exchange(): return lax.all_to_all(x, 'dom', 0, 0, tiled=True).reshape(DOM * ROWS, LANES)  4.88 us
    ppermute x1, waiting for transfers between devices, on_device(): lax.ppermute(solution, 'dom', [(i, i + 1 if i % 2 else i - 1) for i in ra...  4.53 us
    ppermute x2, starting transfers between devices, across(): return x + lax.ppermute(x, 'rhs', [(i, i ^ step) for i in range(4)])  4.3 us
  transfers between devices with their start and end apart: 7, of which 6 were waited for; matrix products, arithmetic and copies ran while one was open for 0% of the time, Pallas kernels for 0%

profile of v3, /device:TPU:1, one launch (start us, length us, event | category | flops | bytes accessed | tf_op | source)
XLA Modules:
  0.0 90.8 jit_solution(7839274970608247888)
XLA Ops:
  0.6 3.3 %collective-permute-start = (f32[12,16,192]{2,1,0:T(8,128)}, f32[12,16,192]{2,1,0:T(8,128)S(1)}, u32[]{:S(2)}, u32[]{:S(2)}) collective-permute-start(f32[12,16,192]{2,1,0:T(8,128)} %own.1), channel_id=1, source_target_pairs={{0,4},{4,0},{8,12},{12,8},{16,20},{20,16},{24,28},{28,24},{32,36},... | collective-permute-start | bytes 442376 | tf_op jit(solution)/shard_map/ppermute | solution.py:284
  4.0 1.9 %collective-permute-start.1 = (f32[12,16,192]{2,1,0:T(8,128)}, f32[12,16,192]{2,1,0:T(8,128)S(1)}, u32[]{:S(2)}, u32[]{:S(2)}) collective-permute-start(f32[12,16,192]{2,1,0:T(8,128)} %own.1), channel_id=1, source_target_pairs={{4,8},{8,4},{12,16},{16,12},{20,24},{24,20},{28,32},{32,28},{36,40... | collective-permute-start | bytes 442376 | tf_op jit(solution)/shard_map/ppermute | solution.py:283
  5.9 0.0 copy-start.4
  5.9 0.0 copy-start.3
  5.9 0.0 copy-start.5
  5.9 0.0 copy-start.1
  5.9 0.0 copy-start.2
  6.0 0.6 copy-done.4
  6.6 0.0 copy-done.3
  6.6 0.0 copy-done.5
  6.6 0.0 collective-permute-done.chip
  6.6 4.5 %collective-permute-done.1.far = f32[12,16,192]{2,1,0:T(8,128)S(1)} collective-permute-done((f32[12,16,192]{2,1,0:T(8,128)}, f32[12,16,192]{2,1,0:T(8,128)S(1)}, u32[]{:S(2)}, u32[]{:S(2)}) %collective-permute-start.1) | collective-permute-done | bytes 147488 | tf_op jit(solution)/shard_map/ppermute | solution.py:283
  11.1 0.0 copy-done.1
  11.1 0.0 copy-done.2
  11.2 5.5 %residual.1 = bf16[512,128]{1,0:T(8,128)(2,1)S(1)} custom-call(s32[16,128]{1,0:T(8,128)S(1)} %pad_add_fusion.table, f32[13824,128]{1,0:T(8,128)} %bitcast.43, f32[12,16,192]{2,1,0:T(8,128)S(1)} %collective-permute-done.chip, f32[12,16,192]{2,1,0:T(8,128)S(1)} %collective-permute-done.1.far, f32[12,16,192]{2,1,0:T(8,128)S(1)} %copy-done.1, ...), custom_call_target="tpu_custom_call" | custom-call | tf_op jit(solution)/shard_map/residual/pallas_call | solution.py:299
  16.7 21.1 %all_to_all.20 = bf16[64,8,128]{2,1,0:T(8,128)(2,1)S(1)} all-to-all(bf16[64,8,128]{2,1,0:T(8,128)(2,1)S(1)} %bitcast.38), channel_id=1, replica_groups=mesh['dom'=64,'rhs'=4] {'dom'}, dimensions={0} | all-to-all | bytes 262144 | tf_op jit(solution)/shard_map/all_to_all | solution.py:309
  37.8 0.0 copy-start
  37.8 1.5 %permute.1 = (bf16[512,128]{1,0:T(8,128)(2,1)}, f32[64,128]{1,0:T(8,128)S(1)}, f32[1,128]{1,0:T(1,128)S(1)}) custom-call(bf16[512,128]{1,0:T(8,128)(2,1)S(1)} %bitcast.40), custom_call_target="tpu_custom_call" | custom-call | flops 4000000000 | bytes 1000000 | tf_op jit(solution)/shard_map/permute/pallas_call | solution.py:314
  39.4 4.9 %all-to-all-start.1 = ((bf16[64,8,128]{2,1,0:T(8,128)(2,1)}), bf16[64,8,128]{2,1,0:T(8,128)(2,1)S(1)}, u32[]{:S(2)}, u32[]{:S(2)}) async-start(bf16[64,8,128]{2,1,0:T(8,128)(2,1)} %bitcast.7), calls=%async_computation.1 | async-start | bytes 262144 | tf_op jit(solution)/shard_map/all_to_all | solution.py:309
  44.3 1.4 %collective-permute-start.2 = (f32[1,128]{1,0:T(1,128)S(1)}, f32[1,128]{1,0:T(1,128)S(1)}, u32[]{:S(2)}, u32[]{:S(2)}) collective-permute-start(f32[1,128]{1,0:T(1,128)S(1)} %get-tuple-element.13), channel_id=1, source_target_pairs={{0,1},{1,0},{2,3},{3,2},{4,5},{5,4},{6,7},{7,6},{8,9},{9,8},{10,11... | collective-permute-start | bytes 1544 | tf_op jit(solution)/shard_map/ppermute | solution.py:312
  45.6 1.3 %collective-permute-done.2 = f32[1,128]{1,0:T(1,128)S(1)} collective-permute-done((f32[1,128]{1,0:T(1,128)S(1)}, f32[1,128]{1,0:T(1,128)S(1)}, u32[]{:S(2)}, u32[]{:S(2)}) %collective-permute-start.2) | collective-permute-done | bytes 544 | tf_op jit(solution)/shard_map/ppermute | solution.py:312
  47.0 7.6 %all-to-all-done.1 = bf16[64,8,128]{2,1,0:T(8,128)(2,1)S(1)} async-done(((bf16[64,8,128]{2,1,0:T(8,128)(2,1)}), bf16[64,8,128]{2,1,0:T(8,128)(2,1)S(1)}, u32[]{:S(2)}, u32[]{:S(2)}) %all-to-all-start.1) | async-done | bytes 131104 | tf_op jit(solution)/shard_map/all_to_all | solution.py:309
  54.6 0.0 copy-done
  54.6 4.3 %update.1 = (bf16[128,192]{1,0:T(8,128)(2,1)}, f32[64,192]{1,0:T(8,128)S(1)}, bf16[768,256]{1,0:T(8,128)(2,1)}, f32[1,128]{1,0:T(1,128)S(1)}) custom-call(bf16[512,128]{1,0:T(8,128)(2,1)S(1)} %bitcast.39, bf16[96,3,8,128]{3,2,1,0:T(8,128)(2,1)S(1)} %bitcast.37, bf16[768,3,8,128]{3,2,1,0:T(8,128)(2,1)} %bitcast.44, f32[1,128]{1,0:T(1,128)S(1)} %add.30.squares), custom_call_target="tpu_custom_call" | custom-call | tf_op jit(solution)/shard_map/update/pallas_call | solution.py:321
  58.9 3.8 %all-to-all-start.2 = ((bf16[8,96,256]{2,1,0:T(8,128)(2,1)}), bf16[8,96,256]{2,1,0:T(8,128)(2,1)S(1)}, u32[]{:S(2)}, u32[]{:S(2)}) async-start(bf16[8,96,256]{2,1,0:T(8,128)(2,1)} %bitcast.16), calls=%async_computation.2 | async-start | bytes 786432 | tf_op jit(solution)/shard_map/all_to_all | solution.py:331
  62.7 2.9 %collective-permute-start.3 = (f32[1,128]{1,0:T(1,128)S(1)}, f32[1,128]{1,0:T(1,128)S(1)}, u32[]{:S(2)}, u32[]{:S(2)}) collective-permute-start(f32[1,128]{1,0:T(1,128)S(1)} %get-tuple-element.17), channel_id=1, source_target_pairs={{0,2},{1,3},{2,0},{3,1},{4,6},{5,7},{6,4},{7,5},{8,10},{9,11},{10,... | collective-permute-start | bytes 1544 | tf_op jit(solution)/shard_map/ppermute | solution.py:312
  65.6 0.1 reshape.82
  65.7 0.1 reshape.83.targets
  65.8 0.8 collective-permute-done.3
  66.6 4.2 %all-to-all-done.2.received = bf16[8,96,256]{2,1,0:T(8,128)(2,1)S(1)} async-done(((bf16[8,96,256]{2,1,0:T(8,128)(2,1)}), bf16[8,96,256]{2,1,0:T(8,128)(2,1)S(1)}, u32[]{:S(2)}, u32[]{:S(2)}) %all-to-all-start.2) | async-done | bytes 393248 | tf_op jit(solution)/shard_map/all_to_all | solution.py:331
  70.8 1.5 %sum.1 = (bf16[64,4,384]{2,1,0:T(4,128)(2,1)}, f32[1,128]{1,0:T(1,128)S(1)}) custom-call(bf16[8,96,256]{2,1,0:T(8,128)(2,1)S(1)} %all-to-all-done.2.received, f32[1,512]{1,0:T(1,128)S(1)} %reshape.83.targets, f32[1,128]{1,0:T(1,128)S(1)} %add.33.squares), custom_call_target="tpu_custom_call" | custom-call | tf_op jit(solution)/shard_map/sum/pallas_call | solution.py:337
  72.3 5.1 %all-to-all-start.3 = ((bf16[64,4,384]{2,1,0:T(4,128)(2,1)}), bf16[64,4,384]{2,1,0:T(4,128)(2,1)S(1)}, u32[]{:S(2)}, u32[]{:S(2)}) async-start(bf16[64,4,384]{2,1,0:T(4,128)(2,1)} %get-tuple-element.18), calls=%async_computation.3 | async-start | bytes 393216 | tf_op jit(solution)/shard_map/all_to_all | solution.py:342
  77.4 10.9 %all-to-all-done.3 = bf16[64,4,384]{2,1,0:T(4,128)(2,1)S(1)} async-done(((bf16[64,4,384]{2,1,0:T(4,128)(2,1)}), bf16[64,4,384]{2,1,0:T(4,128)(2,1)S(1)}, u32[]{:S(2)}, u32[]{:S(2)}) %all-to-all-start.3) | async-done | bytes 196640 | tf_op jit(solution)/shard_map/all_to_all | solution.py:342
  88.3 0.1 reshape.84.received
  88.4 1.3 %final.1 = f32[64,192]{1,0:T(8,128)} custom-call(bf16[256,384]{1,0:T(8,128)(2,1)S(1)} %reshape.84.received, f32[64,192]{1,0:T(8,128)S(1)} %get-tuple-element.19.ancestors), custom_call_target="tpu_custom_call" | custom-call | tf_op jit(solution)/shard_map/final/pallas_call | solution.py:343
  (7 shorter events, 0.0 us)
Async XLA Ops:
  0.6 6.0 %collective-permute-start = (f32[12,16,192]{2,1,0:T(8,128)}, f32[12,16,192]{2,1,0:T(8,128)S(1)}, u32[]{:S(2)}, u32[]{:S(2)}) collective-permute-start(f32[12,16,192]{2,1,0:T(8,128)} %own.1), channel_id=1, source_target_pairs={{0,4},{4,0},{8,12},{12,8},{16,20},{20,16},{24,28},{28,24},{32,36},... | collective-permute-start | bytes 442376 | tf_op jit(solution)/shard_map/ppermute | solution.py:284
  4.0 7.2 %collective-permute-start.1 = (f32[12,16,192]{2,1,0:T(8,128)}, f32[12,16,192]{2,1,0:T(8,128)S(1)}, u32[]{:S(2)}, u32[]{:S(2)}) collective-permute-start(f32[12,16,192]{2,1,0:T(8,128)} %own.1), channel_id=1, source_target_pairs={{4,8},{8,4},{12,16},{16,12},{20,24},{24,20},{28,32},{32,28},{36,40... | collective-permute-start | bytes 442376 | tf_op jit(solution)/shard_map/ppermute | solution.py:283
  5.9 0.7 copy-start.4
  5.9 0.7 copy-start.3
  5.9 0.7 copy-start.5
  5.9 5.2 %copy-start.1 = (f32[12,16,192]{2,1,0:T(8,128)S(1)}, f32[12,16,192]{2,1,0:T(8,128)}, u32[]{:S(2)}) copy-start(f32[12,16,192]{2,1,0:T(8,128)} %own.1) | copy-start | bytes 442372
  5.9 5.2 %copy-start.2 = (f32[12,16,192]{2,1,0:T(8,128)S(1)}, f32[12,16,192]{2,1,0:T(8,128)}, u32[]{:S(2)}) copy-start(f32[12,16,192]{2,1,0:T(8,128)} %loads.1) | copy-start | bytes 442372
  37.8 16.8 %copy-start = (bf16[8,36864]{1,0:T(8,128)(2,1)S(1)}, bf16[8,36864]{1,0:T(8,128)(2,1)}, u32[]{:S(2)}) copy-start(bf16[8,36864]{1,0:T(8,128)(2,1)} %param.13) | copy-start | bytes 1769476
  39.4 15.2 %all-to-all-start.1 = ((bf16[64,8,128]{2,1,0:T(8,128)(2,1)}), bf16[64,8,128]{2,1,0:T(8,128)(2,1)S(1)}, u32[]{:S(2)}, u32[]{:S(2)}) async-start(bf16[64,8,128]{2,1,0:T(8,128)(2,1)} %bitcast.7), calls=%async_computation.1 | async-start | bytes 262144 | tf_op jit(solution)/shard_map/all_to_all | solution.py:309
  44.3 2.7 %collective-permute-start.2 = (f32[1,128]{1,0:T(1,128)S(1)}, f32[1,128]{1,0:T(1,128)S(1)}, u32[]{:S(2)}, u32[]{:S(2)}) collective-permute-start(f32[1,128]{1,0:T(1,128)S(1)} %get-tuple-element.13), channel_id=1, source_target_pairs={{0,1},{1,0},{2,3},{3,2},{4,5},{5,4},{6,7},{7,6},{8,9},{9,8},{10,11... | collective-permute-start | bytes 1544 | tf_op jit(solution)/shard_map/ppermute | solution.py:312
  58.9 11.9 %all-to-all-start.2 = ((bf16[8,96,256]{2,1,0:T(8,128)(2,1)}), bf16[8,96,256]{2,1,0:T(8,128)(2,1)S(1)}, u32[]{:S(2)}, u32[]{:S(2)}) async-start(bf16[8,96,256]{2,1,0:T(8,128)(2,1)} %bitcast.16), calls=%async_computation.2 | async-start | bytes 786432 | tf_op jit(solution)/shard_map/all_to_all | solution.py:331
  62.7 3.9 %collective-permute-start.3 = (f32[1,128]{1,0:T(1,128)S(1)}, f32[1,128]{1,0:T(1,128)S(1)}, u32[]{:S(2)}, u32[]{:S(2)}) collective-permute-start(f32[1,128]{1,0:T(1,128)S(1)} %get-tuple-element.17), channel_id=1, source_target_pairs={{0,2},{1,3},{2,0},{3,1},{4,6},{5,7},{6,4},{7,5},{8,10},{9,11},{10,... | collective-permute-start | bytes 1544 | tf_op jit(solution)/shard_map/ppermute | solution.py:312
  72.3 16.0 %all-to-all-start.3 = ((bf16[64,4,384]{2,1,0:T(4,128)(2,1)}), bf16[64,4,384]{2,1,0:T(4,128)(2,1)S(1)}, u32[]{:S(2)}, u32[]{:S(2)}) async-start(bf16[64,4,384]{2,1,0:T(4,128)(2,1)} %get-tuple-element.18), calls=%async_computation.3 | async-start | bytes 393216 | tf_op jit(solution)/shard_map/all_to_all | solution.py:342

commit v4 on v3

--- a/solution.py
+++ b/solution.py
@@ -60,55 +60,52 @@
     out[...] = iota((ROWS, LANES), 1)
 
 
-def residual_kernel(table, blocks, chip, far, own, loads, lanes, out,
-                    wide, cells, load_cells, message, sems):
+def split_kernel(table, blocks, chip, own, loads, lanes, high, low, cells, start, info, load_cells):
     count = NNZ * 288
-    copies = [pltpu.make_async_copy(blocks.at[pl.ds(g * count, count)], wide.at[pl.ds(g * count, count)],
-                                    sems.at[g]) for g in range(P_SIZE)]
-    for copy in copies:
-        copy.start()
-
     for i in range(P_SIZE):
+        put_cells(loads[i], load_cells, i)
         put_cells(chip[i], cells, i)
         put_cells(own[i], cells, P_SIZE + i)
-        put_cells(far[i], cells, 2 * P_SIZE + i)
-        put_cells(loads[i], load_cells, i)
-
     unit_row, unit_col = iota((PAIRS, 384), 0), iota((PAIRS, 384), 1)
     pair = (unit_row % 32) * 3 + unit_row // 32
     unit = one_hot((unit_col == 2 * pair) | (unit_col == 2 * pair + B + 1))
-    residuals = ([], [])
     for g in range(P_SIZE):
-        if g % 3 == 0:
-            for copy in copies[g:g + 3]:
-                copy.wait()
-        high, low = [], []
+        start[g] = lax.dot_general(unit, load_cells[g], NT, preferred_element_type=F32)
         for j in range(NNZ):
             for t in range(3):
                 tall = jnp.concatenate(
-                    [wide[pl.ds(g * count + 12 * k + j + 4 * t, 32, stride=36), :] for k in range(3)], axis=0)
-                first, second = halves(tall)
-                high.append(first)
-                low.append(second)
+                    [blocks[pl.ds(g * count + 12 * k + j + 4 * t, 32, stride=36), :] for k in range(3)], axis=0)
+                at = (g, slice(None), slice(j * 384 + t * LANES, j * 384 + (t + 1) * LANES))
+                high[at], low[at] = halves(tall)
+
+    lane = lanes[...]
+    notes = jnp.zeros((ROWS, LANES), jnp.int32)
+    for k in range(LEAF):
+        for m in range(UPD):
+            notes = jnp.where(lane == k * UPD + m, table[8 + k, m], notes)
+    for i in range(P_SIZE):
+        source = table[4, i]
+        notes = jnp.where(lane == 64 + i, source // P_SIZE, notes)
+        notes = jnp.where(lane == 76 + i, source % P_SIZE, notes)
+    info[...] = notes.astype(F32)[:1]
+
+
+def residual_kernel(table, high, low, near, start, info, far, out, cells, message):
+    for i in range(P_SIZE):
+        cells[i] = near[i]
+        cells[P_SIZE + i] = near[P_SIZE + i]
+        put_cells(far[i], cells, 2 * P_SIZE + i)
+
+    residuals = ([], [])
+    for g in range(P_SIZE):
         right = jnp.concatenate([cells[table[j, g]] for j in range(NNZ)], axis=1)
-        total = lax.dot_general(unit, load_cells[g], NT, preferred_element_type=F32)
+        total = start[g]
         for side in (high, low):
-            total = total - lax.dot_general(
-                jnp.concatenate(side, axis=1), right, NT, preferred_element_type=F32)
+            total = total - lax.dot_general(side[g], right, NT, preferred_element_type=F32)
         for par in range(2):
             one = total[:, par * 32:par * 32 + 16] + total[:, par * 32 + 16:par * 32 + 32]
             residuals[par].append(one)
 
-    lane = lanes[...]
-    info = jnp.zeros((ROWS, LANES), jnp.int32)
-    for k in range(LEAF):
-        for m in range(UPD):
-            info = jnp.where(lane == k * UPD + m, table[8 + k, m], info)
-    for i in range(P_SIZE):
-        source = table[4, i]
-        info = jnp.where(lane == 64 + i, source // P_SIZE, info)
-        info = jnp.where(lane == 76 + i, source % P_SIZE, info)
-    info = info.astype(F32)[:1]
     squares = jnp.zeros((PAIRS, LANES), F32)
     for par in range(2):
         ones = residuals[par] + [jnp.zeros((PAIRS, CASES), F32)] * 4
@@ -122,7 +119,7 @@
     second = (whole - first).astype(BF16).astype(F32)
     third = whole - first - second
     lane = iota((DOM, LANES), 1)
-    message[pl.ds(6, DOM, stride=ROWS), :] = jnp.broadcast_to(info, (DOM, LANES))
+    message[pl.ds(6, DOM, stride=ROWS), :] = jnp.broadcast_to(info[...], (DOM, LANES))
     message[pl.ds(7, DOM, stride=ROWS), :] = jnp.where(
         lane == 0, first, jnp.where(lane == 1, second, jnp.where(lane == 2, third, 0.0)))
     out[...] = message[...].astype(BF16)
@@ -242,22 +239,21 @@
     source, block = place // ANC, place % ANC
     group = source // (N_Z * N_CORE) * N_CORE + source % N_CORE
     row = iota((32, 256), 0)
-    pick = one_hot((row // GROUP == block) & (row % GROUP == group))
+    pick = one_hot((row % ANC == block) & (row // ANC == group))
     summed = dot(pick, received[...])
-    own = iota((CASES, 384), 1) % CASES == iota((CASES, 384), 0)
-    to_row, to_col = iota((384, B), 0), iota((384, B), 1)
-    total = jnp.zeros((3 * ANC * CASES, B), F32)
+    count = ANC * CASES
+    own = iota((count, 384), 1) % CASES == iota((count, 384), 0) % CASES
+    sides = ([], [])
     for q in range(GROUP):
         left = jnp.concatenate(
-            [jnp.where(own, jnp.broadcast_to(summed[t * GROUP + q:t * GROUP + q + 1], (CASES, 384)), 0.0)
-             for t in range(ANC)], axis=0)
-        first = left.astype(BF16)
-        second, third = halves(left - first.astype(F32))
-        total = total + dot(
-            jnp.concatenate([first, second, third], axis=0),
-            one_hot(to_col == q * 24 + to_row // 16))
-    count = ANC * CASES
-    out[...] = ancestors[...] - (total[:count] + total[count:2 * count] + total[2 * count:])
+            [jnp.broadcast_to(summed[q * ANC + t:q * ANC + t + 1], (CASES, 384)) for t in range(ANC)], axis=0)
+        for side, part in zip(sides, halves(jnp.where(own, left, 0.0))):
+            side.append(part)
+    column = one_hot(iota((384, 24), 1) == iota((384, 24), 0) // CASES)
+    both = dot(jnp.concatenate(sides[0] + sides[1], axis=0), column)
+    both = both[:GROUP * count] + both[GROUP * count:]
+    out[...] = ancestors[...] - jnp.concatenate(
+        [both[q * count:(q + 1) * count] for q in range(GROUP)], axis=1)
 
 
 def call(kernel, name, shapes, in_specs, scratch, megabytes=16, cost=None):
@@ -296,13 +292,18 @@
     (lanes,) = call(
         lane_kernel, "lanes", [((ROWS, LANES), jnp.int32)], [], [], 16,
         pl.CostEstimate(flops=3 * 10**10, bytes_accessed=10**6, transcendentals=0))()
+    high, low, cells, start, info = call(
+        split_kernel, "split",
+        [((P_SIZE, PAIRS, 1536), BF16), ((P_SIZE, PAIRS, 1536), BF16), ((2 * P_SIZE, 64, 384), BF16),
+         ((P_SIZE, PAIRS, 64), F32), ((1, LANES), F32)],
+        [smem] + [vmem] * 5, [pltpu.VMEM((P_SIZE, 64, 384), BF16)], 16,
+        pl.CostEstimate(flops=10**9, bytes_accessed=14 * 10**6, transcendentals=0),
+    )(table, natural, chip, solution, loads, lanes)
     (message,) = call(
         residual_kernel, "residual", [((DOM * ROWS, LANES), BF16)],
-        [smem, hbm] + [vmem] * 5,
-        [pltpu.VMEM((P_SIZE * 1152, LANES), F32),
-         pltpu.VMEM((3 * P_SIZE, 64, 384), BF16), pltpu.VMEM((P_SIZE, 64, 384), BF16),
-         pltpu.VMEM((DOM * ROWS, LANES), F32), dma((P_SIZE,))], 50,
-    )(table, natural, chip, far, solution, loads, lanes)
+        [smem] + [vmem] * 6,
+        [pltpu.VMEM((3 * P_SIZE, 64, 384), BF16), pltpu.VMEM((DOM * ROWS, LANES), F32)], 16,
+    )(table, high, low, cells, start, info, far)
 
     def exchange(x):
         x = x.reshape(DOM, ROWS, LANES)

time: 91.2 us -> 89.5 us (0.981)
  waiting for transfers between devices: 29.4 us -> 24.8 us
  local copies, waits for them, and re-layouts: 0.86 us -> 4.23 us
    ppermute x1, waiting for transfers between devices: 4.53 us -> 0.01 us  [on_device(): lax.ppermute(solution, 'dom', [(i, i + 1 if i % 2 else i - 1) for i in ra...]
    unnamed x12 -> x14, local copies, waits for them, and re-layouts: 0.64 us -> 4.01 us
    pallas_call x1 -> x2, Pallas kernels: 5.52 us -> 5.56 us  [the longest x1 3.17 us: on_device(): call(residual_kernel, 'residual', [((DOM * ROWS, LANES), BF16)], [smem] +...]
  transfers between devices with their start and end apart: 7 -> 7, of which waited for: 6 -> 5; matrix products, arithmetic and copies ran while one was open for 0% -> 0% of each run, Pallas kernels for 0% -> 3%
where the time goes in v4:
time: 89.5 us; the launch traced here: 89.1 us
  waiting for transfers between devices  24.8 us (28%)
  starting transfers between devices  23.2 us (26%)
  blocking collectives  20.7 us (23%)
  Pallas kernels  14.1 us (16%)
  local copies, waits for them, and re-layouts  4.23 us (5%)
  between operations  2 us (2%)
    all_to_all x1, blocking collectives, exchange(): return lax.all_to_all(x, 'dom', 0, 0, tiled=True).reshape(DOM * ROWS, LANES)  20.7 us
    all_to_all x1, waiting for transfers between devices, on_device(): sums = lax.all_to_all(sums, 'dom', 0, 0, tiled=True)  10.9 us
    all_to_all x1, waiting for transfers between devices, exchange(): return lax.all_to_all(x, 'dom', 0, 0, tiled=True).reshape(DOM * ROWS, LANES)  7.65 us
    all_to_all x1, starting transfers between devices, on_device(): sums = lax.all_to_all(sums, 'dom', 0, 0, tiled=True)  5.08 us
    all_to_all x1, starting transfers between devices, exchange(): return lax.all_to_all(x, 'dom', 0, 0, tiled=True).reshape(DOM * ROWS, LANES)  4.88 us
    ppermute x2, starting transfers between devices, across(): return x + lax.ppermute(x, 'rhs', [(i, i ^ step) for i in range(4)])  4.29 us
    pallas_call x1, Pallas kernels, on_device(): call(update_kernel, 'update', [((LEAF * CASES, B), BF16), ((ANC * CASES,...  4.28 us
    all_to_all x1, waiting for transfers between devices, on_device(): lax.all_to_all(message.reshape(GROUP, 96, 256), 'dom', 0, 0, axis_index_g...  4.2 us
  transfers between devices with their start and end apart: 7, of which 5 were waited for; matrix products, arithmetic and copies ran while one was open for 0% of the time, Pallas kernels for 3%

profile of v4, /device:TPU:1, one launch (start us, length us, event | category | flops | bytes accessed | tf_op | source)
XLA Modules:
  0.0 89.1 jit_solution(247643600662118225)
XLA Ops:
  0.6 3.3 %collective-permute-start = (f32[12,16,192]{2,1,0:T(8,128)}, f32[12,16,192]{2,1,0:T(8,128)S(1)}, u32[]{:S(2)}, u32[]{:S(2)}) collective-permute-start(f32[12,16,192]{2,1,0:T(8,128)} %own.1), channel_id=1, source_target_pairs={{0,4},{4,0},{8,12},{12,8},{16,20},{20,16},{24,28},{28,24},{32,36},... | collective-permute-start | bytes 442376 | tf_op jit(solution)/shard_map/ppermute | solution.py:280
  4.0 1.9 %collective-permute-start.1 = (f32[12,16,192]{2,1,0:T(8,128)}, f32[12,16,192]{2,1,0:T(8,128)S(1)}, u32[]{:S(2)}, u32[]{:S(2)}) collective-permute-start(f32[12,16,192]{2,1,0:T(8,128)} %own.1), channel_id=1, source_target_pairs={{4,8},{8,4},{12,16},{16,12},{20,24},{24,20},{28,32},{32,28},{36,40... | collective-permute-start | bytes 442376 | tf_op jit(solution)/shard_map/ppermute | solution.py:279
  5.9 0.0 copy-start.5
  5.9 0.0 copy-start.4
  5.9 0.0 copy-start.6
  5.9 0.0 copy-start.2
  5.9 0.0 copy-start.3
  6.0 0.6 copy-done.5
  6.6 0.0 copy-done.4
  6.6 0.0 copy-done.6
  6.6 0.0 collective-permute-done.chip
  6.6 0.2 copy-done.2
  6.9 0.1 copy-done.3
  7.0 0.0 copy-start
  7.0 3.0 %copy-done = f32[12,4,36864]{2,1,0:T(4,128)S(1)} copy-done((f32[12,4,36864]{2,1,0:T(4,128)S(1)}, f32[12,4,36864]{2,1,0:T(4,128)}, u32[]{:S(2)}) %copy-start) | copy-done | bytes 7077912
  10.0 2.4 %split.1 = (bf16[12,96,1536]{2,1,0:T(8,128)(2,1)S(1)}, bf16[12,96,1536]{2,1,0:T(8,128)(2,1)S(1)}, bf16[24,64,384]{2,1,0:T(8,128)(2,1)S(1)}, f32[12,96,64]{2,1,0:T(8,128)S(1)}, f32[1,128]{1,0:T(1,128)S(1)}) custom-call(s32[16,128]{1,0:T(8,128)S(1)} %pad_add_fusion.table, f32[13824,128]{1,0:T(8,128)S(1)} %bitcast.37, ...), custom_call_target="tpu_custom_call" | custom-call | flops 1000000000 | bytes 14000000 | tf_op jit(solution)/shard_map/split/pallas_call | solution.py:295
  12.4 0.0 collective-permute-done.1.far
  12.4 3.2 %residual.1 = bf16[512,128]{1,0:T(8,128)(2,1)S(1)} custom-call(s32[16,128]{1,0:T(8,128)S(1)} %pad_add_fusion.table, bf16[12,96,1536]{2,1,0:T(8,128)(2,1)S(1)} %get-tuple-element.17.high, bf16[12,96,1536]{2,1,0:T(8,128)(2,1)S(1)} %get-tuple-element.18.low, bf16[24,64,384]{2,1,0:T(8,128)(2,1)S(1)} %get-tuple-element.19.near, ...), custom_call_target="tpu_custom_call" | custom-call | tf_op jit(solution)/shard_map/residual/pallas_call | solution.py:302
  15.6 20.7 %all_to_all.20 = bf16[64,8,128]{2,1,0:T(8,128)(2,1)S(1)} all-to-all(bf16[64,8,128]{2,1,0:T(8,128)(2,1)S(1)} %bitcast.39), channel_id=1, replica_groups=mesh['dom'=64,'rhs'=4] {'dom'}, dimensions={0} | all-to-all | bytes 262144 | tf_op jit(solution)/shard_map/all_to_all | solution.py:310
  36.2 0.0 copy-start.1
  36.2 1.5 %permute.1 = (bf16[512,128]{1,0:T(8,128)(2,1)}, f32[64,128]{1,0:T(8,128)S(1)}, f32[1,128]{1,0:T(1,128)S(1)}) custom-call(bf16[512,128]{1,0:T(8,128)(2,1)S(1)} %bitcast.41), custom_call_target="tpu_custom_call" | custom-call | flops 4000000000 | bytes 1000000 | tf_op jit(solution)/shard_map/permute/pallas_call | solution.py:315
  37.8 4.9 %all-to-all-start.1 = ((bf16[64,8,128]{2,1,0:T(8,128)(2,1)}), bf16[64,8,128]{2,1,0:T(8,128)(2,1)S(1)}, u32[]{:S(2)}, u32[]{:S(2)}) async-start(bf16[64,8,128]{2,1,0:T(8,128)(2,1)} %bitcast.7), calls=%async_computation.1 | async-start | bytes 262144 | tf_op jit(solution)/shard_map/all_to_all | solution.py:310
  42.6 1.4 %collective-permute-start.2 = (f32[1,128]{1,0:T(1,128)S(1)}, f32[1,128]{1,0:T(1,128)S(1)}, u32[]{:S(2)}, u32[]{:S(2)}) collective-permute-start(f32[1,128]{1,0:T(1,128)S(1)} %get-tuple-element.23), channel_id=1, source_target_pairs={{0,1},{1,0},{2,3},{3,2},{4,5},{5,4},{6,7},{7,6},{8,9},{9,8},{10,11... | collective-permute-start | bytes 1544 | tf_op jit(solution)/shard_map/ppermute | solution.py:313
  44.0 1.3 %collective-permute-done.2 = f32[1,128]{1,0:T(1,128)S(1)} collective-permute-done((f32[1,128]{1,0:T(1,128)S(1)}, f32[1,128]{1,0:T(1,128)S(1)}, u32[]{:S(2)}, u32[]{:S(2)}) %collective-permute-start.2) | collective-permute-done | bytes 544 | tf_op jit(solution)/shard_map/ppermute | solution.py:313
  45.4 7.6 %all-to-all-done.1 = bf16[64,8,128]{2,1,0:T(8,128)(2,1)S(1)} async-done(((bf16[64,8,128]{2,1,0:T(8,128)(2,1)}), bf16[64,8,128]{2,1,0:T(8,128)(2,1)S(1)}, u32[]{:S(2)}, u32[]{:S(2)}) %all-to-all-start.1) | async-done | bytes 131104 | tf_op jit(solution)/shard_map/all_to_all | solution.py:310
  53.0 0.0 copy-done.1
  53.0 4.3 %update.1 = (bf16[128,192]{1,0:T(8,128)(2,1)}, f32[64,192]{1,0:T(8,128)S(1)}, bf16[768,256]{1,0:T(8,128)(2,1)}, f32[1,128]{1,0:T(1,128)S(1)}) custom-call(bf16[512,128]{1,0:T(8,128)(2,1)S(1)} %bitcast.40, bf16[96,3,8,128]{3,2,1,0:T(8,128)(2,1)S(1)} %bitcast.38, bf16[768,3,8,128]{3,2,1,0:T(8,128)(2,1)} %bitcast.44, f32[1,128]{1,0:T(1,128)S(1)} %add.30.squares), custom_call_target="tpu_custom_call" | custom-call | tf_op jit(solution)/shard_map/update/pallas_call | solution.py:322
  57.3 3.8 %all-to-all-start.2 = ((bf16[8,96,256]{2,1,0:T(8,128)(2,1)}), bf16[8,96,256]{2,1,0:T(8,128)(2,1)S(1)}, u32[]{:S(2)}, u32[]{:S(2)}) async-start(bf16[8,96,256]{2,1,0:T(8,128)(2,1)} %bitcast.16), calls=%async_computation.2 | async-start | bytes 786432 | tf_op jit(solution)/shard_map/all_to_all | solution.py:332
  61.1 2.9 %collective-permute-start.3 = (f32[1,128]{1,0:T(1,128)S(1)}, f32[1,128]{1,0:T(1,128)S(1)}, u32[]{:S(2)}, u32[]{:S(2)}) collective-permute-start(f32[1,128]{1,0:T(1,128)S(1)} %get-tuple-element.27), channel_id=1, source_target_pairs={{0,2},{1,3},{2,0},{3,1},{4,6},{5,7},{6,4},{7,5},{8,10},{9,11},{10,... | collective-permute-start | bytes 1544 | tf_op jit(solution)/shard_map/ppermute | solution.py:313
  64.0 0.1 reshape.82
  64.1 0.1 reshape.83.targets
  64.2 0.8 collective-permute-done.3
  65.0 4.2 %all-to-all-done.2.received = bf16[8,96,256]{2,1,0:T(8,128)(2,1)S(1)} async-done(((bf16[8,96,256]{2,1,0:T(8,128)(2,1)}), bf16[8,96,256]{2,1,0:T(8,128)(2,1)S(1)}, u32[]{:S(2)}, u32[]{:S(2)}) %all-to-all-start.2) | async-done | bytes 393248 | tf_op jit(solution)/shard_map/all_to_all | solution.py:332
  69.2 1.5 %sum.1 = (bf16[64,4,384]{2,1,0:T(4,128)(2,1)}, f32[1,128]{1,0:T(1,128)S(1)}) custom-call(bf16[8,96,256]{2,1,0:T(8,128)(2,1)S(1)} %all-to-all-done.2.received, f32[1,512]{1,0:T(1,128)S(1)} %reshape.83.targets, f32[1,128]{1,0:T(1,128)S(1)} %add.33.squares), custom_call_target="tpu_custom_call" | custom-call | tf_op jit(solution)/shard_map/sum/pallas_call | solution.py:338
  70.7 5.1 %all-to-all-start.3 = ((bf16[64,4,384]{2,1,0:T(4,128)(2,1)}), bf16[64,4,384]{2,1,0:T(4,128)(2,1)S(1)}, u32[]{:S(2)}, u32[]{:S(2)}) async-start(bf16[64,4,384]{2,1,0:T(4,128)(2,1)} %get-tuple-element.28), calls=%async_computation.3 | async-start | bytes 393216 | tf_op jit(solution)/shard_map/all_to_all | solution.py:343
  75.8 10.9 %all-to-all-done.3 = bf16[64,4,384]{2,1,0:T(4,128)(2,1)S(1)} async-done(((bf16[64,4,384]{2,1,0:T(4,128)(2,1)}), bf16[64,4,384]{2,1,0:T(4,128)(2,1)S(1)}, u32[]{:S(2)}, u32[]{:S(2)}) %all-to-all-start.3) | async-done | bytes 196640 | tf_op jit(solution)/shard_map/all_to_all | solution.py:343
  86.7 0.1 reshape.84.received
  86.7 1.2 %final.1 = f32[64,192]{1,0:T(8,128)} custom-call(bf16[256,384]{1,0:T(8,128)(2,1)S(1)} %reshape.84.received, f32[64,192]{1,0:T(8,128)S(1)} %get-tuple-element.29.ancestors), custom_call_target="tpu_custom_call" | custom-call | tf_op jit(solution)/shard_map/final/pallas_call | solution.py:344
  (7 shorter events, 0.0 us)
Async XLA Ops:
  0.6 6.0 %collective-permute-start = (f32[12,16,192]{2,1,0:T(8,128)}, f32[12,16,192]{2,1,0:T(8,128)S(1)}, u32[]{:S(2)}, u32[]{:S(2)}) collective-permute-start(f32[12,16,192]{2,1,0:T(8,128)} %own.1), channel_id=1, source_target_pairs={{0,4},{4,0},{8,12},{12,8},{16,20},{20,16},{24,28},{28,24},{32,36},... | collective-permute-start | bytes 442376 | tf_op jit(solution)/shard_map/ppermute | solution.py:280
  4.0 8.4 %collective-permute-start.1 = (f32[12,16,192]{2,1,0:T(8,128)}, f32[12,16,192]{2,1,0:T(8,128)S(1)}, u32[]{:S(2)}, u32[]{:S(2)}) collective-permute-start(f32[12,16,192]{2,1,0:T(8,128)} %own.1), channel_id=1, source_target_pairs={{4,8},{8,4},{12,16},{16,12},{20,24},{24,20},{28,32},{32,28},{36,40... | collective-permute-start | bytes 442376 | tf_op jit(solution)/shard_map/ppermute | solution.py:279
  5.9 0.7 copy-start.5
  5.9 0.7 copy-start.4
  5.9 0.7 copy-start.6
  5.9 0.9 %copy-start.2 = (f32[12,16,192]{2,1,0:T(8,128)S(1)}, f32[12,16,192]{2,1,0:T(8,128)}, u32[]{:S(2)}) copy-start(f32[12,16,192]{2,1,0:T(8,128)} %loads.1) | copy-start | bytes 442372
  5.9 1.0 %copy-start.3 = (f32[12,16,192]{2,1,0:T(8,128)S(1)}, f32[12,16,192]{2,1,0:T(8,128)}, u32[]{:S(2)}) copy-start(f32[12,16,192]{2,1,0:T(8,128)} %own.1) | copy-start | bytes 442372
  7.0 3.0 %copy-start = (f32[12,4,36864]{2,1,0:T(4,128)S(1)}, f32[12,4,36864]{2,1,0:T(4,128)}, u32[]{:S(2)}) copy-start(f32[12,4,36864]{2,1,0:T(4,128)} %param.10) | copy-start | bytes 21233668
  36.2 16.8 %copy-start.1 = (bf16[8,36864]{1,0:T(8,128)(2,1)S(1)}, bf16[8,36864]{1,0:T(8,128)(2,1)}, u32[]{:S(2)}) copy-start(bf16[8,36864]{1,0:T(8,128)(2,1)} %param.13) | copy-start | bytes 1769476
  37.8 15.2 %all-to-all-start.1 = ((bf16[64,8,128]{2,1,0:T(8,128)(2,1)}), bf16[64,8,128]{2,1,0:T(8,128)(2,1)S(1)}, u32[]{:S(2)}, u32[]{:S(2)}) async-start(bf16[64,8,128]{2,1,0:T(8,128)(2,1)} %bitcast.7), calls=%async_computation.1 | async-start | bytes 262144 | tf_op jit(solution)/shard_map/all_to_all | solution.py:310
  42.6 2.7 %collective-permute-start.2 = (f32[1,128]{1,0:T(1,128)S(1)}, f32[1,128]{1,0:T(1,128)S(1)}, u32[]{:S(2)}, u32[]{:S(2)}) collective-permute-start(f32[1,128]{1,0:T(1,128)S(1)} %get-tuple-element.23), channel_id=1, source_target_pairs={{0,1},{1,0},{2,3},{3,2},{4,5},{5,4},{6,7},{7,6},{8,9},{9,8},{10,11... | collective-permute-start | bytes 1544 | tf_op jit(solution)/shard_map/ppermute | solution.py:313
  57.3 11.9 %all-to-all-start.2 = ((bf16[8,96,256]{2,1,0:T(8,128)(2,1)}), bf16[8,96,256]{2,1,0:T(8,128)(2,1)S(1)}, u32[]{:S(2)}, u32[]{:S(2)}) async-start(bf16[8,96,256]{2,1,0:T(8,128)(2,1)} %bitcast.16), calls=%async_computation.2 | async-start | bytes 786432 | tf_op jit(solution)/shard_map/all_to_all | solution.py:332
  61.1 3.9 %collective-permute-start.3 = (f32[1,128]{1,0:T(1,128)S(1)}, f32[1,128]{1,0:T(1,128)S(1)}, u32[]{:S(2)}, u32[]{:S(2)}) collective-permute-start(f32[1,128]{1,0:T(1,128)S(1)} %get-tuple-element.27), channel_id=1, source_target_pairs={{0,2},{1,3},{2,0},{3,1},{4,6},{5,7},{6,4},{7,5},{8,10},{9,11},{10,... | collective-permute-start | bytes 1544 | tf_op jit(solution)/shard_map/ppermute | solution.py:313
  70.7 16.0 %all-to-all-start.3 = ((bf16[64,4,384]{2,1,0:T(4,128)(2,1)}), bf16[64,4,384]{2,1,0:T(4,128)(2,1)S(1)}, u32[]{:S(2)}, u32[]{:S(2)}) async-start(bf16[64,4,384]{2,1,0:T(4,128)(2,1)} %get-tuple-element.28), calls=%async_computation.3 | async-start | bytes 393216 | tf_op jit(solution)/shard_map/all_to_all | solution.py:343

commit v5 on v4

--- a/solution.py
+++ b/solution.py
@@ -60,8 +60,13 @@
     out[...] = iota((ROWS, LANES), 1)
 
 
-def split_kernel(table, blocks, chip, own, loads, lanes, high, low, cells, start, info, load_cells):
+def split_kernel(table, blocks, chip, own, loads, lanes, high, low, cells, start, info,
+                 load_cells, wide, sems):
     count = NNZ * 288
+    copies = [pltpu.make_async_copy(blocks.at[pl.ds(g * count, count)], wide.at[pl.ds(g * count, count)],
+                                    sems.at[g]) for g in range(P_SIZE)]
+    for copy in copies:
+        copy.start()
     for i in range(P_SIZE):
         put_cells(loads[i], load_cells, i)
         put_cells(chip[i], cells, i)
@@ -71,13 +76,6 @@
     unit = one_hot((unit_col == 2 * pair) | (unit_col == 2 * pair + B + 1))
     for g in range(P_SIZE):
         start[g] = lax.dot_general(unit, load_cells[g], NT, preferred_element_type=F32)
-        for j in range(NNZ):
-            for t in range(3):
-                tall = jnp.concatenate(
-                    [blocks[pl.ds(g * count + 12 * k + j + 4 * t, 32, stride=36), :] for k in range(3)], axis=0)
-                at = (g, slice(None), slice(j * 384 + t * LANES, j * 384 + (t + 1) * LANES))
-                high[at], low[at] = halves(tall)
-
     lane = lanes[...]
     notes = jnp.zeros((ROWS, LANES), jnp.int32)
     for k in range(LEAF):
@@ -88,6 +86,17 @@
         notes = jnp.where(lane == 64 + i, source // P_SIZE, notes)
         notes = jnp.where(lane == 76 + i, source % P_SIZE, notes)
     info[...] = notes.astype(F32)[:1]
+
+    for g in range(P_SIZE):
+        if g % 2 == 0:
+            for copy in copies[g:g + 2]:
+                copy.wait()
+        for j in range(NNZ):
+            for t in range(3):
+                tall = jnp.concatenate(
+                    [wide[pl.ds(g * count + 12 * k + j + 4 * t, 32, stride=36), :] for k in range(3)], axis=0)
+                at = (g, slice(None), slice(j * 384 + t * LANES, j * 384 + (t + 1) * LANES))
+                high[at], low[at] = halves(tall)
 
 
 def residual_kernel(table, high, low, near, start, info, far, out, cells, message):
@@ -296,7 +305,8 @@
         split_kernel, "split",
         [((P_SIZE, PAIRS, 1536), BF16), ((P_SIZE, PAIRS, 1536), BF16), ((2 * P_SIZE, 64, 384), BF16),
          ((P_SIZE, PAIRS, 64), F32), ((1, LANES), F32)],
-        [smem] + [vmem] * 5, [pltpu.VMEM((P_SIZE, 64, 384), BF16)], 16,
+        [smem, hbm] + [vmem] * 4,
+        [pltpu.VMEM((P_SIZE, 64, 384), BF16), pltpu.VMEM((P_SIZE * 1152, LANES), F32), dma((P_SIZE,))], 41,
         pl.CostEstimate(flops=10**9, bytes_accessed=14 * 10**6, transcendentals=0),
     )(table, natural, chip, solution, loads, lanes)
     (message,) = call(

time: 89.5 us -> 88.7 us (level)
  local copies, waits for them, and re-layouts: 4.23 us -> 1.2 us
  Pallas kernels: 14.1 us -> 16.2 us
    unnamed x14 -> x12, local copies, waits for them, and re-layouts: 4.01 us -> 0.97 us
    pallas_call x1, Pallas kernels: 2.39 us -> 4.49 us  [on_device(): call(split_kernel, 'split', [((P_SIZE, PAIRS, 1536), BF16), ((P_SIZE, PAI...]
  transfers between devices with their start and end apart: 7 -> 7, of which waited for: 5 -> 5; matrix products, arithmetic and copies ran while one was open for 0% -> 0% of each run, Pallas kernels for 3% -> 5%
where the time goes in v5:
time: 88.7 us; the launch traced here: 88.3 us
  waiting for transfers between devices  24.8 us (28%)
  starting transfers between devices  23.3 us (26%)
  blocking collectives  20.8 us (23%)
  Pallas kernels  16.2 us (18%)
  between operations  2 us (2%)
  local copies, waits for them, and re-layouts  1.2 us (1%)
    all_to_all x1, blocking collectives, exchange(): return lax.all_to_all(x, 'dom', 0, 0, tiled=True).reshape(DOM * ROWS, LANES)  20.8 us
    all_to_all x1, waiting for transfers between devices, on_device(): sums = lax.all_to_all(sums, 'dom', 0, 0, tiled=True)  10.9 us
    all_to_all x1, waiting for transfers between devices, exchange(): return lax.all_to_all(x, 'dom', 0, 0, tiled=True).reshape(DOM * ROWS, LANES)  7.65 us
    all_to_all x1, starting transfers between devices, on_device(): sums = lax.all_to_all(sums, 'dom', 0, 0, tiled=True)  5.08 us
    all_to_all x1, starting transfers between devices, exchange(): return lax.all_to_all(x, 'dom', 0, 0, tiled=True).reshape(DOM * ROWS, LANES)  4.88 us
    pallas_call x1, Pallas kernels, on_device(): call(split_kernel, 'split', [((P_SIZE, PAIRS, 1536), BF16), ((P_SIZE, PAI...  4.49 us
    ppermute x2, starting transfers between devices, across(): return x + lax.ppermute(x, 'rhs', [(i, i ^ step) for i in range(4)])  4.3 us
    pallas_call x1, Pallas kernels, on_device(): call(update_kernel, 'update', [((LEAF * CASES, B), BF16), ((ANC * CASES,...  4.26 us
  transfers between devices with their start and end apart: 7, of which 5 were waited for; matrix products, arithmetic and copies ran while one was open for 0% of the time, Pallas kernels for 5%

profile of v5, /device:TPU:1, one launch (start us, length us, event | category | flops | bytes accessed | tf_op | source)
XLA Modules:
  0.0 88.3 jit_solution(4696601927538691066)
XLA Ops:
  0.6 3.3 %collective-permute-start = (f32[12,16,192]{2,1,0:T(8,128)}, f32[12,16,192]{2,1,0:T(8,128)S(1)}, u32[]{:S(2)}, u32[]{:S(2)}) collective-permute-start(f32[12,16,192]{2,1,0:T(8,128)} %own.1), channel_id=1, source_target_pairs={{0,4},{4,0},{8,12},{12,8},{16,20},{20,16},{24,28},{28,24},{32,36},... | collective-permute-start | bytes 442376 | tf_op jit(solution)/shard_map/ppermute | solution.py:289
  4.0 1.9 %collective-permute-start.1 = (f32[12,16,192]{2,1,0:T(8,128)}, f32[12,16,192]{2,1,0:T(8,128)S(1)}, u32[]{:S(2)}, u32[]{:S(2)}) collective-permute-start(f32[12,16,192]{2,1,0:T(8,128)} %own.1), channel_id=1, source_target_pairs={{4,8},{8,4},{12,16},{16,12},{20,24},{24,20},{28,32},{32,28},{36,40... | collective-permute-start | bytes 442376 | tf_op jit(solution)/shard_map/ppermute | solution.py:288
  5.9 0.0 copy-start.4
  5.9 0.0 copy-start.3
  5.9 0.0 copy-start.5
  5.9 0.0 copy-start.1
  5.9 0.0 copy-start.2
  6.0 0.6 copy-done.4
  6.6 0.0 copy-done.3
  6.6 0.0 copy-done.5
  6.6 0.0 collective-permute-done.chip
  6.6 0.2 copy-done.1
  6.9 0.1 copy-done.2
  7.0 4.5 %split.1 = (bf16[12,96,1536]{2,1,0:T(8,128)(2,1)S(1)}, bf16[12,96,1536]{2,1,0:T(8,128)(2,1)S(1)}, bf16[24,64,384]{2,1,0:T(8,128)(2,1)S(1)}, f32[12,96,64]{2,1,0:T(8,128)S(1)}, f32[1,128]{1,0:T(1,128)S(1)}) custom-call(s32[16,128]{1,0:T(8,128)S(1)} %pad_add_fusion.table, f32[13824,128]{1,0:T(8,128)} %bitcast.43, ...), custom_call_target="tpu_custom_call" | custom-call | flops 1000000000 | bytes 14000000 | tf_op jit(solution)/shard_map/split/pallas_call | solution.py:304
  11.5 0.0 collective-permute-done.1.far
  11.5 3.2 %residual.1 = bf16[512,128]{1,0:T(8,128)(2,1)S(1)} custom-call(s32[16,128]{1,0:T(8,128)S(1)} %pad_add_fusion.table, bf16[12,96,1536]{2,1,0:T(8,128)(2,1)S(1)} %get-tuple-element.17.high, bf16[12,96,1536]{2,1,0:T(8,128)(2,1)S(1)} %get-tuple-element.18.low, bf16[24,64,384]{2,1,0:T(8,128)(2,1)S(1)} %get-tuple-element.19.near, ...), custom_call_target="tpu_custom_call" | custom-call | tf_op jit(solution)/shard_map/residual/pallas_call | solution.py:312
  14.6 20.8 %all_to_all.20 = bf16[64,8,128]{2,1,0:T(8,128)(2,1)S(1)} all-to-all(bf16[64,8,128]{2,1,0:T(8,128)(2,1)S(1)} %bitcast.38), channel_id=1, replica_groups=mesh['dom'=64,'rhs'=4] {'dom'}, dimensions={0} | all-to-all | bytes 262144 | tf_op jit(solution)/shard_map/all_to_all | solution.py:320
  35.5 0.0 copy-start
  35.5 1.5 %permute.1 = (bf16[512,128]{1,0:T(8,128)(2,1)}, f32[64,128]{1,0:T(8,128)S(1)}, f32[1,128]{1,0:T(1,128)S(1)}) custom-call(bf16[512,128]{1,0:T(8,128)(2,1)S(1)} %bitcast.40), custom_call_target="tpu_custom_call" | custom-call | flops 4000000000 | bytes 1000000 | tf_op jit(solution)/shard_map/permute/pallas_call | solution.py:325
  37.0 4.9 %all-to-all-start.1 = ((bf16[64,8,128]{2,1,0:T(8,128)(2,1)}), bf16[64,8,128]{2,1,0:T(8,128)(2,1)S(1)}, u32[]{:S(2)}, u32[]{:S(2)}) async-start(bf16[64,8,128]{2,1,0:T(8,128)(2,1)} %bitcast.7), calls=%async_computation.1 | async-start | bytes 262144 | tf_op jit(solution)/shard_map/all_to_all | solution.py:320
  41.9 1.4 %collective-permute-start.2 = (f32[1,128]{1,0:T(1,128)S(1)}, f32[1,128]{1,0:T(1,128)S(1)}, u32[]{:S(2)}, u32[]{:S(2)}) collective-permute-start(f32[1,128]{1,0:T(1,128)S(1)} %get-tuple-element.23), channel_id=1, source_target_pairs={{0,1},{1,0},{2,3},{3,2},{4,5},{5,4},{6,7},{7,6},{8,9},{9,8},{10,11... | collective-permute-start | bytes 1544 | tf_op jit(solution)/shard_map/ppermute | solution.py:323
  43.3 1.3 %collective-permute-done.2 = f32[1,128]{1,0:T(1,128)S(1)} collective-permute-done((f32[1,128]{1,0:T(1,128)S(1)}, f32[1,128]{1,0:T(1,128)S(1)}, u32[]{:S(2)}, u32[]{:S(2)}) %collective-permute-start.2) | collective-permute-done | bytes 544 | tf_op jit(solution)/shard_map/ppermute | solution.py:323
  44.6 7.6 %all-to-all-done.1 = bf16[64,8,128]{2,1,0:T(8,128)(2,1)S(1)} async-done(((bf16[64,8,128]{2,1,0:T(8,128)(2,1)}), bf16[64,8,128]{2,1,0:T(8,128)(2,1)S(1)}, u32[]{:S(2)}, u32[]{:S(2)}) %all-to-all-start.1) | async-done | bytes 131104 | tf_op jit(solution)/shard_map/all_to_all | solution.py:320
  52.3 0.0 copy-done
  52.3 4.3 %update.1 = (bf16[128,192]{1,0:T(8,128)(2,1)}, f32[64,192]{1,0:T(8,128)S(1)}, bf16[768,256]{1,0:T(8,128)(2,1)}, f32[1,128]{1,0:T(1,128)S(1)}) custom-call(bf16[512,128]{1,0:T(8,128)(2,1)S(1)} %bitcast.39, bf16[96,3,8,128]{3,2,1,0:T(8,128)(2,1)S(1)} %bitcast.37, bf16[768,3,8,128]{3,2,1,0:T(8,128)(2,1)} %bitcast.44, f32[1,128]{1,0:T(1,128)S(1)} %add.30.squares), custom_call_target="tpu_custom_call" | custom-call | tf_op jit(solution)/shard_map/update/pallas_call | solution.py:332
  56.5 3.8 %all-to-all-start.2 = ((bf16[8,96,256]{2,1,0:T(8,128)(2,1)}), bf16[8,96,256]{2,1,0:T(8,128)(2,1)S(1)}, u32[]{:S(2)}, u32[]{:S(2)}) async-start(bf16[8,96,256]{2,1,0:T(8,128)(2,1)} %bitcast.16), calls=%async_computation.2 | async-start | bytes 786432 | tf_op jit(solution)/shard_map/all_to_all | solution.py:342
  60.3 2.9 %collective-permute-start.3 = (f32[1,128]{1,0:T(1,128)S(1)}, f32[1,128]{1,0:T(1,128)S(1)}, u32[]{:S(2)}, u32[]{:S(2)}) collective-permute-start(f32[1,128]{1,0:T(1,128)S(1)} %get-tuple-element.27), channel_id=1, source_target_pairs={{0,2},{1,3},{2,0},{3,1},{4,6},{5,7},{6,4},{7,5},{8,10},{9,11},{10,... | collective-permute-start | bytes 1544 | tf_op jit(solution)/shard_map/ppermute | solution.py:323
  63.2 0.1 reshape.82
  63.3 0.1 reshape.83.targets
  63.4 0.8 collective-permute-done.3
  64.2 4.2 %all-to-all-done.2.received = bf16[8,96,256]{2,1,0:T(8,128)(2,1)S(1)} async-done(((bf16[8,96,256]{2,1,0:T(8,128)(2,1)}), bf16[8,96,256]{2,1,0:T(8,128)(2,1)S(1)}, u32[]{:S(2)}, u32[]{:S(2)}) %all-to-all-start.2) | async-done | bytes 393248 | tf_op jit(solution)/shard_map/all_to_all | solution.py:342
  68.4 1.5 %sum.1 = (bf16[64,4,384]{2,1,0:T(4,128)(2,1)}, f32[1,128]{1,0:T(1,128)S(1)}) custom-call(bf16[8,96,256]{2,1,0:T(8,128)(2,1)S(1)} %all-to-all-done.2.received, f32[1,512]{1,0:T(1,128)S(1)} %reshape.83.targets, f32[1,128]{1,0:T(1,128)S(1)} %add.33.squares), custom_call_target="tpu_custom_call" | custom-call | tf_op jit(solution)/shard_map/sum/pallas_call | solution.py:348
  69.9 5.1 %all-to-all-start.3 = ((bf16[64,4,384]{2,1,0:T(4,128)(2,1)}), bf16[64,4,384]{2,1,0:T(4,128)(2,1)S(1)}, u32[]{:S(2)}, u32[]{:S(2)}) async-start(bf16[64,4,384]{2,1,0:T(4,128)(2,1)} %get-tuple-element.28), calls=%async_computation.3 | async-start | bytes 393216 | tf_op jit(solution)/shard_map/all_to_all | solution.py:353
  75.1 10.9 %all-to-all-done.3 = bf16[64,4,384]{2,1,0:T(4,128)(2,1)S(1)} async-done(((bf16[64,4,384]{2,1,0:T(4,128)(2,1)}), bf16[64,4,384]{2,1,0:T(4,128)(2,1)S(1)}, u32[]{:S(2)}, u32[]{:S(2)}) %all-to-all-start.3) | async-done | bytes 196640 | tf_op jit(solution)/shard_map/all_to_all | solution.py:353
  85.9 0.1 reshape.84.received
  86.0 1.2 %final.1 = f32[64,192]{1,0:T(8,128)} custom-call(bf16[256,384]{1,0:T(8,128)(2,1)S(1)} %reshape.84.received, f32[64,192]{1,0:T(8,128)S(1)} %get-tuple-element.29.ancestors), custom_call_target="tpu_custom_call" | custom-call | tf_op jit(solution)/shard_map/final/pallas_call | solution.py:354
  (7 shorter events, 0.0 us)
Async XLA Ops:
  0.6 6.0 %collective-permute-start = (f32[12,16,192]{2,1,0:T(8,128)}, f32[12,16,192]{2,1,0:T(8,128)S(1)}, u32[]{:S(2)}, u32[]{:S(2)}) collective-permute-start(f32[12,16,192]{2,1,0:T(8,128)} %own.1), channel_id=1, source_target_pairs={{0,4},{4,0},{8,12},{12,8},{16,20},{20,16},{24,28},{28,24},{32,36},... | collective-permute-start | bytes 442376 | tf_op jit(solution)/shard_map/ppermute | solution.py:289
  4.0 7.5 %collective-permute-start.1 = (f32[12,16,192]{2,1,0:T(8,128)}, f32[12,16,192]{2,1,0:T(8,128)S(1)}, u32[]{:S(2)}, u32[]{:S(2)}) collective-permute-start(f32[12,16,192]{2,1,0:T(8,128)} %own.1), channel_id=1, source_target_pairs={{4,8},{8,4},{12,16},{16,12},{20,24},{24,20},{28,32},{32,28},{36,40... | collective-permute-start | bytes 442376 | tf_op jit(solution)/shard_map/ppermute | solution.py:288
  5.9 0.7 copy-start.4
  5.9 0.7 copy-start.3
  5.9 0.7 copy-start.5
  5.9 0.9 %copy-start.1 = (f32[12,16,192]{2,1,0:T(8,128)S(1)}, f32[12,16,192]{2,1,0:T(8,128)}, u32[]{:S(2)}) copy-start(f32[12,16,192]{2,1,0:T(8,128)} %loads.1) | copy-start | bytes 442372
  5.9 1.0 %copy-start.2 = (f32[12,16,192]{2,1,0:T(8,128)S(1)}, f32[12,16,192]{2,1,0:T(8,128)}, u32[]{:S(2)}) copy-start(f32[12,16,192]{2,1,0:T(8,128)} %own.1) | copy-start | bytes 442372
  35.5 16.8 %copy-start = (bf16[8,36864]{1,0:T(8,128)(2,1)S(1)}, bf16[8,36864]{1,0:T(8,128)(2,1)}, u32[]{:S(2)}) copy-start(bf16[8,36864]{1,0:T(8,128)(2,1)} %param.13) | copy-start | bytes 1769476
  37.0 15.2 %all-to-all-start.1 = ((bf16[64,8,128]{2,1,0:T(8,128)(2,1)}), bf16[64,8,128]{2,1,0:T(8,128)(2,1)S(1)}, u32[]{:S(2)}, u32[]{:S(2)}) async-start(bf16[64,8,128]{2,1,0:T(8,128)(2,1)} %bitcast.7), calls=%async_computation.1 | async-start | bytes 262144 | tf_op jit(solution)/shard_map/all_to_all | solution.py:320
  41.9 2.7 %collective-permute-start.2 = (f32[1,128]{1,0:T(1,128)S(1)}, f32[1,128]{1,0:T(1,128)S(1)}, u32[]{:S(2)}, u32[]{:S(2)}) collective-permute-start(f32[1,128]{1,0:T(1,128)S(1)} %get-tuple-element.23), channel_id=1, source_target_pairs={{0,1},{1,0},{2,3},{3,2},{4,5},{5,4},{6,7},{7,6},{8,9},{9,8},{10,11... | collective-permute-start | bytes 1544 | tf_op jit(solution)/shard_map/ppermute | solution.py:323
  56.5 11.9 %all-to-all-start.2 = ((bf16[8,96,256]{2,1,0:T(8,128)(2,1)}), bf16[8,96,256]{2,1,0:T(8,128)(2,1)S(1)}, u32[]{:S(2)}, u32[]{:S(2)}) async-start(bf16[8,96,256]{2,1,0:T(8,128)(2,1)} %bitcast.16), calls=%async_computation.2 | async-start | bytes 786432 | tf_op jit(solution)/shard_map/all_to_all | solution.py:342
  60.3 3.9 %collective-permute-start.3 = (f32[1,128]{1,0:T(1,128)S(1)}, f32[1,128]{1,0:T(1,128)S(1)}, u32[]{:S(2)}, u32[]{:S(2)}) collective-permute-start(f32[1,128]{1,0:T(1,128)S(1)} %get-tuple-element.27), channel_id=1, source_target_pairs={{0,2},{1,3},{2,0},{3,1},{4,6},{5,7},{6,4},{7,5},{8,10},{9,11},{10,... | collective-permute-start | bytes 1544 | tf_op jit(solution)/shard_map/ppermute | solution.py:323
  69.9 16.0 %all-to-all-start.3 = ((bf16[64,4,384]{2,1,0:T(4,128)(2,1)}), bf16[64,4,384]{2,1,0:T(4,128)(2,1)S(1)}, u32[]{:S(2)}, u32[]{:S(2)}) async-start(bf16[64,4,384]{2,1,0:T(4,128)(2,1)} %get-tuple-element.28), calls=%async_computation.3 | async-start | bytes 393216 | tf_op jit(solution)/shard_map/all_to_all | solution.py:353

commit v6 on v5

--- a/solution.py
+++ b/solution.py
@@ -168,13 +168,22 @@
     out[...] = message[...].astype(BF16)
 
 
-def update_kernel(received, inverses, tiles, squares, level, ancestors, out, squares_out,
-                  wide, leaf, rest, right, near, sems, partial):
-    copies = [pltpu.make_async_copy(tiles.at[pl.ds(k * PAIRS, PAIRS)], near.at[pl.ds(k * PAIRS, PAIRS)],
-                                    sems.at[k]) for k in range(LEAF)]
+def fetch_kernel(notes, tiles, out, sems):
+    step = PAIRS * LEAF // 8
+    copies = [pltpu.make_async_copy(tiles.at[pl.ds(n * step, step)], out.at[pl.ds(n * step, step)], sems.at[n])
+              for n in range(LEAF // 2)]
     for copy in copies:
         copy.start()
-    squares_out[...] = squares[...]
+    for copy in copies:
+        copy.wait()
+
+
+def update_kernel(received, inverses, tiles, early, level, ancestors, out,
+                  wide, leaf, rest, right, near, sems, partial):
+    copies = [pltpu.make_async_copy(tiles.at[pl.ds(k * PAIRS, PAIRS)], near.at[pl.ds((k - LEAF // 2) * PAIRS, PAIRS)],
+                                    sems.at[k - LEAF // 2]) for k in range(LEAF // 2, LEAF)]
+    for copy in copies:
+        copy.start()
     wide[...] = received[...].astype(F32)
     for k in range(3):
         for par in range(2):
@@ -206,12 +215,13 @@
         right[k * 384:(k + 1) * 384] = doubled(jnp.where(owner == k, solved, 0.0)).astype(BF16)
     step, band = LEAF // 2, PAIRS // 2
     for first in range(0, LEAF, step):
-        for copy in copies[first:first + step]:
-            copy.wait()
+        if first:
+            for copy in copies:
+                copy.wait()
         for r in range(0, PAIRS, band):
             at = slice(r * 8, (r + band) * 8)
             wide_left = jnp.concatenate(
-                [left(near, k * PAIRS + r, band) for k in range(first, first + step)], axis=1)
+                [left(near if first else early, k * PAIRS + r, band) for k in range(step)], axis=1)
             total = dot(wide_left, right[first * 384:(first + step) * 384])
             if first == 0:
                 partial[at] = total
@@ -329,14 +339,18 @@
         pl.CostEstimate(flops=4 * 10**9, bytes_accessed=10**6, transcendentals=0),
     )(exchange(message))
 
-    level, ancestors, message, squares = call(
+    half = (LEAF // 2 * PAIRS, 3, UPD, LANES)
+    (early,) = call(fetch_kernel, "fetch", [(half, BF16)], [vmem, hbm], [dma((LEAF // 2,))], 50,
+                    pl.CostEstimate(flops=2 * 10**9, bytes_accessed=10**6, transcendentals=0),
+                    )(notes, natural_tiles)
+    level, ancestors, message = call(
         update_kernel, "update",
-        [((LEAF * CASES, B), BF16), ((ANC * CASES, B), F32), ((PAIRS * UPD, 256), BF16), ((1, LANES), F32)],
+        [((LEAF * CASES, B), BF16), ((ANC * CASES, B), F32), ((PAIRS * UPD, 256), BF16)],
         [vmem, vmem, hbm, vmem],
         [pltpu.VMEM((DOM * ROWS, LANES), F32), pltpu.VMEM((B, LANES), F32), pltpu.VMEM((B, LANES), F32),
-         pltpu.VMEM((LEAF * 384, 256), BF16), pltpu.VMEM((LEAF * PAIRS, 3, UPD, LANES), BF16),
-         dma((LEAF,)), pltpu.VMEM((PAIRS * UPD, 256), F32)], 52,
-    )(exchange(message), natural_inverses, natural_tiles, across(squares, 1))
+         pltpu.VMEM((LEAF * 384, 256), BF16), pltpu.VMEM(half, BF16),
+         dma((LEAF // 2,)), pltpu.VMEM((PAIRS * UPD, 256), F32)], 48,
+    )(exchange(message), natural_inverses, natural_tiles, early)
 
     groups = [[(x * N_Z + z) * N_CORE + c for x in range(N_X) for c in range(N_CORE)] for z in range(N_Z)]
     received = lax.all_to_all(
@@ -348,8 +362,8 @@
     sums, squares = call(
         sum_kernel, "sum", [((DOM, ANC, 384), BF16), ((1, LANES), F32)], [vmem] * 3,
         [pltpu.VMEM((512, 384), BF16)],
-    )(received, near, across(squares, 2))
-    residual_rms = jnp.sqrt(squares[0, 0] / (DOM * P_SIZE * CASES * 4 * B))
+    )(received, near, across(squares, 1))
+    residual_rms = jnp.sqrt(across(squares, 2)[0, 0] / (DOM * P_SIZE * CASES * 4 * B))
     sums = lax.all_to_all(sums, "dom", 0, 0, tiled=True)
     (ancestor_rhs,) = call(final_kernel, "final", [((ANC * CASES, B), F32)], [vmem] * 2, [])(
         sums.reshape(DOM * ANC, 384), ancestors)

time: 88.7 us -> 88.2 us (level)
  waiting for transfers between devices: 24.8 us -> 23.1 us
  Pallas kernels: 16.2 us -> 17.3 us
    all_to_all x1, waiting for transfers between devices: 10.9 us -> 6.86 us  [on_device(): sums = lax.all_to_all(sums, 'dom', 0, 0, tiled=True)]
    pallas_call x0 -> x1, Pallas kernels: none -> 1.7 us  [on_device(): call(fetch_kernel, 'fetch', [(half, BF16)], [vmem, hbm], [dma((LEAF // 2,...]
    all_to_all x1, waiting for transfers between devices: 4.2 us -> 5.7 us  [on_device(): lax.all_to_all(message.reshape(GROUP, 96, 256), 'dom', 0, 0, axis_index_g...]
    all_to_all x1, waiting for transfers between devices: 7.65 us -> 8.65 us  [exchange(): return lax.all_to_all(x, 'dom', 0, 0, tiled=True).reshape(DOM * ROWS, LANES)]
  transfers between devices with their start and end apart: 7 -> 7, of which waited for: 5 -> 5; matrix products, arithmetic and copies ran while one was open for 0% -> 0% of each run, Pallas kernels for 5% -> 7%
where the time goes in v6:
time: 88.2 us; the launch traced here: 87.7 us
  starting transfers between devices  23.3 us (26%)
  waiting for transfers between devices  23.1 us (26%)
  blocking collectives  20.8 us (24%)
  Pallas kernels  17.3 us (20%)
  between operations  2.02 us (2%)
  local copies, waits for them, and re-layouts  1.2 us (1%)
    all_to_all x1, blocking collectives, exchange(): return lax.all_to_all(x, 'dom', 0, 0, tiled=True).reshape(DOM * ROWS, LANES)  20.8 us
    all_to_all x1, waiting for transfers between devices, exchange(): return lax.all_to_all(x, 'dom', 0, 0, tiled=True).reshape(DOM * ROWS, LANES)  8.65 us
    all_to_all x1, waiting for transfers between devices, on_device(): sums = lax.all_to_all(sums, 'dom', 0, 0, tiled=True)  6.86 us
    all_to_all x1, waiting for transfers between devices, on_device(): lax.all_to_all(message.reshape(GROUP, 96, 256), 'dom', 0, 0, axis_index_g...  5.7 us
    all_to_all x1, starting transfers between devices, on_device(): sums = lax.all_to_all(sums, 'dom', 0, 0, tiled=True)  5.08 us
    all_to_all x1, starting transfers between devices, exchange(): return lax.all_to_all(x, 'dom', 0, 0, tiled=True).reshape(DOM * ROWS, LANES)  4.88 us
    pallas_call x1, Pallas kernels, on_device(): call(split_kernel, 'split', [((P_SIZE, PAIRS, 1536), BF16), ((P_SIZE, PAI...  4.49 us
    ppermute x2, starting transfers between devices, across(): return x + lax.ppermute(x, 'rhs', [(i, i ^ step) for i in range(4)])  4.3 us
  transfers between devices with their start and end apart: 7, of which 5 were waited for; matrix products, arithmetic and copies ran while one was open for 0% of the time, Pallas kernels for 7%

profile of v6, /device:TPU:1, one launch (start us, length us, event | category | flops | bytes accessed | tf_op | source)
XLA Modules:
  0.0 87.7 jit_solution(11789493103823892237)
XLA Ops:
  0.6 3.3 %collective-permute-start = (f32[12,16,192]{2,1,0:T(8,128)}, f32[12,16,192]{2,1,0:T(8,128)S(1)}, u32[]{:S(2)}, u32[]{:S(2)}) collective-permute-start(f32[12,16,192]{2,1,0:T(8,128)} %own.1), channel_id=1, source_target_pairs={{0,4},{4,0},{8,12},{12,8},{16,20},{20,16},{24,28},{28,24},{32,36},... | collective-permute-start | bytes 442376 | tf_op jit(solution)/shard_map/ppermute | solution.py:299
  4.0 1.9 %collective-permute-start.1 = (f32[12,16,192]{2,1,0:T(8,128)}, f32[12,16,192]{2,1,0:T(8,128)S(1)}, u32[]{:S(2)}, u32[]{:S(2)}) collective-permute-start(f32[12,16,192]{2,1,0:T(8,128)} %own.1), channel_id=1, source_target_pairs={{4,8},{8,4},{12,16},{16,12},{20,24},{24,20},{28,32},{32,28},{36,40... | collective-permute-start | bytes 442376 | tf_op jit(solution)/shard_map/ppermute | solution.py:298
  5.9 0.0 copy-start.4
  5.9 0.0 copy-start.3
  5.9 0.0 copy-start.5
  5.9 0.0 copy-start.1
  5.9 0.0 copy-start.2
  6.0 0.6 copy-done.4
  6.6 0.0 copy-done.3
  6.6 0.0 copy-done.5
  6.6 0.0 collective-permute-done.chip
  6.6 0.2 copy-done.1
  6.9 0.1 copy-done.2
  7.0 4.5 %split.1 = (bf16[12,96,1536]{2,1,0:T(8,128)(2,1)S(1)}, bf16[12,96,1536]{2,1,0:T(8,128)(2,1)S(1)}, bf16[24,64,384]{2,1,0:T(8,128)(2,1)S(1)}, f32[12,96,64]{2,1,0:T(8,128)S(1)}, f32[1,128]{1,0:T(1,128)S(1)}) custom-call(s32[16,128]{1,0:T(8,128)S(1)} %pad_add_fusion.table, f32[13824,128]{1,0:T(8,128)} %bitcast.42, ...), custom_call_target="tpu_custom_call" | custom-call | flops 1000000000 | bytes 14000000 | tf_op jit(solution)/shard_map/split/pallas_call | solution.py:314
  11.5 0.0 collective-permute-done.1.far
  11.5 3.2 %residual.1 = bf16[512,128]{1,0:T(8,128)(2,1)S(1)} custom-call(s32[16,128]{1,0:T(8,128)S(1)} %pad_add_fusion.table, bf16[12,96,1536]{2,1,0:T(8,128)(2,1)S(1)} %get-tuple-element.16.high, bf16[12,96,1536]{2,1,0:T(8,128)(2,1)S(1)} %get-tuple-element.17.low, bf16[24,64,384]{2,1,0:T(8,128)(2,1)S(1)} %get-tuple-element.18.near, ...), custom_call_target="tpu_custom_call" | custom-call | tf_op jit(solution)/shard_map/residual/pallas_call | solution.py:322
  14.6 20.8 %all_to_all.20 = bf16[64,8,128]{2,1,0:T(8,128)(2,1)S(1)} all-to-all(bf16[64,8,128]{2,1,0:T(8,128)(2,1)S(1)} %bitcast.39), channel_id=1, replica_groups=mesh['dom'=64,'rhs'=4] {'dom'}, dimensions={0} | all-to-all | bytes 262144 | tf_op jit(solution)/shard_map/all_to_all | solution.py:330
  35.5 1.5 %permute.1 = (bf16[512,128]{1,0:T(8,128)(2,1)}, f32[64,128]{1,0:T(8,128)S(1)}, f32[1,128]{1,0:T(1,128)S(1)}) custom-call(bf16[512,128]{1,0:T(8,128)(2,1)S(1)} %bitcast.40), custom_call_target="tpu_custom_call" | custom-call | flops 4000000000 | bytes 1000000 | tf_op jit(solution)/shard_map/permute/pallas_call | solution.py:335
  37.0 4.9 %all-to-all-start.1 = ((bf16[64,8,128]{2,1,0:T(8,128)(2,1)}), bf16[64,8,128]{2,1,0:T(8,128)(2,1)S(1)}, u32[]{:S(2)}, u32[]{:S(2)}) async-start(bf16[64,8,128]{2,1,0:T(8,128)(2,1)} %bitcast.7), calls=%async_computation.1 | async-start | bytes 262144 | tf_op jit(solution)/shard_map/all_to_all | solution.py:330
  41.9 0.0 copy-start
  41.9 1.7 %fetch.1.early = bf16[384,3,8,128]{3,2,1,0:T(8,128)(2,1)S(1)} custom-call(f32[64,128]{1,0:T(8,128)S(1)} %get-tuple-element.22.notes, bf16[768,3,8,128]{3,2,1,0:T(8,128)(2,1)} %bitcast.43), custom_call_target="tpu_custom_call" | custom-call | flops 2000000000 | bytes 1000000 | tf_op jit(solution)/shard_map/fetch/pallas_call | solution.py:343
  43.6 8.6 %all-to-all-done.1 = bf16[64,8,128]{2,1,0:T(8,128)(2,1)S(1)} async-done(((bf16[64,8,128]{2,1,0:T(8,128)(2,1)}), bf16[64,8,128]{2,1,0:T(8,128)(2,1)S(1)}, u32[]{:S(2)}, u32[]{:S(2)}) %all-to-all-start.1) | async-done | bytes 131104 | tf_op jit(solution)/shard_map/all_to_all | solution.py:330
  52.3 0.0 copy-done
  52.3 3.7 %update.1 = (bf16[128,192]{1,0:T(8,128)(2,1)}, f32[64,192]{1,0:T(8,128)S(1)}, bf16[768,256]{1,0:T(8,128)(2,1)}) custom-call(bf16[512,128]{1,0:T(8,128)(2,1)S(1)} %bitcast.38, bf16[96,3,8,128]{3,2,1,0:T(8,128)(2,1)S(1)} %bitcast.37, bf16[768,3,8,128]{3,2,1,0:T(8,128)(2,1)} %bitcast.44, bf16[384,3,8,128]{3,2,1,0:T(8,128)(2,1)S(1)} %fetch.1.early), custom_call_target="tpu_custom_call" | custom-call | tf_op jit(solution)/shard_map/update/pallas_call | solution.py:346
  56.0 3.8 %all-to-all-start.2 = ((bf16[8,96,256]{2,1,0:T(8,128)(2,1)}), bf16[8,96,256]{2,1,0:T(8,128)(2,1)S(1)}, u32[]{:S(2)}, u32[]{:S(2)}) async-start(bf16[8,96,256]{2,1,0:T(8,128)(2,1)} %bitcast.18), calls=%async_computation.2 | async-start | bytes 786432 | tf_op jit(solution)/shard_map/all_to_all | solution.py:356
  59.7 1.3 %collective-permute-start.2 = (f32[1,128]{1,0:T(1,128)S(1)}, f32[1,128]{1,0:T(1,128)S(1)}, u32[]{:S(2)}, u32[]{:S(2)}) collective-permute-start(f32[1,128]{1,0:T(1,128)S(1)} %get-tuple-element.25), channel_id=1, source_target_pairs={{0,1},{1,0},{2,3},{3,2},{4,5},{5,4},{6,7},{7,6},{8,9},{9,8},{10,11... | collective-permute-start | bytes 1544 | tf_op jit(solution)/shard_map/ppermute | solution.py:333
  61.0 0.1 reshape.82
  61.1 0.1 reshape.83.targets
  61.2 0.9 %collective-permute-done.2 = f32[1,128]{1,0:T(1,128)S(1)} collective-permute-done((f32[1,128]{1,0:T(1,128)S(1)}, f32[1,128]{1,0:T(1,128)S(1)}, u32[]{:S(2)}, u32[]{:S(2)}) %collective-permute-start.2) | collective-permute-done | bytes 544 | tf_op jit(solution)/shard_map/ppermute | solution.py:333
  62.1 5.7 %all-to-all-done.2.received = bf16[8,96,256]{2,1,0:T(8,128)(2,1)S(1)} async-done(((bf16[8,96,256]{2,1,0:T(8,128)(2,1)}), bf16[8,96,256]{2,1,0:T(8,128)(2,1)S(1)}, u32[]{:S(2)}, u32[]{:S(2)}) %all-to-all-start.2) | async-done | bytes 393248 | tf_op jit(solution)/shard_map/all_to_all | solution.py:356
  67.8 1.5 %sum.1 = (bf16[64,4,384]{2,1,0:T(4,128)(2,1)}, f32[1,128]{1,0:T(1,128)S(1)}) custom-call(bf16[8,96,256]{2,1,0:T(8,128)(2,1)S(1)} %all-to-all-done.2.received, f32[1,512]{1,0:T(1,128)S(1)} %reshape.83.targets, f32[1,128]{1,0:T(1,128)S(1)} %add.32.squares), custom_call_target="tpu_custom_call" | custom-call | tf_op jit(solution)/shard_map/sum/pallas_call | solution.py:362
  69.3 5.1 %all-to-all-start.3 = ((bf16[64,4,384]{2,1,0:T(4,128)(2,1)}), bf16[64,4,384]{2,1,0:T(4,128)(2,1)S(1)}, u32[]{:S(2)}, u32[]{:S(2)}) async-start(bf16[64,4,384]{2,1,0:T(4,128)(2,1)} %get-tuple-element.26), calls=%async_computation.3 | async-start | bytes 393216 | tf_op jit(solution)/shard_map/all_to_all | solution.py:367
  74.4 3.0 %collective-permute-start.3 = (f32[1,128]{1,0:T(1,128)S(1)}, f32[1,128]{1,0:T(1,128)S(1)}, u32[]{:S(2)}, u32[]{:S(2)}) collective-permute-start(f32[1,128]{1,0:T(1,128)S(1)} %get-tuple-element.28), channel_id=1, source_target_pairs={{0,2},{1,3},{2,0},{3,1},{4,6},{5,7},{6,4},{7,5},{8,10},{9,11},{10,... | collective-permute-start | bytes 1544 | tf_op jit(solution)/shard_map/ppermute | solution.py:333
  77.4 1.0 %collective-permute-done.3 = f32[1,128]{1,0:T(1,128)S(1)} collective-permute-done((f32[1,128]{1,0:T(1,128)S(1)}, f32[1,128]{1,0:T(1,128)S(1)}, u32[]{:S(2)}, u32[]{:S(2)}) %collective-permute-start.3) | collective-permute-done | bytes 544 | tf_op jit(solution)/shard_map/ppermute | solution.py:333
  78.5 6.9 %all-to-all-done.3 = bf16[64,4,384]{2,1,0:T(4,128)(2,1)S(1)} async-done(((bf16[64,4,384]{2,1,0:T(4,128)(2,1)}), bf16[64,4,384]{2,1,0:T(4,128)(2,1)S(1)}, u32[]{:S(2)}, u32[]{:S(2)}) %all-to-all-start.3) | async-done | bytes 196640 | tf_op jit(solution)/shard_map/all_to_all | solution.py:367
  85.3 0.1 reshape.84.received
  85.4 1.2 %final.1 = f32[64,192]{1,0:T(8,128)} custom-call(bf16[256,384]{1,0:T(8,128)(2,1)S(1)} %reshape.84.received, f32[64,192]{1,0:T(8,128)S(1)} %get-tuple-element.27.ancestors), custom_call_target="tpu_custom_call" | custom-call | tf_op jit(solution)/shard_map/final/pallas_call | solution.py:368
  (7 shorter events, 0.0 us)
Async XLA Ops:
  0.6 6.0 %collective-permute-start = (f32[12,16,192]{2,1,0:T(8,128)}, f32[12,16,192]{2,1,0:T(8,128)S(1)}, u32[]{:S(2)}, u32[]{:S(2)}) collective-permute-start(f32[12,16,192]{2,1,0:T(8,128)} %own.1), channel_id=1, source_target_pairs={{0,4},{4,0},{8,12},{12,8},{16,20},{20,16},{24,28},{28,24},{32,36},... | collective-permute-start | bytes 442376 | tf_op jit(solution)/shard_map/ppermute | solution.py:299
  4.0 7.5 %collective-permute-start.1 = (f32[12,16,192]{2,1,0:T(8,128)}, f32[12,16,192]{2,1,0:T(8,128)S(1)}, u32[]{:S(2)}, u32[]{:S(2)}) collective-permute-start(f32[12,16,192]{2,1,0:T(8,128)} %own.1), channel_id=1, source_target_pairs={{4,8},{8,4},{12,16},{16,12},{20,24},{24,20},{28,32},{32,28},{36,40... | collective-permute-start | bytes 442376 | tf_op jit(solution)/shard_map/ppermute | solution.py:298
  5.9 0.7 copy-start.4
  5.9 0.7 copy-start.3
  5.9 0.7 copy-start.5
  5.9 0.9 %copy-start.1 = (f32[12,16,192]{2,1,0:T(8,128)S(1)}, f32[12,16,192]{2,1,0:T(8,128)}, u32[]{:S(2)}) copy-start(f32[12,16,192]{2,1,0:T(8,128)} %loads.1) | copy-start | bytes 442372
  5.9 1.0 %copy-start.2 = (f32[12,16,192]{2,1,0:T(8,128)S(1)}, f32[12,16,192]{2,1,0:T(8,128)}, u32[]{:S(2)}) copy-start(f32[12,16,192]{2,1,0:T(8,128)} %own.1) | copy-start | bytes 442372
  37.0 15.2 %all-to-all-start.1 = ((bf16[64,8,128]{2,1,0:T(8,128)(2,1)}), bf16[64,8,128]{2,1,0:T(8,128)(2,1)S(1)}, u32[]{:S(2)}, u32[]{:S(2)}) async-start(bf16[64,8,128]{2,1,0:T(8,128)(2,1)} %bitcast.7), calls=%async_computation.1 | async-start | bytes 262144 | tf_op jit(solution)/shard_map/all_to_all | solution.py:330
  41.9 10.4 %copy-start = (bf16[8,36864]{1,0:T(8,128)(2,1)S(1)}, bf16[8,36864]{1,0:T(8,128)(2,1)}, u32[]{:S(2)}) copy-start(bf16[8,36864]{1,0:T(8,128)(2,1)} %param.13) | copy-start | bytes 1769476
  56.0 11.9 %all-to-all-start.2 = ((bf16[8,96,256]{2,1,0:T(8,128)(2,1)}), bf16[8,96,256]{2,1,0:T(8,128)(2,1)S(1)}, u32[]{:S(2)}, u32[]{:S(2)}) async-start(bf16[8,96,256]{2,1,0:T(8,128)(2,1)} %bitcast.18), calls=%async_computation.2 | async-start | bytes 786432 | tf_op jit(solution)/shard_map/all_to_all | solution.py:356
  59.7 2.4 %collective-permute-start.2 = (f32[1,128]{1,0:T(1,128)S(1)}, f32[1,128]{1,0:T(1,128)S(1)}, u32[]{:S(2)}, u32[]{:S(2)}) collective-permute-start(f32[1,128]{1,0:T(1,128)S(1)} %get-tuple-element.25), channel_id=1, source_target_pairs={{0,1},{1,0},{2,3},{3,2},{4,5},{5,4},{6,7},{7,6},{8,9},{9,8},{10,11... | collective-permute-start | bytes 1544 | tf_op jit(solution)/shard_map/ppermute | solution.py:333
  69.3 16.0 %all-to-all-start.3 = ((bf16[64,4,384]{2,1,0:T(4,128)(2,1)}), bf16[64,4,384]{2,1,0:T(4,128)(2,1)S(1)}, u32[]{:S(2)}, u32[]{:S(2)}) async-start(bf16[64,4,384]{2,1,0:T(4,128)(2,1)} %get-tuple-element.26), calls=%async_computation.3 | async-start | bytes 393216 | tf_op jit(solution)/shard_map/all_to_all | solution.py:367
  74.4 4.0 %collective-permute-start.3 = (f32[1,128]{1,0:T(1,128)S(1)}, f32[1,128]{1,0:T(1,128)S(1)}, u32[]{:S(2)}, u32[]{:S(2)}) collective-permute-start(f32[1,128]{1,0:T(1,128)S(1)} %get-tuple-element.28), channel_id=1, source_target_pairs={{0,2},{1,3},{2,0},{3,1},{4,6},{5,7},{6,4},{7,5},{8,10},{9,11},{10,... | collective-permute-start | bytes 1544 | tf_op jit(solution)/shard_map/ppermute | solution.py:333

commit v7 on v6

--- a/solution.py
+++ b/solution.py
@@ -122,25 +122,41 @@
             tile = jnp.concatenate(ones[8 * t:8 * t + 8], axis=1)
             squares = squares + tile * tile
             for k in range(3):
-                message[pl.ds(par * 256 + 2 * k + t, 32, stride=ROWS), :] = tile[k * 32:(k + 1) * 32]
+                message[k, pl.ds(par * 64 + t, 32, stride=2), :] = tile[k * 32:(k + 1) * 32]
     whole = jnp.sum(squares).reshape(1, 1)
     first = whole.astype(BF16).astype(F32)
     second = (whole - first).astype(BF16).astype(F32)
     third = whole - first - second
     lane = iota((DOM, LANES), 1)
-    message[pl.ds(6, DOM, stride=ROWS), :] = jnp.broadcast_to(info[...], (DOM, LANES))
-    message[pl.ds(7, DOM, stride=ROWS), :] = jnp.where(
-        lane == 0, first, jnp.where(lane == 1, second, jnp.where(lane == 2, third, 0.0)))
-    out[...] = message[...].astype(BF16)
+    notes = jnp.broadcast_to(info[...], (DOM, LANES))
+    parts = jnp.where(lane == 64, first, jnp.where(lane == 65, second, jnp.where(lane == 66, third, 0.0)))
+    for k, extra in enumerate((pltpu.roll(notes, 64, 1), notes, parts)):
+        at = pl.ds(1, DOM, stride=2)
+        message[k, at, :] = jnp.where(lane < 64, message[k, at, :], extra)
+    out[...] = packed(message)
+
+
+def packed(message):
+    whole = jnp.concatenate([message[k] for k in range(3)], axis=1)
+    return whole.reshape(DOM, 2, 384).astype(BF16)
+
+
+def unpacked(received, wide):
+    whole = received[...].astype(F32).reshape(2 * DOM, 384)
+    for k in range(3):
+        wide[k] = whole[:, k * LANES:(k + 1) * LANES]
 
 
 def permute_kernel(received, out, notes, squares, wide, message):
-    wide[...] = received[...].astype(F32)
-    info = wide[pl.ds(6, DOM, stride=ROWS), :]
-    notes[...] = info
-    squares[...] = jnp.broadcast_to(jnp.sum(wide[pl.ds(7, DOM, stride=ROWS), :]).reshape(1, 1), (1, LANES))
+    unpacked(received, wide)
+    odd = pl.ds(1, DOM, stride=2)
+    info = wide[1, odd, :]
+    notes[...] = pltpu.roll(wide[0, odd, :], 64, 1)
+    upper = iota((DOM, LANES), 1) >= 64
+    squares[...] = jnp.broadcast_to(
+        jnp.sum(jnp.where(upper, wide[2, odd, :], 0.0)).reshape(1, 1), (1, LANES))
     rows = jnp.concatenate(
-        [wide[pl.ds(s, DOM, stride=ROWS), :].astype(BF16) for s in range(6)], axis=1)
+        [wide[k, pl.ds(t, DOM, stride=2), :].astype(BF16) for k in range(3) for t in range(2)], axis=1)
     lane = iota((DOM, LANES), 1)
     source = iota((DOM, DOM), 1).astype(F32)
     place = (iota((DOM, 256), 1) // CASES).astype(F32)
@@ -162,10 +178,8 @@
             for i in range(count):
                 at = (LEAF * t + i) * DOM
                 moved = jnp.where(lane // CASES == i, copies[at:at + DOM], moved)
-            message[pl.ds(2 * k + t, DOM, stride=ROWS), :] = moved
-    for s in (6, 7):
-        message[pl.ds(s, DOM, stride=ROWS), :] = jnp.zeros((DOM, LANES), F32)
-    out[...] = message[...].astype(BF16)
+            message[k, pl.ds(t, DOM, stride=2), :] = moved
+    out[...] = packed(message)
 
 
 def fetch_kernel(notes, tiles, out, sems):
@@ -184,12 +198,12 @@
                                     sems.at[k - LEAF // 2]) for k in range(LEAF // 2, LEAF)]
     for copy in copies:
         copy.start()
-    wide[...] = received[...].astype(F32)
+    unpacked(received, wide)
     for k in range(3):
         for par in range(2):
             at = pl.ds(2 * k + par, 32, stride=6)
-            leaf[at, :] = wide[pl.ds(par * 256 + 2 * k, 32, stride=ROWS), :]
-            rest[at, :] = wide[pl.ds(par * 256 + 2 * k + 1, 32, stride=ROWS), :]
+            leaf[at, :] = wide[k, pl.ds(par * 64, 32, stride=2), :]
+            rest[at, :] = wide[k, pl.ds(par * 64 + 1, 32, stride=2), :]
 
     def doubled(x):
         zeros = jnp.zeros_like(x)
@@ -320,22 +334,21 @@
         pl.CostEstimate(flops=10**9, bytes_accessed=14 * 10**6, transcendentals=0),
     )(table, natural, chip, solution, loads, lanes)
     (message,) = call(
-        residual_kernel, "residual", [((DOM * ROWS, LANES), BF16)],
+        residual_kernel, "residual", [((DOM, 2, 384), BF16)],
         [smem] + [vmem] * 6,
-        [pltpu.VMEM((3 * P_SIZE, 64, 384), BF16), pltpu.VMEM((DOM * ROWS, LANES), F32)], 16,
+        [pltpu.VMEM((3 * P_SIZE, 64, 384), BF16), pltpu.VMEM((3, 2 * DOM, LANES), F32)], 16,
     )(table, high, low, cells, start, info, far)
 
     def exchange(x):
-        x = x.reshape(DOM, ROWS, LANES)
-        return lax.all_to_all(x, "dom", 0, 0, tiled=True).reshape(DOM * ROWS, LANES)
+        return lax.all_to_all(x, "dom", 0, 0, tiled=True)
 
     def across(x, step):
         return x + lax.ppermute(x, "rhs", [(i, i ^ step) for i in range(4)])
 
     message, notes, squares = call(
         permute_kernel, "permute",
-        [((DOM * ROWS, LANES), BF16), ((DOM, LANES), F32), ((1, LANES), F32)], [vmem],
-        [pltpu.VMEM((DOM * ROWS, LANES), F32), pltpu.VMEM((DOM * ROWS, LANES), F32)], 16,
+        [((DOM, 2, 384), BF16), ((DOM, LANES), F32), ((1, LANES), F32)], [vmem],
+        [pltpu.VMEM((3, 2 * DOM, LANES), F32), pltpu.VMEM((3, 2 * DOM, LANES), F32)], 16,
         pl.CostEstimate(flops=4 * 10**9, bytes_accessed=10**6, transcendentals=0),
     )(exchange(message))
 
@@ -347,7 +360,7 @@
         update_kernel, "update",
         [((LEAF * CASES, B), BF16), ((ANC * CASES, B), F32), ((PAIRS * UPD, 256), BF16)],
         [vmem, vmem, hbm, vmem],
-        [pltpu.VMEM((DOM * ROWS, LANES), F32), pltpu.VMEM((B, LANES), F32), pltpu.VMEM((B, LANES), F32),
+        [pltpu.VMEM((3, 2 * DOM, LANES), F32), pltpu.VMEM((B, LANES), F32), pltpu.VMEM((B, LANES), F32),
          pltpu.VMEM((LEAF * 384, 256), BF16), pltpu.VMEM(half, BF16),
          dma((LEAF // 2,)), pltpu.VMEM((PAIRS * UPD, 256), F32)], 48,
     )(exchange(message), natural_inverses, natural_tiles, early)

time: 88.2 us -> 87.6 us (level)
  no operation moved by 1% of the time
where the time goes in v7:
time: 87.6 us; the launch traced here: 87.2 us
  waiting for transfers between devices  23.2 us (26%)
  starting transfers between devices  22.6 us (26%)
  blocking collectives  20.7 us (24%)
  Pallas kernels  17.5 us (20%)
  between operations  2.02 us (2%)
  local copies, waits for them, and re-layouts  1.2 us (1%)
    all_to_all x1, blocking collectives, exchange(): return lax.all_to_all(x, 'dom', 0, 0, tiled=True)  20.7 us
    all_to_all x1, waiting for transfers between devices, exchange(): return lax.all_to_all(x, 'dom', 0, 0, tiled=True)  8.58 us
    all_to_all x1, waiting for transfers between devices, on_device(): sums = lax.all_to_all(sums, 'dom', 0, 0, tiled=True)  6.97 us
    all_to_all x1, waiting for transfers between devices, on_device(): lax.all_to_all(message.reshape(GROUP, 96, 256), 'dom', 0, 0, axis_index_g...  5.7 us
    all_to_all x1, starting transfers between devices, on_device(): sums = lax.all_to_all(sums, 'dom', 0, 0, tiled=True)  4.91 us
    pallas_call x1, Pallas kernels, on_device(): call(split_kernel, 'split', [((P_SIZE, PAIRS, 1536), BF16), ((P_SIZE, PAI...  4.49 us
    all_to_all x1, starting transfers between devices, exchange(): return lax.all_to_all(x, 'dom', 0, 0, tiled=True)  4.44 us
    ppermute x2, starting transfers between devices, across(): return x + lax.ppermute(x, 'rhs', [(i, i ^ step) for i in range(4)])  4.29 us
  transfers between devices with their start and end apart: 7, of which 5 were waited for; matrix products, arithmetic and copies ran while one was open for 0% of the time, Pallas kernels for 7%

profile of v7, /device:TPU:1, one launch (start us, length us, event | category | flops | bytes accessed | tf_op | source)
XLA Modules:
  0.0 87.2 jit_solution(4467860037062458822)
XLA Ops:
  0.6 3.3 %collective-permute-start = (f32[12,16,192]{2,1,0:T(8,128)}, f32[12,16,192]{2,1,0:T(8,128)S(1)}, u32[]{:S(2)}, u32[]{:S(2)}) collective-permute-start(f32[12,16,192]{2,1,0:T(8,128)} %own.1), channel_id=1, source_target_pairs={{0,4},{4,0},{8,12},{12,8},{16,20},{20,16},{24,28},{28,24},{32,36},... | collective-permute-start | bytes 442376 | tf_op jit(solution)/shard_map/ppermute | solution.py:313
  4.0 1.9 %collective-permute-start.1 = (f32[12,16,192]{2,1,0:T(8,128)}, f32[12,16,192]{2,1,0:T(8,128)S(1)}, u32[]{:S(2)}, u32[]{:S(2)}) collective-permute-start(f32[12,16,192]{2,1,0:T(8,128)} %own.1), channel_id=1, source_target_pairs={{4,8},{8,4},{12,16},{16,12},{20,24},{24,20},{28,32},{32,28},{36,40... | collective-permute-start | bytes 442376 | tf_op jit(solution)/shard_map/ppermute | solution.py:312
  5.9 0.0 copy-start.4
  5.9 0.0 copy-start.3
  5.9 0.0 copy-start.5
  5.9 0.0 copy-start.1
  5.9 0.0 copy-start.2
  6.0 0.6 copy-done.4
  6.6 0.0 copy-done.3
  6.6 0.0 copy-done.5
  6.6 0.0 collective-permute-done.chip
  6.6 0.2 copy-done.1
  6.9 0.1 copy-done.2
  7.0 4.5 %split.1 = (bf16[12,96,1536]{2,1,0:T(8,128)(2,1)S(1)}, bf16[12,96,1536]{2,1,0:T(8,128)(2,1)S(1)}, bf16[24,64,384]{2,1,0:T(8,128)(2,1)S(1)}, f32[12,96,64]{2,1,0:T(8,128)S(1)}, f32[1,128]{1,0:T(1,128)S(1)}) custom-call(s32[16,128]{1,0:T(8,128)S(1)} %pad_add_fusion.table, f32[13824,128]{1,0:T(8,128)} %bitcast.35, ...), custom_call_target="tpu_custom_call" | custom-call | flops 1000000000 | bytes 14000000 | tf_op jit(solution)/shard_map/split/pallas_call | solution.py:328
  11.5 0.0 collective-permute-done.1.far
  11.5 3.3 %residual.1 = bf16[64,2,384]{2,1,0:T(2,128)(2,1)S(1)} custom-call(s32[16,128]{1,0:T(8,128)S(1)} %pad_add_fusion.table, bf16[12,96,1536]{2,1,0:T(8,128)(2,1)S(1)} %get-tuple-element.16.high, bf16[12,96,1536]{2,1,0:T(8,128)(2,1)S(1)} %get-tuple-element.17.low, bf16[24,64,384]{2,1,0:T(8,128)(2,1)S(1)} %get-tuple-element.18.near, ...), custom_call_target="tpu_custom_call" | custom-call | tf_op jit(solution)/shard_map/residual/pallas_call | solution.py:336
  14.7 20.7 %all_to_all.20.received = bf16[64,2,384]{2,1,0:T(2,128)(2,1)S(1)} all-to-all(bf16[64,2,384]{2,1,0:T(2,128)(2,1)S(1)} %residual.1), channel_id=1, replica_groups=mesh['dom'=64,'rhs'=4] {'dom'}, dimensions={0} | all-to-all | bytes 196608 | tf_op jit(solution)/shard_map/all_to_all | solution.py:343
  35.4 1.6 %permute.1 = (bf16[64,2,384]{2,1,0:T(2,128)(2,1)}, f32[64,128]{1,0:T(8,128)S(1)}, f32[1,128]{1,0:T(1,128)S(1)}) custom-call(bf16[64,2,384]{2,1,0:T(2,128)(2,1)S(1)} %all_to_all.20.received), custom_call_target="tpu_custom_call" | custom-call | flops 4000000000 | bytes 1000000 | tf_op jit(solution)/shard_map/permute/pallas_call | solution.py:348
  37.0 4.4 %all-to-all-start.1 = ((bf16[64,2,384]{2,1,0:T(2,128)(2,1)}), bf16[64,2,384]{2,1,0:T(2,128)(2,1)S(1)}, u32[]{:S(2)}, u32[]{:S(2)}) async-start(bf16[64,2,384]{2,1,0:T(2,128)(2,1)} %get-tuple-element.21), calls=%async_computation.1 | async-start | bytes 196608 | tf_op jit(solution)/shard_map/all_to_all | solution.py:343
  41.4 0.0 copy-start
  41.4 1.7 %fetch.1.early = bf16[384,3,8,128]{3,2,1,0:T(8,128)(2,1)S(1)} custom-call(f32[64,128]{1,0:T(8,128)S(1)} %get-tuple-element.22.notes, bf16[768,3,8,128]{3,2,1,0:T(8,128)(2,1)} %bitcast.36), custom_call_target="tpu_custom_call" | custom-call | flops 2000000000 | bytes 1000000 | tf_op jit(solution)/shard_map/fetch/pallas_call | solution.py:356
  43.1 8.6 %all-to-all-done.1.received = bf16[64,2,384]{2,1,0:T(2,128)(2,1)S(1)} async-done(((bf16[64,2,384]{2,1,0:T(2,128)(2,1)}), bf16[64,2,384]{2,1,0:T(2,128)(2,1)S(1)}, u32[]{:S(2)}, u32[]{:S(2)}) %all-to-all-start.1) | async-done | bytes 98336 | tf_op jit(solution)/shard_map/all_to_all | solution.py:343
  51.7 0.0 copy-done
  51.7 3.7 %update.1 = (bf16[128,192]{1,0:T(8,128)(2,1)}, f32[64,192]{1,0:T(8,128)S(1)}, bf16[768,256]{1,0:T(8,128)(2,1)}) custom-call(bf16[64,2,384]{2,1,0:T(2,128)(2,1)S(1)} %all-to-all-done.1.received, bf16[96,3,8,128]{3,2,1,0:T(8,128)(2,1)S(1)} %bitcast.33, bf16[768,3,8,128]{3,2,1,0:T(8,128)(2,1)} %bitcast.37, bf16[384,3,8,128]{3,2,1,0:T(8,128)(2,1)S(1)} %fetch.1.early), custom_call_target="tpu_custom_call" | custom-call | tf_op jit(solution)/shard_map/update/pallas_call | solution.py:359
  55.5 3.8 %all-to-all-start.2 = ((bf16[8,96,256]{2,1,0:T(8,128)(2,1)}), bf16[8,96,256]{2,1,0:T(8,128)(2,1)S(1)}, u32[]{:S(2)}, u32[]{:S(2)}) async-start(bf16[8,96,256]{2,1,0:T(8,128)(2,1)} %bitcast.14), calls=%async_computation.2 | async-start | bytes 786432 | tf_op jit(solution)/shard_map/all_to_all | solution.py:369
  59.2 1.3 %collective-permute-start.2 = (f32[1,128]{1,0:T(1,128)S(1)}, f32[1,128]{1,0:T(1,128)S(1)}, u32[]{:S(2)}, u32[]{:S(2)}) collective-permute-start(f32[1,128]{1,0:T(1,128)S(1)} %get-tuple-element.25), channel_id=1, source_target_pairs={{0,1},{1,0},{2,3},{3,2},{4,5},{5,4},{6,7},{7,6},{8,9},{9,8},{10,11... | collective-permute-start | bytes 1544 | tf_op jit(solution)/shard_map/ppermute | solution.py:346
  60.5 0.1 reshape.66
  60.6 0.1 reshape.67.targets
  60.7 0.9 %collective-permute-done.2 = f32[1,128]{1,0:T(1,128)S(1)} collective-permute-done((f32[1,128]{1,0:T(1,128)S(1)}, f32[1,128]{1,0:T(1,128)S(1)}, u32[]{:S(2)}, u32[]{:S(2)}) %collective-permute-start.2) | collective-permute-done | bytes 544 | tf_op jit(solution)/shard_map/ppermute | solution.py:346
  61.6 5.7 %all-to-all-done.2.received = bf16[8,96,256]{2,1,0:T(8,128)(2,1)S(1)} async-done(((bf16[8,96,256]{2,1,0:T(8,128)(2,1)}), bf16[8,96,256]{2,1,0:T(8,128)(2,1)S(1)}, u32[]{:S(2)}, u32[]{:S(2)}) %all-to-all-start.2) | async-done | bytes 393248 | tf_op jit(solution)/shard_map/all_to_all | solution.py:369
  67.3 1.5 %sum.1 = (bf16[64,4,384]{2,1,0:T(4,128)(2,1)}, f32[1,128]{1,0:T(1,128)S(1)}) custom-call(bf16[8,96,256]{2,1,0:T(8,128)(2,1)S(1)} %all-to-all-done.2.received, f32[1,512]{1,0:T(1,128)S(1)} %reshape.67.targets, f32[1,128]{1,0:T(1,128)S(1)} %add.32.squares), custom_call_target="tpu_custom_call" | custom-call | tf_op jit(solution)/shard_map/sum/pallas_call | solution.py:375
  68.8 4.9 %all-to-all-start.3 = ((bf16[64,4,384]{2,1,0:T(4,128)(2,1)}), bf16[64,4,384]{2,1,0:T(4,128)(2,1)S(1)}, u32[]{:S(2)}, u32[]{:S(2)}) async-start(bf16[64,4,384]{2,1,0:T(4,128)(2,1)} %get-tuple-element.26), calls=%async_computation.3 | async-start | bytes 393216 | tf_op jit(solution)/shard_map/all_to_all | solution.py:380
  73.8 3.0 %collective-permute-start.3 = (f32[1,128]{1,0:T(1,128)S(1)}, f32[1,128]{1,0:T(1,128)S(1)}, u32[]{:S(2)}, u32[]{:S(2)}) collective-permute-start(f32[1,128]{1,0:T(1,128)S(1)} %get-tuple-element.28), channel_id=1, source_target_pairs={{0,2},{1,3},{2,0},{3,1},{4,6},{5,7},{6,4},{7,5},{8,10},{9,11},{10,... | collective-permute-start | bytes 1544 | tf_op jit(solution)/shard_map/ppermute | solution.py:346
  76.8 1.0 %collective-permute-done.3 = f32[1,128]{1,0:T(1,128)S(1)} collective-permute-done((f32[1,128]{1,0:T(1,128)S(1)}, f32[1,128]{1,0:T(1,128)S(1)}, u32[]{:S(2)}, u32[]{:S(2)}) %collective-permute-start.3) | collective-permute-done | bytes 544 | tf_op jit(solution)/shard_map/ppermute | solution.py:346
  77.8 7.0 %all-to-all-done.3 = bf16[64,4,384]{2,1,0:T(4,128)(2,1)S(1)} async-done(((bf16[64,4,384]{2,1,0:T(4,128)(2,1)}), bf16[64,4,384]{2,1,0:T(4,128)(2,1)S(1)}, u32[]{:S(2)}, u32[]{:S(2)}) %all-to-all-start.3) | async-done | bytes 196640 | tf_op jit(solution)/shard_map/all_to_all | solution.py:380
  84.8 0.1 reshape.68.received
  84.9 1.2 %final.1 = f32[64,192]{1,0:T(8,128)} custom-call(bf16[256,384]{1,0:T(8,128)(2,1)S(1)} %reshape.68.received, f32[64,192]{1,0:T(8,128)S(1)} %get-tuple-element.27.ancestors), custom_call_target="tpu_custom_call" | custom-call | tf_op jit(solution)/shard_map/final/pallas_call | solution.py:381
  (7 shorter events, 0.0 us)
Async XLA Ops:
  0.6 6.0 %collective-permute-start = (f32[12,16,192]{2,1,0:T(8,128)}, f32[12,16,192]{2,1,0:T(8,128)S(1)}, u32[]{:S(2)}, u32[]{:S(2)}) collective-permute-start(f32[12,16,192]{2,1,0:T(8,128)} %own.1), channel_id=1, source_target_pairs={{0,4},{4,0},{8,12},{12,8},{16,20},{20,16},{24,28},{28,24},{32,36},... | collective-permute-start | bytes 442376 | tf_op jit(solution)/shard_map/ppermute | solution.py:313
  4.0 7.5 %collective-permute-start.1 = (f32[12,16,192]{2,1,0:T(8,128)}, f32[12,16,192]{2,1,0:T(8,128)S(1)}, u32[]{:S(2)}, u32[]{:S(2)}) collective-permute-start(f32[12,16,192]{2,1,0:T(8,128)} %own.1), channel_id=1, source_target_pairs={{4,8},{8,4},{12,16},{16,12},{20,24},{24,20},{28,32},{32,28},{36,40... | collective-permute-start | bytes 442376 | tf_op jit(solution)/shard_map/ppermute | solution.py:312
  5.9 0.7 copy-start.4
  5.9 0.7 copy-start.3
  5.9 0.7 copy-start.5
  5.9 0.9 %copy-start.1 = (f32[12,16,192]{2,1,0:T(8,128)S(1)}, f32[12,16,192]{2,1,0:T(8,128)}, u32[]{:S(2)}) copy-start(f32[12,16,192]{2,1,0:T(8,128)} %loads.1) | copy-start | bytes 442372
  5.9 1.0 %copy-start.2 = (f32[12,16,192]{2,1,0:T(8,128)S(1)}, f32[12,16,192]{2,1,0:T(8,128)}, u32[]{:S(2)}) copy-start(f32[12,16,192]{2,1,0:T(8,128)} %own.1) | copy-start | bytes 442372
  37.0 14.7 %all-to-all-start.1 = ((bf16[64,2,384]{2,1,0:T(2,128)(2,1)}), bf16[64,2,384]{2,1,0:T(2,128)(2,1)S(1)}, u32[]{:S(2)}, u32[]{:S(2)}) async-start(bf16[64,2,384]{2,1,0:T(2,128)(2,1)} %get-tuple-element.21), calls=%async_computation.1 | async-start | bytes 196608 | tf_op jit(solution)/shard_map/all_to_all | solution.py:343
  41.4 10.3 %copy-start = (bf16[8,36864]{1,0:T(8,128)(2,1)S(1)}, bf16[8,36864]{1,0:T(8,128)(2,1)}, u32[]{:S(2)}) copy-start(bf16[8,36864]{1,0:T(8,128)(2,1)} %param.13) | copy-start | bytes 1769476
  55.5 11.9 %all-to-all-start.2 = ((bf16[8,96,256]{2,1,0:T(8,128)(2,1)}), bf16[8,96,256]{2,1,0:T(8,128)(2,1)S(1)}, u32[]{:S(2)}, u32[]{:S(2)}) async-start(bf16[8,96,256]{2,1,0:T(8,128)(2,1)} %bitcast.14), calls=%async_computation.2 | async-start | bytes 786432 | tf_op jit(solution)/shard_map/all_to_all | solution.py:369
  59.2 2.4 %collective-permute-start.2 = (f32[1,128]{1,0:T(1,128)S(1)}, f32[1,128]{1,0:T(1,128)S(1)}, u32[]{:S(2)}, u32[]{:S(2)}) collective-permute-start(f32[1,128]{1,0:T(1,128)S(1)} %get-tuple-element.25), channel_id=1, source_target_pairs={{0,1},{1,0},{2,3},{3,2},{4,5},{5,4},{6,7},{7,6},{8,9},{9,8},{10,11... | collective-permute-start | bytes 1544 | tf_op jit(solution)/shard_map/ppermute | solution.py:346
  68.8 16.0 %all-to-all-start.3 = ((bf16[64,4,384]{2,1,0:T(4,128)(2,1)}), bf16[64,4,384]{2,1,0:T(4,128)(2,1)S(1)}, u32[]{:S(2)}, u32[]{:S(2)}) async-start(bf16[64,4,384]{2,1,0:T(4,128)(2,1)} %get-tuple-element.26), calls=%async_computation.3 | async-start | bytes 393216 | tf_op jit(solution)/shard_map/all_to_all | solution.py:380
  73.8 4.0 %collective-permute-start.3 = (f32[1,128]{1,0:T(1,128)S(1)}, f32[1,128]{1,0:T(1,128)S(1)}, u32[]{:S(2)}, u32[]{:S(2)}) collective-permute-start(f32[1,128]{1,0:T(1,128)S(1)} %get-tuple-element.28), channel_id=1, source_target_pairs={{0,2},{1,3},{2,0},{3,1},{4,6},{5,7},{6,4},{7,5},{8,10},{9,11},{10,... | collective-permute-start | bytes 1544 | tf_op jit(solution)/shard_map/ppermute | solution.py:346

commit v8 on v7

--- a/solution.py
+++ b/solution.py
@@ -182,17 +182,28 @@
     out[...] = packed(message)
 
 
-def fetch_kernel(notes, tiles, out, sems):
-    step = PAIRS * LEAF // 8
-    copies = [pltpu.make_async_copy(tiles.at[pl.ds(n * step, step)], out.at[pl.ds(n * step, step)], sems.at[n])
-              for n in range(LEAF // 2)]
+def left(ref, start, count):
+    return jnp.concatenate(
+        [ref[pl.ds(start, count), t].reshape(count * 8, LANES) for t in range(3)], axis=1)
+
+
+def fetch_kernel(notes, inverses, tiles, out, ready, gather, near, sems):
+    copies = [pltpu.make_async_copy(tiles.at[pl.ds(n * PAIRS, PAIRS)], near.at[pl.ds(n * PAIRS, PAIRS)],
+                                    sems.at[n]) for n in range(LEAF // 2)]
     for copy in copies:
         copy.start()
-    for copy in copies:
+    ready[...] = left(inverses, 0, PAIRS)
+    gather[...] = one_hot(iota((B, 768), 1) // 8 == iota((B, 768), 0) // 2)
+    for n, copy in enumerate(copies):
         copy.wait()
-
-
-def update_kernel(received, inverses, tiles, early, level, ancestors, out,
+        out[:, n * 384:(n + 1) * 384] = left(near, n * PAIRS, PAIRS)
+
+
+def select_kernel(targets, out):
+    out[...] = one_hot(targets[...] == iota((256, 512), 0).astype(F32))
+
+
+def update_kernel(received, ready, gather, tiles, early, level, ancestors, out,
                   wide, leaf, rest, right, near, sems, partial):
     copies = [pltpu.make_async_copy(tiles.at[pl.ds(k * PAIRS, PAIRS)], near.at[pl.ds((k - LEAF // 2) * PAIRS, PAIRS)],
                                     sems.at[k - LEAF // 2]) for k in range(LEAF // 2, LEAF)]
@@ -210,15 +221,10 @@
         return jnp.concatenate(
             [jnp.concatenate([x, zeros], axis=1), jnp.concatenate([zeros, x], axis=1)], axis=0)
 
-    def left(ref, start, count):
-        return jnp.concatenate(
-            [ref[pl.ds(start, count), t].reshape(count * 8, LANES) for t in range(3)], axis=1)
-
-    solved = dot(left(inverses, 0, PAIRS), doubled(leaf[...].astype(BF16)))
+    solved = dot(ready[...], doubled(leaf[...].astype(BF16)))
     own = iota((768, 256), 0) % 8 == (iota((768, 256), 1) % LANES) // 16
     solved = jnp.where(own, solved, 0.0).astype(BF16)
-    gather = one_hot(iota((B, 768), 1) // 8 == iota((B, 768), 0) // 2)
-    solved = dot(gather, solved)
+    solved = dot(gather[...], solved)
     solved = jnp.where(iota((B, LANES), 0) % 2 == 0, solved[:, :LANES], solved[:, LANES:])
     unit = one_hot(iota((LANES, LANES), 0) == iota((LANES, LANES), 1))
     level[...] = lax.dot_general(unit, solved.astype(BF16), NT, preferred_element_type=F32).astype(BF16)
@@ -234,8 +240,10 @@
                 copy.wait()
         for r in range(0, PAIRS, band):
             at = slice(r * 8, (r + band) * 8)
-            wide_left = jnp.concatenate(
-                [left(near if first else early, k * PAIRS + r, band) for k in range(step)], axis=1)
+            if first:
+                wide_left = jnp.concatenate([left(near, k * PAIRS + r, band) for k in range(step)], axis=1)
+            else:
+                wide_left = early[at]
             total = dot(wide_left, right[first * 384:(first + step) * 384])
             if first == 0:
                 partial[at] = total
@@ -243,9 +251,8 @@
                 out[at] = (partial[at] + total).astype(BF16)
 
 
-def sum_kernel(received, targets, squares, out, squares_out, right):
+def sum_kernel(received, select, squares, out, squares_out, right):
     squares_out[...] = squares[...]
-    select = one_hot(targets[...] == iota((256, 512), 0).astype(F32))
     group = iota((64, LANES), 1) // CASES
     for tile in range(3):
         parts = []
@@ -264,7 +271,7 @@
             parts = turned
         for k in range(LEAF):
             right[k * 64:(k + 1) * 64, tile * LANES:(tile + 1) * LANES] = parts[k].astype(BF16)
-    out[...] = dot(select, right[...]).reshape(DOM, ANC, 384).astype(BF16)
+    out[...] = dot(select[...], right[...]).reshape(DOM, ANC, 384).astype(BF16)
 
 
 def final_kernel(received, ancestors, out):
@@ -353,17 +360,20 @@
     )(exchange(message))
 
     half = (LEAF // 2 * PAIRS, 3, UPD, LANES)
-    (early,) = call(fetch_kernel, "fetch", [(half, BF16)], [vmem, hbm], [dma((LEAF // 2,))], 50,
-                    pl.CostEstimate(flops=2 * 10**9, bytes_accessed=10**6, transcendentals=0),
-                    )(notes, natural_tiles)
+    early, ready, gather = call(
+        fetch_kernel, "fetch",
+        [((PAIRS * UPD, LEAF // 2 * 384), BF16), ((PAIRS * LEAF, 384), BF16), ((B, PAIRS * LEAF), BF16)],
+        [vmem, vmem, hbm], [pltpu.VMEM(half, BF16), dma((LEAF // 2,))], 50,
+        pl.CostEstimate(flops=2 * 10**9, bytes_accessed=10**6, transcendentals=0),
+    )(notes, natural_inverses, natural_tiles)
     level, ancestors, message = call(
         update_kernel, "update",
         [((LEAF * CASES, B), BF16), ((ANC * CASES, B), F32), ((PAIRS * UPD, 256), BF16)],
-        [vmem, vmem, hbm, vmem],
+        [vmem, vmem, vmem, hbm, vmem],
         [pltpu.VMEM((3, 2 * DOM, LANES), F32), pltpu.VMEM((B, LANES), F32), pltpu.VMEM((B, LANES), F32),
          pltpu.VMEM((LEAF * 384, 256), BF16), pltpu.VMEM(half, BF16),
          dma((LEAF // 2,)), pltpu.VMEM((PAIRS * UPD, 256), F32)], 48,
-    )(exchange(message), natural_inverses, natural_tiles, early)
+    )(exchange(message), ready, gather, natural_tiles, early)
 
     groups = [[(x * N_Z + z) * N_CORE + c for x in range(N_X) for c in range(N_CORE)] for z in range(N_Z)]
     received = lax.all_to_all(
@@ -372,10 +382,12 @@
     near = lax.dynamic_index_in_dim(notes.reshape(N_X, N_Z, N_CORE, LANES), z, axis=1, keepdims=False)
     near = near.reshape(GROUP, LANES)[:, :LEAF * UPD].reshape(GROUP, LEAF, UPD)
     near = near.transpose(1, 0, 2).reshape(1, LEAF * GROUP * UPD)
+    (select,) = call(select_kernel, "select", [((256, 512), BF16)], [vmem], [], 16,
+                     pl.CostEstimate(flops=10**9, bytes_accessed=10**6, transcendentals=0))(near)
     sums, squares = call(
         sum_kernel, "sum", [((DOM, ANC, 384), BF16), ((1, LANES), F32)], [vmem] * 3,
         [pltpu.VMEM((512, 384), BF16)],
-    )(received, near, across(squares, 1))
+    )(received, select, across(squares, 1))
     residual_rms = jnp.sqrt(across(squares, 2)[0, 0] / (DOM * P_SIZE * CASES * 4 * B))
     sums = lax.all_to_all(sums, "dom", 0, 0, tiled=True)
     (ancestor_rhs,) = call(final_kernel, "final", [((ANC * CASES, B), F32)], [vmem] * 2, [])(

time: 87.6 us -> 87.4 us (level)
  waiting for transfers between devices: 23.2 us -> 22 us
  local copies, waits for them, and re-layouts: 1.2 us -> 2.25 us
    all_to_all x1, waiting for transfers between devices: 8.58 us -> 7.47 us  [exchange(): return lax.all_to_all(x, 'dom', 0, 0, tiled=True)]
    unnamed x12, local copies, waits for them, and re-layouts: 0.98 us -> 2.03 us
where the time goes in v8:
time: 87.4 us; the launch traced here: 86.9 us
  starting transfers between devices  22.6 us (26%)
  waiting for transfers between devices  22 us (25%)
  blocking collectives  20.7 us (24%)
  Pallas kernels  17.3 us (20%)
  local copies, waits for them, and re-layouts  2.25 us (3%)
  between operations  2.03 us (2%)
    all_to_all x1, blocking collectives, exchange(): return lax.all_to_all(x, 'dom', 0, 0, tiled=True)  20.7 us
    all_to_all x1, waiting for transfers between devices, exchange(): return lax.all_to_all(x, 'dom', 0, 0, tiled=True)  7.47 us
    all_to_all x1, waiting for transfers between devices, on_device(): sums = lax.all_to_all(sums, 'dom', 0, 0, tiled=True)  6.97 us
    all_to_all x1, waiting for transfers between devices, on_device(): lax.all_to_all(message.reshape(GROUP, 96, 256), 'dom', 0, 0, axis_index_g...  5.7 us
    all_to_all x1, starting transfers between devices, on_device(): sums = lax.all_to_all(sums, 'dom', 0, 0, tiled=True)  4.92 us
    pallas_call x1, Pallas kernels, on_device(): call(split_kernel, 'split', [((P_SIZE, PAIRS, 1536), BF16), ((P_SIZE, PAI...  4.49 us
    all_to_all x1, starting transfers between devices, exchange(): return lax.all_to_all(x, 'dom', 0, 0, tiled=True)  4.44 us
    ppermute x2, starting transfers between devices, across(): return x + lax.ppermute(x, 'rhs', [(i, i ^ step) for i in range(4)])  4.28 us
  transfers between devices with their start and end apart: 7, of which 5 were waited for; matrix products, arithmetic and copies ran while one was open for 0% of the time, Pallas kernels for 7%

profile of v8, /device:TPU:1, one launch (start us, length us, event | category | flops | bytes accessed | tf_op | source)
XLA Modules:
  0.0 86.9 jit_solution(17066862593543338450)
XLA Ops:
  0.6 3.3 %collective-permute-start = (f32[12,16,192]{2,1,0:T(8,128)}, f32[12,16,192]{2,1,0:T(8,128)S(1)}, u32[]{:S(2)}, u32[]{:S(2)}) collective-permute-start(f32[12,16,192]{2,1,0:T(8,128)} %own.1), channel_id=1, source_target_pairs={{0,4},{4,0},{8,12},{12,8},{16,20},{20,16},{24,28},{28,24},{32,36},... | collective-permute-start | bytes 442376 | tf_op jit(solution)/shard_map/ppermute | solution.py:320
  4.0 1.9 %collective-permute-start.1 = (f32[12,16,192]{2,1,0:T(8,128)}, f32[12,16,192]{2,1,0:T(8,128)S(1)}, u32[]{:S(2)}, u32[]{:S(2)}) collective-permute-start(f32[12,16,192]{2,1,0:T(8,128)} %own.1), channel_id=1, source_target_pairs={{4,8},{8,4},{12,16},{16,12},{20,24},{24,20},{28,32},{32,28},{36,40... | collective-permute-start | bytes 442376 | tf_op jit(solution)/shard_map/ppermute | solution.py:319
  5.9 0.0 copy-start.4
  5.9 0.0 copy-start.3
  5.9 0.0 copy-start.5
  5.9 0.0 copy-start
  5.9 0.0 copy-start.1
  6.0 0.6 copy-done.4
  6.6 0.0 copy-done.3
  6.6 0.0 copy-done.5
  6.6 0.0 collective-permute-done.chip
  6.6 0.2 copy-done
  6.9 0.1 copy-done.1
  7.0 4.5 %split.1 = (bf16[12,96,1536]{2,1,0:T(8,128)(2,1)S(1)}, bf16[12,96,1536]{2,1,0:T(8,128)(2,1)S(1)}, bf16[24,64,384]{2,1,0:T(8,128)(2,1)S(1)}, f32[12,96,64]{2,1,0:T(8,128)S(1)}, f32[1,128]{1,0:T(1,128)S(1)}) custom-call(s32[16,128]{1,0:T(8,128)S(1)} %pad_add_fusion.table, f32[13824,128]{1,0:T(8,128)} %bitcast.35, ...), custom_call_target="tpu_custom_call" | custom-call | flops 1000000000 | bytes 14000000 | tf_op jit(solution)/shard_map/split/pallas_call | solution.py:335
  11.5 0.0 collective-permute-done.1.far
  11.5 3.3 %residual.1 = bf16[64,2,384]{2,1,0:T(2,128)(2,1)S(1)} custom-call(s32[16,128]{1,0:T(8,128)S(1)} %pad_add_fusion.table, bf16[12,96,1536]{2,1,0:T(8,128)(2,1)S(1)} %get-tuple-element.19.high, bf16[12,96,1536]{2,1,0:T(8,128)(2,1)S(1)} %get-tuple-element.20.low, bf16[24,64,384]{2,1,0:T(8,128)(2,1)S(1)} %get-tuple-element.21.near, ...), custom_call_target="tpu_custom_call" | custom-call | tf_op jit(solution)/shard_map/residual/pallas_call | solution.py:343
  14.7 20.7 %all_to_all.20.received = bf16[64,2,384]{2,1,0:T(2,128)(2,1)S(1)} all-to-all(bf16[64,2,384]{2,1,0:T(2,128)(2,1)S(1)} %residual.1), channel_id=1, replica_groups=mesh['dom'=64,'rhs'=4] {'dom'}, dimensions={0} | all-to-all | bytes 196608 | tf_op jit(solution)/shard_map/all_to_all | solution.py:350
  35.4 1.6 %permute.1 = (bf16[64,2,384]{2,1,0:T(2,128)(2,1)}, f32[64,128]{1,0:T(8,128)S(1)}, f32[1,128]{1,0:T(1,128)S(1)}) custom-call(bf16[64,2,384]{2,1,0:T(2,128)(2,1)S(1)} %all_to_all.20.received), custom_call_target="tpu_custom_call" | custom-call | flops 4000000000 | bytes 1000000 | tf_op jit(solution)/shard_map/permute/pallas_call | solution.py:355
  37.0 4.4 %all-to-all-start.1 = ((bf16[64,2,384]{2,1,0:T(2,128)(2,1)}), bf16[64,2,384]{2,1,0:T(2,128)(2,1)S(1)}, u32[]{:S(2)}, u32[]{:S(2)}) async-start(bf16[64,2,384]{2,1,0:T(2,128)(2,1)} %get-tuple-element.24), calls=%async_computation.1 | async-start | bytes 196608 | tf_op jit(solution)/shard_map/all_to_all | solution.py:350
  41.4 0.0 copy-start.2
  41.5 1.1 %copy-done.2 = bf16[8,36864]{1,0:T(8,128)(2,1)S(1)} copy-done((bf16[8,36864]{1,0:T(8,128)(2,1)S(1)}, bf16[8,36864]{1,0:T(8,128)(2,1)}, u32[]{:S(2)}) %copy-start.2) | copy-done | bytes 589848
  42.5 1.7 %fetch.1 = (bf16[768,1536]{1,0:T(8,128)(2,1)S(1)}, bf16[768,384]{1,0:T(8,128)(2,1)S(1)}, bf16[192,768]{1,0:T(8,128)(2,1)S(1)}) custom-call(f32[64,128]{1,0:T(8,128)S(1)} %get-tuple-element.25.notes, bf16[96,3,8,128]{3,2,1,0:T(8,128)(2,1)S(1)} %bitcast.34, bf16[768,3,8,128]{3,2,1,0:T(8,128)(2,1)} %bitcast.36), custom_call_target="tpu_custom_call" | custom-call | flops 2000000000 | bytes 1000000 | tf_op jit(solution)/shard_map/fetch/pallas_call | solution.py:363
  44.2 7.5 %all-to-all-done.1.received = bf16[64,2,384]{2,1,0:T(2,128)(2,1)S(1)} async-done(((bf16[64,2,384]{2,1,0:T(2,128)(2,1)}), bf16[64,2,384]{2,1,0:T(2,128)(2,1)S(1)}, u32[]{:S(2)}, u32[]{:S(2)}) %all-to-all-start.1) | async-done | bytes 98336 | tf_op jit(solution)/shard_map/all_to_all | solution.py:350
  51.7 3.5 %update.1 = (bf16[128,192]{1,0:T(8,128)(2,1)}, f32[64,192]{1,0:T(8,128)S(1)}, bf16[768,256]{1,0:T(8,128)(2,1)}) custom-call(bf16[64,2,384]{2,1,0:T(2,128)(2,1)S(1)} %all-to-all-done.1.received, bf16[768,384]{1,0:T(8,128)(2,1)S(1)} %get-tuple-element.26.ready, bf16[192,768]{1,0:T(8,128)(2,1)S(1)} %get-tuple-element.27.gather, ...), custom_call_target="tpu_custom_call" | custom-call | tf_op jit(solution)/shard_map/update/pallas_call | solution.py:369
  55.2 3.8 %all-to-all-start.2 = ((bf16[8,96,256]{2,1,0:T(8,128)(2,1)}), bf16[8,96,256]{2,1,0:T(8,128)(2,1)S(1)}, u32[]{:S(2)}, u32[]{:S(2)}) async-start(bf16[8,96,256]{2,1,0:T(8,128)(2,1)} %bitcast.12), calls=%async_computation.2 | async-start | bytes 786432 | tf_op jit(solution)/shard_map/all_to_all | solution.py:379
  58.9 1.3 %collective-permute-start.2 = (f32[1,128]{1,0:T(1,128)S(1)}, f32[1,128]{1,0:T(1,128)S(1)}, u32[]{:S(2)}, u32[]{:S(2)}) collective-permute-start(f32[1,128]{1,0:T(1,128)S(1)} %get-tuple-element.31), channel_id=1, source_target_pairs={{0,1},{1,0},{2,3},{3,2},{4,5},{5,4},{6,7},{7,6},{8,9},{9,8},{10,11... | collective-permute-start | bytes 1544 | tf_op jit(solution)/shard_map/ppermute | solution.py:353
  60.2 0.1 reshape.66
  60.3 0.1 reshape.67.targets
  60.4 0.1 select.12
  60.5 0.8 collective-permute-done.2
  61.3 5.7 %all-to-all-done.2.received = bf16[8,96,256]{2,1,0:T(8,128)(2,1)S(1)} async-done(((bf16[8,96,256]{2,1,0:T(8,128)(2,1)}), bf16[8,96,256]{2,1,0:T(8,128)(2,1)S(1)}, u32[]{:S(2)}, u32[]{:S(2)}) %all-to-all-start.2) | async-done | bytes 393248 | tf_op jit(solution)/shard_map/all_to_all | solution.py:379
  67.0 1.5 %sum.1 = (bf16[64,4,384]{2,1,0:T(4,128)(2,1)}, f32[1,128]{1,0:T(1,128)S(1)}) custom-call(bf16[8,96,256]{2,1,0:T(8,128)(2,1)S(1)} %all-to-all-done.2.received, bf16[256,512]{1,0:T(8,128)(2,1)S(1)} %select.12, f32[1,128]{1,0:T(1,128)S(1)} %add.32.squares), custom_call_target="tpu_custom_call" | custom-call | tf_op jit(solution)/shard_map/sum/pallas_call | solution.py:387
  68.5 4.9 %all-to-all-start.3 = ((bf16[64,4,384]{2,1,0:T(4,128)(2,1)}), bf16[64,4,384]{2,1,0:T(4,128)(2,1)S(1)}, u32[]{:S(2)}, u32[]{:S(2)}) async-start(bf16[64,4,384]{2,1,0:T(4,128)(2,1)} %get-tuple-element.32), calls=%async_computation.3 | async-start | bytes 393216 | tf_op jit(solution)/shard_map/all_to_all | solution.py:392
  73.5 3.0 %collective-permute-start.3 = (f32[1,128]{1,0:T(1,128)S(1)}, f32[1,128]{1,0:T(1,128)S(1)}, u32[]{:S(2)}, u32[]{:S(2)}) collective-permute-start(f32[1,128]{1,0:T(1,128)S(1)} %get-tuple-element.34), channel_id=1, source_target_pairs={{0,2},{1,3},{2,0},{3,1},{4,6},{5,7},{6,4},{7,5},{8,10},{9,11},{10,... | collective-permute-start | bytes 1544 | tf_op jit(solution)/shard_map/ppermute | solution.py:353
  76.4 1.0 %collective-permute-done.3 = f32[1,128]{1,0:T(1,128)S(1)} collective-permute-done((f32[1,128]{1,0:T(1,128)S(1)}, f32[1,128]{1,0:T(1,128)S(1)}, u32[]{:S(2)}, u32[]{:S(2)}) %collective-permute-start.3) | collective-permute-done | bytes 544 | tf_op jit(solution)/shard_map/ppermute | solution.py:353
  77.5 7.0 %all-to-all-done.3 = bf16[64,4,384]{2,1,0:T(4,128)(2,1)S(1)} async-done(((bf16[64,4,384]{2,1,0:T(4,128)(2,1)}), bf16[64,4,384]{2,1,0:T(4,128)(2,1)S(1)}, u32[]{:S(2)}, u32[]{:S(2)}) %all-to-all-start.3) | async-done | bytes 196640 | tf_op jit(solution)/shard_map/all_to_all | solution.py:392
  84.5 0.1 reshape.68.received
  84.6 1.2 %final.1 = f32[64,192]{1,0:T(8,128)} custom-call(bf16[256,384]{1,0:T(8,128)(2,1)S(1)} %reshape.68.received, f32[64,192]{1,0:T(8,128)S(1)} %get-tuple-element.33.ancestors), custom_call_target="tpu_custom_call" | custom-call | tf_op jit(solution)/shard_map/final/pallas_call | solution.py:393
  (7 shorter events, 0.0 us)
Async XLA Ops:
  0.6 6.0 %collective-permute-start = (f32[12,16,192]{2,1,0:T(8,128)}, f32[12,16,192]{2,1,0:T(8,128)S(1)}, u32[]{:S(2)}, u32[]{:S(2)}) collective-permute-start(f32[12,16,192]{2,1,0:T(8,128)} %own.1), channel_id=1, source_target_pairs={{0,4},{4,0},{8,12},{12,8},{16,20},{20,16},{24,28},{28,24},{32,36},... | collective-permute-start | bytes 442376 | tf_op jit(solution)/shard_map/ppermute | solution.py:320
  4.0 7.5 %collective-permute-start.1 = (f32[12,16,192]{2,1,0:T(8,128)}, f32[12,16,192]{2,1,0:T(8,128)S(1)}, u32[]{:S(2)}, u32[]{:S(2)}) collective-permute-start(f32[12,16,192]{2,1,0:T(8,128)} %own.1), channel_id=1, source_target_pairs={{4,8},{8,4},{12,16},{16,12},{20,24},{24,20},{28,32},{32,28},{36,40... | collective-permute-start | bytes 442376 | tf_op jit(solution)/shard_map/ppermute | solution.py:319
  5.9 0.7 copy-start.4
  5.9 0.7 copy-start.3
  5.9 0.7 copy-start.5
  5.9 0.9 %copy-start = (f32[12,16,192]{2,1,0:T(8,128)S(1)}, f32[12,16,192]{2,1,0:T(8,128)}, u32[]{:S(2)}) copy-start(f32[12,16,192]{2,1,0:T(8,128)} %loads.1) | copy-start | bytes 442372
  5.9 1.0 %copy-start.1 = (f32[12,16,192]{2,1,0:T(8,128)S(1)}, f32[12,16,192]{2,1,0:T(8,128)}, u32[]{:S(2)}) copy-start(f32[12,16,192]{2,1,0:T(8,128)} %own.1) | copy-start | bytes 442372
  37.0 14.7 %all-to-all-start.1 = ((bf16[64,2,384]{2,1,0:T(2,128)(2,1)}), bf16[64,2,384]{2,1,0:T(2,128)(2,1)S(1)}, u32[]{:S(2)}, u32[]{:S(2)}) async-start(bf16[64,2,384]{2,1,0:T(2,128)(2,1)} %get-tuple-element.24), calls=%async_computation.1 | async-start | bytes 196608 | tf_op jit(solution)/shard_map/all_to_all | solution.py:350
  41.4 1.1 %copy-start.2 = (bf16[8,36864]{1,0:T(8,128)(2,1)S(1)}, bf16[8,36864]{1,0:T(8,128)(2,1)}, u32[]{:S(2)}) copy-start(bf16[8,36864]{1,0:T(8,128)(2,1)} %param.13) | copy-start | bytes 1769476
  55.2 11.9 %all-to-all-start.2 = ((bf16[8,96,256]{2,1,0:T(8,128)(2,1)}), bf16[8,96,256]{2,1,0:T(8,128)(2,1)S(1)}, u32[]{:S(2)}, u32[]{:S(2)}) async-start(bf16[8,96,256]{2,1,0:T(8,128)(2,1)} %bitcast.12), calls=%async_computation.2 | async-start | bytes 786432 | tf_op jit(solution)/shard_map/all_to_all | solution.py:379
  58.9 2.4 %collective-permute-start.2 = (f32[1,128]{1,0:T(1,128)S(1)}, f32[1,128]{1,0:T(1,128)S(1)}, u32[]{:S(2)}, u32[]{:S(2)}) collective-permute-start(f32[1,128]{1,0:T(1,128)S(1)} %get-tuple-element.31), channel_id=1, source_target_pairs={{0,1},{1,0},{2,3},{3,2},{4,5},{5,4},{6,7},{7,6},{8,9},{9,8},{10,11... | collective-permute-start | bytes 1544 | tf_op jit(solution)/shard_map/ppermute | solution.py:353
  68.5 16.0 %all-to-all-start.3 = ((bf16[64,4,384]{2,1,0:T(4,128)(2,1)}), bf16[64,4,384]{2,1,0:T(4,128)(2,1)S(1)}, u32[]{:S(2)}, u32[]{:S(2)}) async-start(bf16[64,4,384]{2,1,0:T(4,128)(2,1)} %get-tuple-element.32), calls=%async_computation.3 | async-start | bytes 393216 | tf_op jit(solution)/shard_map/all_to_all | solution.py:392
  73.5 4.0 %collective-permute-start.3 = (f32[1,128]{1,0:T(1,128)S(1)}, f32[1,128]{1,0:T(1,128)S(1)}, u32[]{:S(2)}, u32[]{:S(2)}) collective-permute-start(f32[1,128]{1,0:T(1,128)S(1)} %get-tuple-element.34), channel_id=1, source_target_pairs={{0,2},{1,3},{2,0},{3,1},{4,6},{5,7},{6,4},{7,5},{8,10},{9,11},{10,... | collective-permute-start | bytes 1544 | tf_op jit(solution)/shard_map/ppermute | solution.py:353

commit v9 on v8

--- a/solution.py
+++ b/solution.py
@@ -203,8 +203,15 @@
     out[...] = one_hot(targets[...] == iota((256, 512), 0).astype(F32))
 
 
-def update_kernel(received, ready, gather, tiles, early, level, ancestors, out,
-                  wide, leaf, rest, right, near, sems, partial):
+def turn_kernel(solved, rest, level, ancestors):
+    unit = one_hot(iota((LANES, LANES), 0) == iota((LANES, LANES), 1))
+    level[...] = lax.dot_general(unit, solved[...], NT, preferred_element_type=F32).astype(BF16)
+    ancestors[...] = lax.dot_general(
+        unit[:64], rest[...].astype(BF16), NT, preferred_element_type=F32)
+
+
+def update_kernel(received, ready, gather, tiles, early, level, rest, out,
+                  wide, leaf, right, near, sems, partial):
     copies = [pltpu.make_async_copy(tiles.at[pl.ds(k * PAIRS, PAIRS)], near.at[pl.ds((k - LEAF // 2) * PAIRS, PAIRS)],
                                     sems.at[k - LEAF // 2]) for k in range(LEAF // 2, LEAF)]
     for copy in copies:
@@ -226,10 +233,7 @@
     solved = jnp.where(own, solved, 0.0).astype(BF16)
     solved = dot(gather[...], solved)
     solved = jnp.where(iota((B, LANES), 0) % 2 == 0, solved[:, :LANES], solved[:, LANES:])
-    unit = one_hot(iota((LANES, LANES), 0) == iota((LANES, LANES), 1))
-    level[...] = lax.dot_general(unit, solved.astype(BF16), NT, preferred_element_type=F32).astype(BF16)
-    ancestors[...] = lax.dot_general(
-        unit[:64], rest[...].astype(BF16), NT, preferred_element_type=F32)
+    level[...] = solved.astype(BF16)
     owner = iota((B, LANES), 1) // 16
     for k in range(LEAF):
         right[k * 384:(k + 1) * 384] = doubled(jnp.where(owner == k, solved, 0.0)).astype(BF16)
@@ -366,15 +370,18 @@
         [vmem, vmem, hbm], [pltpu.VMEM(half, BF16), dma((LEAF // 2,))], 50,
         pl.CostEstimate(flops=2 * 10**9, bytes_accessed=10**6, transcendentals=0),
     )(notes, natural_inverses, natural_tiles)
-    level, ancestors, message = call(
+    solved, rest, message = call(
         update_kernel, "update",
-        [((LEAF * CASES, B), BF16), ((ANC * CASES, B), F32), ((PAIRS * UPD, 256), BF16)],
+        [((B, LANES), BF16), ((B, LANES), F32), ((PAIRS * UPD, 256), BF16)],
         [vmem, vmem, vmem, hbm, vmem],
-        [pltpu.VMEM((3, 2 * DOM, LANES), F32), pltpu.VMEM((B, LANES), F32), pltpu.VMEM((B, LANES), F32),
+        [pltpu.VMEM((3, 2 * DOM, LANES), F32), pltpu.VMEM((B, LANES), F32),
          pltpu.VMEM((LEAF * 384, 256), BF16), pltpu.VMEM(half, BF16),
          dma((LEAF // 2,)), pltpu.VMEM((PAIRS * UPD, 256), F32)], 48,
     )(exchange(message), ready, gather, natural_tiles, early)
 
+    level, ancestors = call(
+        turn_kernel, "turn", [((LEAF * CASES, B), BF16), ((ANC * CASES, B), F32)], [vmem] * 2, [], 16,
+        pl.CostEstimate(flops=10**9, bytes_accessed=10**6, transcendentals=0))(solved, rest)
     groups = [[(x * N_Z + z) * N_CORE + c for x in range(N_X) for c in range(N_CORE)] for z in range(N_Z)]
     received = lax.all_to_all(
         message.reshape(GROUP, 96, 256), "dom", 0, 0, axis_index_groups=groups, tiled=True)

time: 87.4 us -> 87.4 us (level)
    pallas_call x1 -> x2, Pallas kernels: 3.48 us -> 4.31 us  [the longest x1 3.48 us: on_device(): call(update_kernel, 'update', [((B, LANES), BF16), ((B, LANES), F32), ((P...]
  transfers between devices with their start and end apart: 7 -> 7, of which waited for: 5 -> 5; matrix products, arithmetic and copies ran while one was open for 0% -> 0% of each run, Pallas kernels for 7% -> 8%
where the time goes in v9:
time: 87.4 us; the launch traced here: 86.9 us
  starting transfers between devices  22.6 us (26%)
  waiting for transfers between devices  21.2 us (24%)
  blocking collectives  20.7 us (24%)
  Pallas kernels  18.1 us (21%)
  local copies, waits for them, and re-layouts  2.25 us (3%)
  between operations  2.03 us (2%)
    all_to_all x1, blocking collectives, exchange(): return lax.all_to_all(x, 'dom', 0, 0, tiled=True)  20.7 us
    all_to_all x1, waiting for transfers between devices, exchange(): return lax.all_to_all(x, 'dom', 0, 0, tiled=True)  7.54 us
    all_to_all x1, waiting for transfers between devices, on_device(): sums = lax.all_to_all(sums, 'dom', 0, 0, tiled=True)  6.97 us
    all_to_all x1, waiting for transfers between devices, on_device(): lax.all_to_all(message.reshape(GROUP, 96, 256), 'dom', 0, 0, axis_index_g...  5.7 us
    all_to_all x1, starting transfers between devices, on_device(): sums = lax.all_to_all(sums, 'dom', 0, 0, tiled=True)  4.92 us
    pallas_call x1, Pallas kernels, on_device(): call(split_kernel, 'split', [((P_SIZE, PAIRS, 1536), BF16), ((P_SIZE, PAI...  4.49 us
    all_to_all x1, starting transfers between devices, exchange(): return lax.all_to_all(x, 'dom', 0, 0, tiled=True)  4.42 us
    ppermute x2, starting transfers between devices, across(): return x + lax.ppermute(x, 'rhs', [(i, i ^ step) for i in range(4)])  4.29 us
  transfers between devices with their start and end apart: 7, of which 5 were waited for; matrix products, arithmetic and copies ran while one was open for 0% of the time, Pallas kernels for 8%

profile of v9, /device:TPU:1, one launch (start us, length us, event | category | flops | bytes accessed | tf_op | source)
XLA Modules:
  0.0 86.9 jit_solution(3463599748318649532)
XLA Ops:
  0.6 3.3 %collective-permute-start = (f32[12,16,192]{2,1,0:T(8,128)}, f32[12,16,192]{2,1,0:T(8,128)S(1)}, u32[]{:S(2)}, u32[]{:S(2)}) collective-permute-start(f32[12,16,192]{2,1,0:T(8,128)} %own.1), channel_id=1, source_target_pairs={{0,4},{4,0},{8,12},{12,8},{16,20},{20,16},{24,28},{28,24},{32,36},... | collective-permute-start | bytes 442376 | tf_op jit(solution)/shard_map/ppermute | solution.py:324
  4.0 1.9 %collective-permute-start.1 = (f32[12,16,192]{2,1,0:T(8,128)}, f32[12,16,192]{2,1,0:T(8,128)S(1)}, u32[]{:S(2)}, u32[]{:S(2)}) collective-permute-start(f32[12,16,192]{2,1,0:T(8,128)} %own.1), channel_id=1, source_target_pairs={{4,8},{8,4},{12,16},{16,12},{20,24},{24,20},{28,32},{32,28},{36,40... | collective-permute-start | bytes 442376 | tf_op jit(solution)/shard_map/ppermute | solution.py:323
  5.9 0.0 copy-start.4
  5.9 0.0 copy-start.3
  5.9 0.0 copy-start.5
  5.9 0.0 copy-start
  5.9 0.0 copy-start.1
  6.0 0.6 copy-done.4
  6.6 0.0 copy-done.3
  6.6 0.0 copy-done.5
  6.6 0.0 collective-permute-done.chip
  6.6 0.2 copy-done
  6.9 0.1 copy-done.1
  7.0 4.5 %split.1 = (bf16[12,96,1536]{2,1,0:T(8,128)(2,1)S(1)}, bf16[12,96,1536]{2,1,0:T(8,128)(2,1)S(1)}, bf16[24,64,384]{2,1,0:T(8,128)(2,1)S(1)}, f32[12,96,64]{2,1,0:T(8,128)S(1)}, f32[1,128]{1,0:T(1,128)S(1)}) custom-call(s32[16,128]{1,0:T(8,128)S(1)} %pad_add_fusion.table, f32[13824,128]{1,0:T(8,128)} %bitcast.35, ...), custom_call_target="tpu_custom_call" | custom-call | flops 1000000000 | bytes 14000000 | tf_op jit(solution)/shard_map/split/pallas_call | solution.py:339
  11.5 0.0 collective-permute-done.1.far
  11.5 3.3 %residual.1 = bf16[64,2,384]{2,1,0:T(2,128)(2,1)S(1)} custom-call(s32[16,128]{1,0:T(8,128)S(1)} %pad_add_fusion.table, bf16[12,96,1536]{2,1,0:T(8,128)(2,1)S(1)} %get-tuple-element.21.high, bf16[12,96,1536]{2,1,0:T(8,128)(2,1)S(1)} %get-tuple-element.22.low, bf16[24,64,384]{2,1,0:T(8,128)(2,1)S(1)} %get-tuple-element.23.near, ...), custom_call_target="tpu_custom_call" | custom-call | tf_op jit(solution)/shard_map/residual/pallas_call | solution.py:347
  14.7 20.7 %all_to_all.20.received = bf16[64,2,384]{2,1,0:T(2,128)(2,1)S(1)} all-to-all(bf16[64,2,384]{2,1,0:T(2,128)(2,1)S(1)} %residual.1), channel_id=1, replica_groups=mesh['dom'=64,'rhs'=4] {'dom'}, dimensions={0} | all-to-all | bytes 196608 | tf_op jit(solution)/shard_map/all_to_all | solution.py:354
  35.4 1.6 %permute.1 = (bf16[64,2,384]{2,1,0:T(2,128)(2,1)}, f32[64,128]{1,0:T(8,128)S(1)}, f32[1,128]{1,0:T(1,128)S(1)}) custom-call(bf16[64,2,384]{2,1,0:T(2,128)(2,1)S(1)} %all_to_all.20.received), custom_call_target="tpu_custom_call" | custom-call | flops 4000000000 | bytes 1000000 | tf_op jit(solution)/shard_map/permute/pallas_call | solution.py:359
  37.0 4.4 %all-to-all-start.1 = ((bf16[64,2,384]{2,1,0:T(2,128)(2,1)}), bf16[64,2,384]{2,1,0:T(2,128)(2,1)S(1)}, u32[]{:S(2)}, u32[]{:S(2)}) async-start(bf16[64,2,384]{2,1,0:T(2,128)(2,1)} %get-tuple-element.26), calls=%async_computation.1 | async-start | bytes 196608 | tf_op jit(solution)/shard_map/all_to_all | solution.py:354
  41.4 0.0 copy-start.2
  41.4 1.1 %copy-done.2 = bf16[8,36864]{1,0:T(8,128)(2,1)S(1)} copy-done((bf16[8,36864]{1,0:T(8,128)(2,1)S(1)}, bf16[8,36864]{1,0:T(8,128)(2,1)}, u32[]{:S(2)}) %copy-start.2) | copy-done | bytes 589848
  42.5 1.7 %fetch.1 = (bf16[768,1536]{1,0:T(8,128)(2,1)S(1)}, bf16[768,384]{1,0:T(8,128)(2,1)S(1)}, bf16[192,768]{1,0:T(8,128)(2,1)S(1)}) custom-call(f32[64,128]{1,0:T(8,128)S(1)} %get-tuple-element.27.notes, bf16[96,3,8,128]{3,2,1,0:T(8,128)(2,1)S(1)} %bitcast.34, bf16[768,3,8,128]{3,2,1,0:T(8,128)(2,1)} %bitcast.36), custom_call_target="tpu_custom_call" | custom-call | flops 2000000000 | bytes 1000000 | tf_op jit(solution)/shard_map/fetch/pallas_call | solution.py:367
  44.2 7.5 %all-to-all-done.1.received = bf16[64,2,384]{2,1,0:T(2,128)(2,1)S(1)} async-done(((bf16[64,2,384]{2,1,0:T(2,128)(2,1)}), bf16[64,2,384]{2,1,0:T(2,128)(2,1)S(1)}, u32[]{:S(2)}, u32[]{:S(2)}) %all-to-all-start.1) | async-done | bytes 98336 | tf_op jit(solution)/shard_map/all_to_all | solution.py:354
  51.7 3.5 %update.1 = (bf16[192,128]{1,0:T(8,128)(2,1)S(1)}, f32[192,128]{1,0:T(8,128)S(1)}, bf16[768,256]{1,0:T(8,128)(2,1)}) custom-call(bf16[64,2,384]{2,1,0:T(2,128)(2,1)S(1)} %all-to-all-done.1.received, bf16[768,384]{1,0:T(8,128)(2,1)S(1)} %get-tuple-element.28.ready, bf16[192,768]{1,0:T(8,128)(2,1)S(1)} %get-tuple-element.29.gather, ...), custom_call_target="tpu_custom_call" | custom-call | tf_op jit(solution)/shard_map/update/pallas_call | solution.py:373
  55.2 3.8 %all-to-all-start.2 = ((bf16[8,96,256]{2,1,0:T(8,128)(2,1)}), bf16[8,96,256]{2,1,0:T(8,128)(2,1)S(1)}, u32[]{:S(2)}, u32[]{:S(2)}) async-start(bf16[8,96,256]{2,1,0:T(8,128)(2,1)} %bitcast.12), calls=%async_computation.2 | async-start | bytes 786432 | tf_op jit(solution)/shard_map/all_to_all | solution.py:386
  59.0 1.3 %collective-permute-start.2 = (f32[1,128]{1,0:T(1,128)S(1)}, f32[1,128]{1,0:T(1,128)S(1)}, u32[]{:S(2)}, u32[]{:S(2)}) collective-permute-start(f32[1,128]{1,0:T(1,128)S(1)} %get-tuple-element.35), channel_id=1, source_target_pairs={{0,1},{1,0},{2,3},{3,2},{4,5},{5,4},{6,7},{7,6},{8,9},{9,8},{10,11... | collective-permute-start | bytes 1544 | tf_op jit(solution)/shard_map/ppermute | solution.py:357
  60.3 0.1 reshape.66
  60.3 0.1 reshape.67.targets
  60.4 0.1 select.12
  60.5 0.9 collective-permute-done.2
  61.4 5.7 %all-to-all-done.2.received = bf16[8,96,256]{2,1,0:T(8,128)(2,1)S(1)} async-done(((bf16[8,96,256]{2,1,0:T(8,128)(2,1)}), bf16[8,96,256]{2,1,0:T(8,128)(2,1)S(1)}, u32[]{:S(2)}, u32[]{:S(2)}) %all-to-all-start.2) | async-done | bytes 393248 | tf_op jit(solution)/shard_map/all_to_all | solution.py:386
  67.1 1.5 %sum.1 = (bf16[64,4,384]{2,1,0:T(4,128)(2,1)}, f32[1,128]{1,0:T(1,128)S(1)}) custom-call(bf16[8,96,256]{2,1,0:T(8,128)(2,1)S(1)} %all-to-all-done.2.received, bf16[256,512]{1,0:T(8,128)(2,1)S(1)} %select.12, f32[1,128]{1,0:T(1,128)S(1)} %add.32.squares), custom_call_target="tpu_custom_call" | custom-call | tf_op jit(solution)/shard_map/sum/pallas_call | solution.py:394
  68.6 4.9 %all-to-all-start.3 = ((bf16[64,4,384]{2,1,0:T(4,128)(2,1)}), bf16[64,4,384]{2,1,0:T(4,128)(2,1)S(1)}, u32[]{:S(2)}, u32[]{:S(2)}) async-start(bf16[64,4,384]{2,1,0:T(4,128)(2,1)} %get-tuple-element.36), calls=%async_computation.3 | async-start | bytes 393216 | tf_op jit(solution)/shard_map/all_to_all | solution.py:399
  73.5 3.0 %collective-permute-start.3 = (f32[1,128]{1,0:T(1,128)S(1)}, f32[1,128]{1,0:T(1,128)S(1)}, u32[]{:S(2)}, u32[]{:S(2)}) collective-permute-start(f32[1,128]{1,0:T(1,128)S(1)} %get-tuple-element.38), channel_id=1, source_target_pairs={{0,2},{1,3},{2,0},{3,1},{4,6},{5,7},{6,4},{7,5},{8,10},{9,11},{10,... | collective-permute-start | bytes 1544 | tf_op jit(solution)/shard_map/ppermute | solution.py:357
  76.5 0.8 turn.1
  77.3 0.2 collective-permute-done.3
  77.5 7.0 %all-to-all-done.3 = bf16[64,4,384]{2,1,0:T(4,128)(2,1)S(1)} async-done(((bf16[64,4,384]{2,1,0:T(4,128)(2,1)}), bf16[64,4,384]{2,1,0:T(4,128)(2,1)S(1)}, u32[]{:S(2)}, u32[]{:S(2)}) %all-to-all-start.3) | async-done | bytes 196640 | tf_op jit(solution)/shard_map/all_to_all | solution.py:399
  84.5 0.1 reshape.68.received
  84.6 1.2 %final.1 = f32[64,192]{1,0:T(8,128)} custom-call(bf16[256,384]{1,0:T(8,128)(2,1)S(1)} %reshape.68.received, f32[64,192]{1,0:T(8,128)S(1)} %get-tuple-element.37.ancestors), custom_call_target="tpu_custom_call" | custom-call | tf_op jit(solution)/shard_map/final/pallas_call | solution.py:400
  (7 shorter events, 0.0 us)
Async XLA Ops:
  0.6 6.0 %collective-permute-start = (f32[12,16,192]{2,1,0:T(8,128)}, f32[12,16,192]{2,1,0:T(8,128)S(1)}, u32[]{:S(2)}, u32[]{:S(2)}) collective-permute-start(f32[12,16,192]{2,1,0:T(8,128)} %own.1), channel_id=1, source_target_pairs={{0,4},{4,0},{8,12},{12,8},{16,20},{20,16},{24,28},{28,24},{32,36},... | collective-permute-start | bytes 442376 | tf_op jit(solution)/shard_map/ppermute | solution.py:324
  4.0 7.5 %collective-permute-start.1 = (f32[12,16,192]{2,1,0:T(8,128)}, f32[12,16,192]{2,1,0:T(8,128)S(1)}, u32[]{:S(2)}, u32[]{:S(2)}) collective-permute-start(f32[12,16,192]{2,1,0:T(8,128)} %own.1), channel_id=1, source_target_pairs={{4,8},{8,4},{12,16},{16,12},{20,24},{24,20},{28,32},{32,28},{36,40... | collective-permute-start | bytes 442376 | tf_op jit(solution)/shard_map/ppermute | solution.py:323
  5.9 0.7 copy-start.4
  5.9 0.7 copy-start.3
  5.9 0.7 copy-start.5
  5.9 0.9 %copy-start = (f32[12,16,192]{2,1,0:T(8,128)S(1)}, f32[12,16,192]{2,1,0:T(8,128)}, u32[]{:S(2)}) copy-start(f32[12,16,192]{2,1,0:T(8,128)} %loads.1) | copy-start | bytes 442372
  5.9 1.0 %copy-start.1 = (f32[12,16,192]{2,1,0:T(8,128)S(1)}, f32[12,16,192]{2,1,0:T(8,128)}, u32[]{:S(2)}) copy-start(f32[12,16,192]{2,1,0:T(8,128)} %own.1) | copy-start | bytes 442372
  37.0 14.7 %all-to-all-start.1 = ((bf16[64,2,384]{2,1,0:T(2,128)(2,1)}), bf16[64,2,384]{2,1,0:T(2,128)(2,1)S(1)}, u32[]{:S(2)}, u32[]{:S(2)}) async-start(bf16[64,2,384]{2,1,0:T(2,128)(2,1)} %get-tuple-element.26), calls=%async_computation.1 | async-start | bytes 196608 | tf_op jit(solution)/shard_map/all_to_all | solution.py:354
  41.4 1.1 %copy-start.2 = (bf16[8,36864]{1,0:T(8,128)(2,1)S(1)}, bf16[8,36864]{1,0:T(8,128)(2,1)}, u32[]{:S(2)}) copy-start(bf16[8,36864]{1,0:T(8,128)(2,1)} %param.13) | copy-start | bytes 1769476
  55.2 11.9 %all-to-all-start.2 = ((bf16[8,96,256]{2,1,0:T(8,128)(2,1)}), bf16[8,96,256]{2,1,0:T(8,128)(2,1)S(1)}, u32[]{:S(2)}, u32[]{:S(2)}) async-start(bf16[8,96,256]{2,1,0:T(8,128)(2,1)} %bitcast.12), calls=%async_computation.2 | async-start | bytes 786432 | tf_op jit(solution)/shard_map/all_to_all | solution.py:386
  59.0 2.4 %collective-permute-start.2 = (f32[1,128]{1,0:T(1,128)S(1)}, f32[1,128]{1,0:T(1,128)S(1)}, u32[]{:S(2)}, u32[]{:S(2)}) collective-permute-start(f32[1,128]{1,0:T(1,128)S(1)} %get-tuple-element.35), channel_id=1, source_target_pairs={{0,1},{1,0},{2,3},{3,2},{4,5},{5,4},{6,7},{7,6},{8,9},{9,8},{10,11... | collective-permute-start | bytes 1544 | tf_op jit(solution)/shard_map/ppermute | solution.py:357
  68.6 16.0 %all-to-all-start.3 = ((bf16[64,4,384]{2,1,0:T(4,128)(2,1)}), bf16[64,4,384]{2,1,0:T(4,128)(2,1)S(1)}, u32[]{:S(2)}, u32[]{:S(2)}) async-start(bf16[64,4,384]{2,1,0:T(4,128)(2,1)} %get-tuple-element.36), calls=%async_computation.3 | async-start | bytes 393216 | tf_op jit(solution)/shard_map/all_to_all | solution.py:399
  73.5 4.0 %collective-permute-start.3 = (f32[1,128]{1,0:T(1,128)S(1)}, f32[1,128]{1,0:T(1,128)S(1)}, u32[]{:S(2)}, u32[]{:S(2)}) collective-permute-start(f32[1,128]{1,0:T(1,128)S(1)} %get-tuple-element.38), channel_id=1, source_target_pairs={{0,2},{1,3},{2,0},{3,1},{4,6},{5,7},{6,4},{7,5},{8,10},{9,11},{10,... | collective-permute-start | bytes 1544 | tf_op jit(solution)/shard_map/ppermute | solution.py:357
